TPU v7x, 32 devices: a whole 2x2x4 slice. The times are simulated.
32 devices in a mesh: ctx: 8 (over z, core), wt: 4 (over y, x).
Axes of the slice: x: 2, y: 2, z: 4, core: 2. Of those that a mesh axis runs over, the one named last changes fastest.
Arguments:
- tokens: bfloat16 [4, 2048, 1536], P('wt', 'ctx'), may hold values from -6 to 6
- segments: int32 [4, 2048], P('wt'), may hold values from 0 to 2, as said below
- routes: int32 [4, 2048, 2], P('wt', 'ctx'), may hold values from 0 to 3, all different within a row; in each aligned block of 256 rows (0 to 255, 256 to 511, ..., all dimensions but the last counted through in order) at most 160 rows name the same one
- route_weights: float32 [4, 2048, 2], P('wt', 'ctx'), may hold values from 0.3 to 1
- gain_attn: bfloat16 [1536], P('wt'), may hold values from 0.25 to 1.75
- w_query: bfloat16 [1536, 1536], P('wt'), may hold values from -0.15625 to 0.15625
- w_key: bfloat16 [1536, 512], P('wt'), may hold values from -0.15625 to 0.15625
- w_value: bfloat16 [1536, 512], P('wt'), may hold values from -0.15625 to 0.15625
- w_out: bfloat16 [1536, 1536], P('wt'), may hold values from -0.625 to 0.625
- gain_ffn: bfloat16 [1536], P('wt'), may hold values from 0.25 to 1.75
- w_gate: bfloat16 [4, 1536, 1024], P(None, None, 'wt'), may hold values from -0.15625 to 0.15625
- w_up: bfloat16 [4, 1536, 1024], P(None, None, 'wt'), may hold values from -0.15625 to 0.15625
- w_down: bfloat16 [4, 1024, 1536], P(None, 'wt'), may hold values from -0.1875 to 0.1875
- cotangent: bfloat16 [4, 2048, 1536], P('wt', 'ctx'), may hold values from -6 to 6
Outputs:
- output: bfloat16 [4, 2048, 1536], P('wt', 'ctx')
- grad_tokens: float32 [4, 2048, 1536], P('wt', 'ctx')
- grad_gain_attn: float32 [1536], P('wt')
- grad_w_query: float32 [1536, 1536], P('wt')
- grad_w_key: float32 [1536, 512], P('wt')
- grad_w_value: float32 [1536, 512], P('wt')
- grad_w_out: float32 [1536, 1536], P('wt')
- grad_gain_ffn: float32 [1536], P('wt')
- grad_w_gate: float32 [4, 1536, 1024], P(None, None, 'wt')
- grad_w_up: float32 [4, 1536, 1024], P(None, None, 'wt')
- grad_w_down: float32 [4, 1024, 1536], P(None, 'wt')
Inputs may be any that keep to these rules, and one draw needn't show every extreme that they name: `segments`: numbers in position order (not in the dealt order of the token arrays); they never fall along a sequence and rise by at most one from a position to the next, start at 0, and the first document covers positions 0 to 1151. Every sequence's last position holds (896) // 400. `routes`: the two experts of a row differ; among the rows of one device no expert is named more than 160 times, a bound that some block reaches.
All inputs are finite; a program needn't handle non-finite values.
Results may differ from a plain program's by a relative error of at most 0.014.
Values may be sent and summed in bfloat16 or wider, within the bound.
No kernel may reach another device: no remote copies, remote signals or barrier semaphores. Data moves between devices by JAX's collectives and lax.ppermute only.
A program may use at most 320 MiB of HBM per device.

v0:
```python
import jax
import jax.numpy as jnp
from jax import lax
from jax.sharding import PartitionSpec as P

HEADS = 24
KV_HEADS = 8
HEAD_DIM = 64


EPSILON = 1e-06
NEG_LARGE = -1e30


def positions(count, shard, ctx_count, offset):
    index = jnp.arange(count, dtype=jnp.int32) + offset
    device = index // shard
    inner = index % shard
    half_len = shard // 2
    placed = jnp.where(
        inner < half_len,
        device * half_len + inner,
        (2 * ctx_count - 1 - device) * half_len + inner - half_len,
    )
    return placed


def inv_root(values):
    return lax.rsqrt(jnp.mean(values * values, axis=-1, keepdims=True) + EPSILON)


def rows_dot(left, right):
    return lax.dot_general(
        left, right, (((0,), (0,)), ((), ())), preferred_element_type=jnp.float32
    )


def back_dot(left, right):
    return lax.dot_general(
        left, right, (((1,), (1,)), ((), ())), preferred_element_type=jnp.float32
    )


def expert_forward(rows_in, gate_w, up_w, down_w):
    gate_pre = jnp.einsum("ecd,edf->ecf", rows_in, gate_w, preferred_element_type=jnp.float32)
    up_pre = jnp.einsum("ecd,edf->ecf", rows_in, up_w, preferred_element_type=jnp.float32)
    hidden = (jax.nn.silu(gate_pre) * up_pre).astype(jnp.bfloat16)
    result = jnp.einsum("ecf,efd->ecd", hidden, down_w, preferred_element_type=jnp.float32)
    return (gate_pre, up_pre, hidden, result)


def expert_backward(rows_in, grad_out, gate_pre, up_pre, hidden, gate_w, up_w, down_w):
    grad_hidden = jnp.einsum("ecd,efd->ecf", grad_out, down_w, preferred_element_type=jnp.float32)
    sigma = jax.nn.sigmoid(gate_pre)
    grad_gate = (grad_hidden * up_pre * sigma * (1.0 + gate_pre * (1.0 - sigma))).astype(
        jnp.bfloat16
    )
    grad_up = (grad_hidden * jax.nn.silu(gate_pre)).astype(jnp.bfloat16)
    grad_down = jnp.einsum("ecf,ecd->efd", hidden, grad_out, preferred_element_type=jnp.float32)
    grad_gate_w = jnp.einsum("ecd,ecf->edf", rows_in, grad_gate, preferred_element_type=jnp.float32)
    grad_up_w = jnp.einsum("ecd,ecf->edf", rows_in, grad_up, preferred_element_type=jnp.float32)
    grad_rows = jnp.einsum("ecf,edf->ecd", grad_gate, gate_w, preferred_element_type=jnp.float32)
    grad_rows = grad_rows + jnp.einsum(
        "ecf,edf->ecd", grad_up, up_w, preferred_element_type=jnp.float32
    )
    return (grad_gate_w, grad_up_w, grad_down, grad_rows)


def body(
    tokens,
    segments,
    routes,
    route_weights,
    gain_attn,
    w_query,
    w_key,
    w_value,
    w_out,
    gain_ffn,
    w_gate,
    w_up,
    w_down,
    cotangent,
):
    row_count = tokens.shape[1]
    model_width = tokens.shape[2]
    ctx_count = lax.axis_size("ctx")
    ctx_place = lax.axis_index("ctx")
    seg_row = segments[0]
    seq_len = seg_row.shape[0]
    capacity = 5 * row_count // 8
    expert_count = w_gate.shape[0]
    group = HEADS // KV_HEADS
    scale = HEAD_DIM ** (-0.5)
    kv_width = KV_HEADS * HEAD_DIM
    gain_a, weight_q, weight_k, weight_v, weight_o, gain_f, weight_g, weight_u, weight_d = (
        lax.all_gather(gain_attn, "wt", axis=0, tiled=True),
        lax.all_gather(w_query, "wt", axis=0, tiled=True),
        lax.all_gather(w_key, "wt", axis=0, tiled=True),
        lax.all_gather(w_value, "wt", axis=0, tiled=True),
        lax.all_gather(w_out, "wt", axis=0, tiled=True),
        lax.all_gather(gain_ffn, "wt", axis=0, tiled=True),
        lax.all_gather(w_gate, "wt", axis=2, tiled=True),
        lax.all_gather(w_up, "wt", axis=2, tiled=True),
        lax.all_gather(w_down, "wt", axis=1, tiled=True),
    )
    inputs_f = tokens[0].astype(jnp.float32)
    upstream = cotangent[0].astype(jnp.float32)
    root_a = inv_root(inputs_f)
    scaled_a = inputs_f * root_a
    gain_af = gain_a.astype(jnp.float32)
    normed = (scaled_a * gain_af).astype(jnp.bfloat16)
    queries = jnp.dot(normed, weight_q, preferred_element_type=jnp.float32).astype(jnp.bfloat16)
    keys_local = jnp.dot(normed, weight_k, preferred_element_type=jnp.float32).astype(jnp.bfloat16)
    values_local = jnp.dot(normed, weight_v, preferred_element_type=jnp.float32).astype(
        jnp.bfloat16
    )
    keys_all, values_all = (
        lax.all_gather(keys_local, "ctx", axis=0, tiled=True),
        lax.all_gather(values_local, "ctx", axis=0, tiled=True),
    )
    query_pos = positions(row_count, row_count, ctx_count, ctx_place * row_count)
    key_pos = positions(seq_len, row_count, ctx_count, 0)
    query_seg = jnp.take(seg_row, query_pos)
    key_seg = jnp.take(seg_row, key_pos)
    key_block = min(512, seq_len)
    block_count = seq_len // key_block
    blocked_all = (
        keys_all.reshape(block_count, key_block, KV_HEADS, HEAD_DIM),
        values_all.reshape(block_count, key_block, KV_HEADS, HEAD_DIM),
        key_pos.reshape(block_count, key_block),
        key_seg.reshape(block_count, key_block),
    )
    query_heads = queries.reshape(row_count, KV_HEADS, group, HEAD_DIM)
    state_shape = (KV_HEADS, group, row_count)
    head_shape = (row_count, KV_HEADS, group, HEAD_DIM)

    def block_scores(blocked):
        scores = scale * jnp.einsum(
            "rgcd,kgd->gcrk", query_heads, blocked[0], preferred_element_type=jnp.float32
        )
        allowed = (blocked[3][None, :] == query_seg[:, None]) & (
            blocked[2][None, :] <= query_pos[:, None]
        )
        return (jnp.where(allowed, scores, NEG_LARGE), allowed)

    def total_step(running, blocked):
        peak, mass = running
        scores, allowed = block_scores(blocked)
        new_peak = jnp.maximum(peak, jnp.max(scores, axis=-1))
        mass = mass * jnp.exp(peak - new_peak) + jnp.sum(
            jnp.exp(scores - new_peak[..., None]), axis=-1
        )
        return ((new_peak, mass), None)

    (peak, mass), unused = lax.scan(
        total_step,
        (jnp.full(state_shape, NEG_LARGE, jnp.float32), jnp.zeros(state_shape, jnp.float32)),
        blocked_all,
    )
    log_total = peak + jnp.log(mass)

    def block_probs(blocked):
        scores, allowed = block_scores(blocked)
        return jnp.where(allowed, jnp.exp(scores - log_total[..., None]), 0.0)

    def mix_step(running, blocked):
        probs = block_probs(blocked).astype(jnp.bfloat16)
        return (
            running
            + jnp.einsum("gcrk,kgd->rgcd", probs, blocked[1], preferred_element_type=jnp.float32),
            None,
        )

    attended, unused = lax.scan(mix_step, jnp.zeros(head_shape, jnp.float32), blocked_all)
    attended = attended.reshape(row_count, model_width).astype(jnp.bfloat16)
    resid = inputs_f + jnp.dot(attended, weight_o, preferred_element_type=jnp.float32)
    root_f = inv_root(resid)
    scaled_f = resid * root_f
    gain_ff = gain_f.astype(jnp.float32)
    normed_f = (scaled_f * gain_ff).astype(jnp.bfloat16)
    route_ids = routes[0]
    route_wts = route_weights[0]
    picks = (
        (route_ids[:, :, None] == jnp.arange(expert_count, dtype=jnp.int32)[None, None, :])
        .astype(jnp.int32)
        .reshape(2 * row_count, expert_count)
    )
    earlier = jnp.cumsum(picks, axis=0) - picks
    slot_rank = jnp.sum(earlier * picks, axis=1)
    slot_index = route_ids.reshape(2 * row_count) * capacity + slot_rank
    slot_owner = (
        jnp.full((expert_count * capacity,), 2 * row_count, jnp.int32)
        .at[slot_index]
        .set(jnp.arange(2 * row_count, dtype=jnp.int32))
    )
    dispatched = jnp.take(normed_f, slot_owner // 2, axis=0, mode="fill", fill_value=0).reshape(
        expert_count, capacity, model_width
    )
    gate_pre, up_pre, hidden, expert_out = expert_forward(dispatched, weight_g, weight_u, weight_d)
    picked = jnp.take(
        expert_out.reshape(expert_count * capacity, model_width), slot_index, axis=0
    ).reshape(row_count, 2, model_width)
    result = resid + jnp.sum(route_wts[:, :, None] * picked, axis=1)
    grad_pick = (
        (route_wts[:, :, None] * upstream[:, None, :])
        .astype(jnp.bfloat16)
        .reshape(2 * row_count, model_width)
    )
    grad_disp = jnp.take(grad_pick, slot_owner, axis=0, mode="fill", fill_value=0).reshape(
        expert_count, capacity, model_width
    )
    grad_gate_w, grad_up_w, grad_down_w, grad_disp_rows = expert_backward(
        dispatched, grad_disp, gate_pre, up_pre, hidden, weight_g, weight_u, weight_d
    )
    grad_normed_f = jnp.sum(
        jnp.take(
            grad_disp_rows.reshape(expert_count * capacity, model_width), slot_index, axis=0
        ).reshape(row_count, 2, model_width),
        axis=1,
    )
    grad_gain_f = jnp.sum(grad_normed_f * scaled_f, axis=0)
    scaled_grad_f = grad_normed_f * gain_ff
    grad_resid = upstream + root_f * (
        scaled_grad_f - scaled_f * jnp.mean(scaled_grad_f * scaled_f, axis=-1, keepdims=True)
    )
    grad_branch = grad_resid.astype(jnp.bfloat16)
    grad_out_w = rows_dot(attended, grad_branch)
    grad_att = back_dot(grad_branch, weight_o).astype(jnp.bfloat16).reshape(head_shape)

    def delta_step(running, blocked):
        probs = block_probs(blocked)
        grad_probs = jnp.einsum(
            "rgcd,kgd->gcrk", grad_att, blocked[1], preferred_element_type=jnp.float32
        )
        return (running + jnp.sum(probs * grad_probs, axis=-1), None)

    row_delta, unused = lax.scan(delta_step, jnp.zeros(state_shape, jnp.float32), blocked_all)

    def grad_step(running, blocked):
        probs = block_probs(blocked)
        grad_probs = jnp.einsum(
            "rgcd,kgd->gcrk", grad_att, blocked[1], preferred_element_type=jnp.float32
        )
        grad_scores = (probs * (grad_probs - row_delta[..., None])).astype(jnp.bfloat16)
        running = running + scale * jnp.einsum(
            "gcrk,kgd->rgcd", grad_scores, blocked[0], preferred_element_type=jnp.float32
        )
        key_part = scale * jnp.einsum(
            "gcrk,rgcd->kgd", grad_scores, query_heads, preferred_element_type=jnp.float32
        )
        value_part = jnp.einsum(
            "gcrk,rgcd->kgd",
            probs.astype(jnp.bfloat16),
            grad_att,
            preferred_element_type=jnp.float32,
        )
        return (running, (key_part, value_part))

    grad_query, (key_parts, value_parts) = lax.scan(
        grad_step, jnp.zeros(head_shape, jnp.float32), blocked_all
    )
    grad_keys_all = key_parts.reshape(seq_len, kv_width)
    grad_values_all = value_parts.reshape(seq_len, kv_width)
    grad_keys, grad_values = (
        lax.psum_scatter(grad_keys_all, "ctx", scatter_dimension=0, tiled=True),
        lax.psum_scatter(grad_values_all, "ctx", scatter_dimension=0, tiled=True),
    )
    grad_keys = grad_keys.astype(jnp.bfloat16)
    grad_values = grad_values.astype(jnp.bfloat16)
    grad_query = grad_query.reshape(row_count, model_width).astype(jnp.bfloat16)
    grad_q_w = rows_dot(normed, grad_query)
    grad_k_w = rows_dot(normed, grad_keys)
    grad_v_w = rows_dot(normed, grad_values)
    grad_normed = (
        back_dot(grad_query, weight_q)
        + back_dot(grad_keys, weight_k)
        + back_dot(grad_values, weight_v)
    )
    grad_gain_a = jnp.sum(grad_normed * scaled_a, axis=0)
    scaled_grad_a = grad_normed * gain_af
    grad_input = grad_resid + root_a * (
        scaled_grad_a - scaled_a * jnp.mean(scaled_grad_a * scaled_a, axis=-1, keepdims=True)
    )
    shard_ga, shard_q, shard_k, shard_v, shard_o, shard_gf, shard_gate, shard_up, shard_down = (
        lax.psum_scatter(grad_gain_a, "wt", scatter_dimension=0, tiled=True),
        lax.psum_scatter(grad_q_w, "wt", scatter_dimension=0, tiled=True),
        lax.psum_scatter(grad_k_w, "wt", scatter_dimension=0, tiled=True),
        lax.psum_scatter(grad_v_w, "wt", scatter_dimension=0, tiled=True),
        lax.psum_scatter(grad_out_w, "wt", scatter_dimension=0, tiled=True),
        lax.psum_scatter(grad_gain_f, "wt", scatter_dimension=0, tiled=True),
        lax.psum_scatter(grad_gate_w, "wt", scatter_dimension=2, tiled=True),
        lax.psum_scatter(grad_up_w, "wt", scatter_dimension=2, tiled=True),
        lax.psum_scatter(grad_down_w, "wt", scatter_dimension=1, tiled=True),
    )
    total_ga, total_q, total_k, total_v, total_o, total_gf, total_gate, total_up, total_down = (
        lax.psum(
            (
                shard_ga,
                shard_q,
                shard_k,
                shard_v,
                shard_o,
                shard_gf,
                shard_gate,
                shard_up,
                shard_down,
            ),
            "ctx",
        )
    )
    return (
        result.astype(jnp.bfloat16)[None],
        grad_input[None],
        total_ga,
        total_q,
        total_k,
        total_v,
        total_o,
        total_gf,
        total_gate,
        total_up,
        total_down,
    )


def solution(mesh):
    return jax.shard_map(
        body,
        mesh=mesh,
        in_specs=(
            P("wt", "ctx", None),
            P("wt", None),
            P("wt", "ctx", None),
            P("wt", "ctx", None),
            P("wt"),
            P("wt", None),
            P("wt", None),
            P("wt", None),
            P("wt", None),
            P("wt"),
            P(None, None, "wt"),
            P(None, None, "wt"),
            P(None, "wt", None),
            P("wt", "ctx", None),
        ),
        out_specs=(
            P("wt", "ctx", None),
            P("wt", "ctx", None),
            P("wt"),
            P("wt", None),
            P("wt", None),
            P("wt", None),
            P("wt", None),
            P("wt"),
            P(None, None, "wt"),
            P(None, None, "wt"),
            P(None, "wt", None),
        ),
        check_vma=False,
    )
```

profile of v0, /device:TPU:0, one launch (start us, length us, event | category | flops | bytes accessed | tf_op | source)
XLA Modules:
  0.0 2647.9 jit_solution(9396852622898460749)
XLA Ops:
  20.5 23.1 all-gather.16.cloned.1.call-done
  46.6 29.8 %all-gather.12.cloned.1.call-done = bf16[1536,512]{1,0:T(8,128)(2,1)} async-done(((bf16[384,512]{1,0:T(8,128)(2,1)}), bf16[1536,512]{1,0:T(8,128)(2,1)}) %all-gather.12.cloned.1.call-update) | async-done | bytes 1572880 | tf_op jit(solution)/shard_map/all_gather | solution.py:100
  150.2 46.5 %all-gather.20.cloned.1.call-done = bf16[1536,1536]{1,0:T(8,128)(2,1)} async-done(((bf16[384,1536]{1,0:T(8,128)(2,1)}), bf16[1536,1536]{1,0:T(8,128)(2,1)}) %all-gather.20.cloned.1.call-update) | async-done | bytes 4718608 | tf_op jit(solution)/shard_map/all_gather | solution.py:98
  202.8 56.9 %while.50 = (s32[]{:T(128)}, f32[8,3,256]{2,1,0:T(4,128)S(1)}, f32[8,3,256]{2,1,0:T(4,128)S(1)}, s32[4,512]{1,0:T(4,128)S(1)}, s32[256]{0:T(256)S(1)}, /*index=5...) while((s32[]{:T(128)}, f32[8,3,256]{2,1,0:T(4,128)S(1)}, ...), condition=%wide.region_4.5_spmd.clone, body=%wide.region_1.4_spmd.clone.sunk | while | flops 425104384 | bytes 27204740 | solution.py:156
  260.3 27.7 %while.51 = (s32[]{:T(128)}, f32[256,8,3,64]{0,3,2,1:T(8,128)}, bf16[4,512,8,64]{1,3,2,0:T(8,128)(2,1)}, s32[4,512]{1,0:T(4,128)S(1)}, s32[256]{0:T(256)S(1)}, /...) while((s32[]{:T(128)}, f32[256,8,3,64]{0,3,2,1:T(8,128)}, ...), condition=%wide.region_6.7_spmd.clone, body=%wide.region_5.6_spmd.clone.sunk | while | flops 822221824 | bytes 5292167 | solution.py:175
  300.1 79.6 %all-gather.26.cloned.1.call-done = bf16[4,1536,1024]{2,1,0:T(8,128)(2,1)} async-done(((bf16[4,1536,256]{2,1,0:T(8,128)(2,1)}), bf16[4,1536,1024]{2,1,0:T(8,128)(2,1)}) %all-gather.26.cloned.1.call-update) | async-done | bytes 12582928 | tf_op jit(solution)/shard_map/all_gather | solution.py:104
  388.1 115.9 %all-gather.24.cloned.1.call-done = bf16[4,1536,1024]{2,1,0:T(8,128)(2,1)} async-done(((bf16[4,1536,256]{2,1,0:T(8,128)(2,1)}), bf16[4,1536,1024]{2,1,0:T(8,128)(2,1)}) %all-gather.24.cloned.1.call-update) | async-done | bytes 12582928 | tf_op jit(solution)/shard_map/all_gather | solution.py:103
  512.4 116.0 %all-gather.28.cloned.1.call-done = bf16[4,1024,1536]{2,1,0:T(8,128)(2,1)} async-done(((bf16[4,256,1536]{2,1,0:T(8,128)(2,1)}), bf16[4,1024,1536]{2,1,0:T(8,128)(2,1)}) %all-gather.28.cloned.1.call-update) | async-done | bytes 12582928 | tf_op jit(solution)/shard_map/all_gather | solution.py:105
  628.4 12.3 multiply_convert_fusion.1
  720.6 41.4 %while.52 = (s32[]{:T(128)}, f32[8,3,256]{2,1,0:T(4,128)}, s32[4,512]{1,0:T(4,128)}, s32[256]{0:T(256)S(1)}, s32[4,512]{1,0:T(4,128)S(1)}, /*index=5*/bf16[4,512...) while((s32[]{:T(128)}, f32[8,3,256]{2,1,0:T(4,128)}, ...), condition=%wide.region_17.19_spmd.clone, body=%wide.region_15.18_spmd.clone.sunk | while | flops 824587264 | bytes 28197004 | solution.py:238
  762.1 290.0 %while.53 = (s32[]{:T(128)}, f32[256,8,3,64]{0,3,2,1:T(8,128)S(1)}, f32[4,512,8,64]{1,0,3,2:T(4,128)}, f32[4,512,8,64]{1,0,3,2:T(4,128)}, bf16[4,512,8,64]{1,3,2...) while((s32[]{:T(128)}, f32[256,8,3,64]{0,3,2,1:T(8,128)S(1)}, ...), condition=%wide.region_19.21_spmd.clone, body=%wide.region_18.20_spmd.clone.sunk | while | flops 2052856832 | bytes 125805256 | solution.py:260
  780.9 21.0 dynamic_update_slice.11
  813.6 21.0 dynamic_update_slice.12
  853.3 21.0 dynamic_update_slice.11
  886.0 21.0 dynamic_update_slice.12
  925.7 21.0 dynamic_update_slice.11
  958.4 21.0 dynamic_update_slice.12
  998.1 21.0 dynamic_update_slice.11
  1030.9 21.0 dynamic_update_slice.12
  1064.5 43.9 %reduce-scatter.10.cloned.1.call-done = f32[256,512]{0,1:T(8,128)} async-done(((f32[2048,512]{0,1:T(8,128)}), f32[256,512]{0,1:T(8,128)}) %reduce-scatter.10.cloned.1.call-update) | async-done | bytes 524304 | tf_op jit(solution)/shard_map/reduce_scatter | solution.py:266
  1111.9 47.6 %reduce-scatter.12.cloned.1.call-done = f32[256,512]{0,1:T(8,128)} async-done(((f32[2048,512]{0,1:T(8,128)}), f32[256,512]{0,1:T(8,128)}) %reduce-scatter.12.cloned.1.call-update) | async-done | bytes 524304 | tf_op jit(solution)/shard_map/reduce_scatter | solution.py:267
  1176.7 11.9 fusion.94
  1188.6 12.2 fusion.93
  1214.2 38.4 %reduce-scatter.18.cloned.1.call-done = f32[384,512]{1,0:T(8,128)} async-done(((f32[1536,512]{1,0:T(8,128)}), f32[384,512]{1,0:T(8,128)}) %reduce-scatter.18.cloned.1.call-update) | async-done | bytes 786448 | tf_op jit(solution)/shard_map/reduce_scatter | solution.py:289
  1252.6 98.0 %reduce-scatter.14.cloned.1.call-done = f32[384,1536]{1,0:T(8,128)} async-done(((f32[1536,1536]{1,0:T(8,128)}), f32[384,1536]{1,0:T(8,128)}) %reduce-scatter.14.cloned.1.call-update) | async-done | bytes 2359312 | tf_op jit(solution)/shard_map/reduce_scatter | solution.py:287
  1350.6 98.0 %reduce-scatter.20.cloned.1.call-done = f32[384,1536]{1,0:T(8,128)} async-done(((f32[1536,1536]{1,0:T(8,128)}), f32[384,1536]{1,0:T(8,128)}) %reduce-scatter.20.cloned.1.call-update) | async-done | bytes 2359312 | tf_op jit(solution)/shard_map/reduce_scatter | solution.py:290
  1448.6 224.8 %reduce-scatter.22.cloned.1.call-done = f32[4,1536,256]{2,1,0:T(8,128)} async-done(((f32[4,1536,1024]{2,1,0:T(8,128)}), f32[4,1536,256]{2,1,0:T(8,128)}) %reduce-scatter.22.cloned.1.call-update) | async-done | bytes 6291472 | tf_op jit(solution)/shard_map/reduce_scatter | solution.py:292
  1673.4 225.1 %reduce-scatter.24.cloned.1.call-done = f32[4,1536,256]{2,1,0:T(8,128)} async-done(((f32[4,1536,1024]{2,1,0:T(8,128)}), f32[4,1536,256]{2,1,0:T(8,128)}) %reduce-scatter.24.cloned.1.call-update) | async-done | bytes 6291472 | tf_op jit(solution)/shard_map/reduce_scatter | solution.py:293
  1898.6 224.9 %reduce-scatter.26.cloned.1.call-done = f32[4,256,1536]{2,1,0:T(8,128)} async-done(((f32[4,1024,1536]{2,1,0:T(8,128)}), f32[4,256,1536]{2,1,0:T(8,128)}) %reduce-scatter.26.cloned.1.call-update) | async-done | bytes 6291472 | tf_op jit(solution)/shard_map/reduce_scatter | solution.py:294
  2133.2 15.0 all-reduce.4
  2148.4 15.2 all-reduce.2
  2166.6 455.8 %all-reduce.7.cloned.1.call-done = (f32[384,1536]{1,0:T(8,128)}, f32[384,512]{1,0:T(8,128)}, f32[384,512]{1,0:T(8,128)}, f32[384,1536]{1,0:T(8,128)}, f32[4,1536...) async-done(((f32[384,1536]{1,0:T(8,128)}, f32[384,512]{1,0:T(8,128)}, f32[384,512]{1,0:T(8,128)}, f32[384,1536]{1,0:T(8,128)}, ...) | async-done | bytes 25165840 | tf_op jit(solution)/shard_map/psum | solution.py:297
  (394 shorter events, 528.6 us)
Async XLA Ops:
  7.2 81.1 %copy-start = (s32[1,2048]{1,0:T(1,128)S(1)}, s32[1,2048]{1,0:T(1,128)}, u32[]{:S(2)}) copy-start(s32[1,2048]{1,0:T(1,128)} %param.25) | copy-start | bytes 24580
  7.2 36.4 %all-gather.16.cloned.1.call-start = ((), (), s32[]{:S(2)}) async-start(), calls=%async_computation.11 | async-start | bytes 1966080 | tf_op jit(solution)/shard_map/all_gather | solution.py:99
  7.9 68.5 %all-gather.12.cloned.1.call-start = ((), (), s32[]{:S(2)}) async-start(), calls=%async_computation.9 | async-start | bytes 1966080 | tf_op jit(solution)/shard_map/all_gather | solution.py:100
  8.7 115.1 %all-gather.18.cloned.1.call-start = ((), (), s32[]{:S(2)}) async-start(), calls=%async_computation.12 | async-start | bytes 2359296 | tf_op jit(solution)/shard_map/all_gather | solution.py:119
  19.0 177.8 %copy-start.37 = (f32[1536]{0:T(1024)}, f32[1536]{0:T(1024)S(1)}, u32[]{:S(2)}) copy-start(f32[1536]{0:T(1024)S(1)} %reshape.490) | copy-start | bytes 18436
  19.0 57.5 %copy-start.7 = (bf16[1,256,1536]{2,1,0:T(8,128)(2,1)S(1)}, bf16[1,256,1536]{2,1,0:T(8,128)(2,1)}, u32[]{:S(2)}) copy-start(bf16[1,256,1536]{2,1,0:T(8,128)(2,1)} %param.24) | copy-start | bytes 2359300
  20.5 176.2 %copy-start.42 = (f32[256]{0:T(256)}, f32[256]{0:T(256)S(1)}, u32[]{:S(2)}) copy-start(f32[256]{0:T(256)S(1)} %add_rsqrt_fusion.1) | copy-start | bytes 3076
  46.6 91.8 %all-gather.14.cloned.1.call-start = ((), (), s32[]{:S(2)}) async-start(), calls=%async_computation.10 | async-start | bytes 2359296 | tf_op jit(solution)/shard_map/all_gather | solution.py:120
  79.2 117.5 %all-gather.20.cloned.1.call-start = ((), (), s32[]{:S(2)}) async-start(), calls=%async_computation.13 | async-start | bytes 5898240 | tf_op jit(solution)/shard_map/all_gather | solution.py:98
  79.8 211.5 %all-gather.22.cloned.1.call-start = ((), (), s32[]{:S(2)}) async-start(), calls=%async_computation.14 | async-start | bytes 5898240 | tf_op jit(solution)/shard_map/all_gather | solution.py:101
  80.4 299.4 %all-gather.26.cloned.1.call-start = ((), (), s32[]{:S(2)}) async-start(), calls=%async_computation.16 | async-start | bytes 15728640 | tf_op jit(solution)/shard_map/all_gather | solution.py:104
  81.1 422.9 %all-gather.24.cloned.1.call-start = ((), (), s32[]{:S(2)}) async-start(), calls=%async_computation.15 | async-start | bytes 15728640 | tf_op jit(solution)/shard_map/all_gather | solution.py:103
  81.9 546.5 %all-gather.28.cloned.1.call-start = ((), (), s32[]{:S(2)}) async-start(), calls=%async_computation.17 | async-start | bytes 15728640 | tf_op jit(solution)/shard_map/all_gather | solution.py:105
  82.6 1025.8 %reduce-scatter.10.cloned.1.call-start = ((), (), s32[]{:S(2)}) async-start(), calls=%async_computation.18 | async-start | bytes 4718592 | tf_op jit(solution)/shard_map/reduce_scatter | solution.py:266
  90.0 20.6 copy-start.23
  109.9 185.7 %copy-start.40 = (f32[1536]{0:T(1024)}, f32[1536]{0:T(1024)S(1)}, u32[]{:S(2)}) copy-start(f32[1536]{0:T(1024)S(1)} %reshape.491) | copy-start | bytes 18436
  110.0 394.0 %copy-start.35 = (pred[4,160]{1,0:T(4,128)(4,1)}, pred[4,160]{1,0:T(4,128)(4,1)S(1)}, u32[]{:S(2)}) copy-start(pred[4,160]{1,0:T(4,128)(4,1)S(1)} %broadcast_in_dim.140) | copy-start | bytes 1924
  144.6 52.2 %copy-start.8 = (bf16[1,256,1536]{2,1,0:T(8,128)(2,1)S(1)}, bf16[1,256,1536]{2,1,0:T(8,128)(2,1)}, u32[]{:S(2)}) copy-start(bf16[1,256,1536]{2,1,0:T(8,128)(2,1)} %param.24) | copy-start | bytes 2359300
  300.1 203.8 %copy-start.5 = (bf16[640,1536]{1,0:T(8,128)(2,1)}, bf16[640,1536]{1,0:T(8,128)(2,1)S(1)}, u32[]{:S(2)}) copy-start(bf16[640,1536]{1,0:T(8,128)(2,1)S(1)} %gather_fusion.2) | copy-start | bytes 5898244
  720.6 41.4 %copy-start.3 = (f32[256,8,3,64]{0,3,2,1:T(8,128)S(1)}, f32[256,8,3,64]{0,3,2,1:T(8,128)}, u32[]{:S(2)}) copy-start(f32[256,8,3,64]{0,3,2,1:T(8,128)} %custom-call.4) | copy-start | bytes 4718596
  1058.2 101.2 %reduce-scatter.12.cloned.1.call-start = ((), (), s32[]{:S(2)}) async-start(), calls=%async_computation.19 | async-start | bytes 4718592 | tf_op jit(solution)/shard_map/reduce_scatter | solution.py:267
  1064.4 44.0 %copy-start.9 = (bf16[1,256,1536]{2,1,0:T(8,128)(2,1)S(1)}, bf16[1,256,1536]{2,1,0:T(8,128)(2,1)}, u32[]{:S(2)}) copy-start(bf16[1,256,1536]{2,1,0:T(8,128)(2,1)} %param.24) | copy-start | bytes 2359300
  1064.5 44.0 %copy-start.38 = (f32[1536]{0:T(1024)S(1)}, f32[1536]{0:T(1024)}, u32[]{:S(2)}) copy-start(f32[1536]{0:T(1024)} %copy-done.37) | copy-start | bytes 18436
  1064.5 44.0 %copy-start.43 = (f32[256]{0:T(256)S(1)}, f32[256]{0:T(256)}, u32[]{:S(2)}) copy-start(f32[256]{0:T(256)} %copy-done.42) | copy-start | bytes 3076
  1064.5 149.7 %reduce-scatter.16.cloned.1.call-start = ((), (), s32[]{:S(2)}) async-start(), calls=%async_computation.21 | async-start | bytes 3932160 | tf_op jit(solution)/shard_map/reduce_scatter | solution.py:288
  1111.9 140.7 %reduce-scatter.18.cloned.1.call-start = ((), (), s32[]{:S(2)}) async-start(), calls=%async_computation.22 | async-start | bytes 3932160 | tf_op jit(solution)/shard_map/reduce_scatter | solution.py:289
  1162.9 187.7 %reduce-scatter.14.cloned.1.call-start = ((), (), s32[]{:S(2)}) async-start(), calls=%async_computation.20 | async-start | bytes 11796480 | tf_op jit(solution)/shard_map/reduce_scatter | solution.py:287
  1168.4 280.2 %reduce-scatter.20.cloned.1.call-start = ((), (), s32[]{:S(2)}) async-start(), calls=%async_computation.23 | async-start | bytes 11796480 | tf_op jit(solution)/shard_map/reduce_scatter | solution.py:290
  1175.0 498.4 %reduce-scatter.22.cloned.1.call-start = ((), (), s32[]{:S(2)}) async-start(), calls=%async_computation.24 | async-start | bytes 31457280 | tf_op jit(solution)/shard_map/reduce_scatter | solution.py:292
  1188.6 710.0 %reduce-scatter.24.cloned.1.call-start = ((), (), s32[]{:S(2)}) async-start(), calls=%async_computation.25 | async-start | bytes 31457280 | tf_op jit(solution)/shard_map/reduce_scatter | solution.py:293
  1200.8 922.6 %reduce-scatter.26.cloned.1.call-start = ((), (), s32[]{:S(2)}) async-start(), calls=%async_computation.26 | async-start | bytes 31457280 | tf_op jit(solution)/shard_map/reduce_scatter | solution.py:294
  1214.1 1408.3 %all-reduce.7.cloned.1.call-start = ((), (), s32[]{:S(2)}) async-start(), calls=%async_computation.27 | async-start | bytes 50331648 | tf_op jit(solution)/shard_map/psum | solution.py:297
  (50 other events, 239.9 us)
Sparse Core Ops, SparseCore 0:
  9.9 33.6 all-gather.15
  45.4 30.9 all-gather.11
  78.6 29.1 all-gather.17
  109.8 28.5 all-gather.13
  140.1 56.5 all-gather.19
  198.4 57.0 all-gather.21
  257.3 122.3 all-gather.25
  381.6 122.3 all-gather.23
  505.8 122.5 all-gather.27
  1058.4 50.0 reduce-scatter.9
  1111.3 48.1 reduce-scatter.11
  1162.9 42.0 reduce-scatter.15
  1208.6 43.9 reduce-scatter.17
  1255.5 95.0 reduce-scatter.13
  1353.5 95.0 reduce-scatter.19
  1451.6 221.8 reduce-scatter.21
  1676.7 221.8 reduce-scatter.23
  1901.5 221.8 reduce-scatter.25
  2127.2 495.1 all-reduce.6
where the time goes:
time: 2660 us; the launch traced here: 2650 us
  waiting for transfers between devices  1880 us (71%)
  matrix products  328 us (12%)
  local copies, waits for them, and re-layouts  303 us (11%)
  other arithmetic  74.8 us (3%)
  blocking collectives  47.7 us (2%)
    psum x1, waiting for transfers between devices, body(): lax.psum((shard_ga, shard_q, shard_k, shard_v, shard_o, shard_gf, shard_g...  456 us
    reduce_scatter x1, waiting for transfers between devices, body(): lax.psum_scatter(grad_up_w, 'wt', scatter_dimension=2, tiled=True)  225 us
    reduce_scatter x1, waiting for transfers between devices, body(): lax.psum_scatter(grad_down_w, 'wt', scatter_dimension=1, tiled=True)  225 us
    reduce_scatter x1, waiting for transfers between devices, body(): lax.psum_scatter(grad_gate_w, 'wt', scatter_dimension=2, tiled=True)  225 us
    dynamic_update_slice x16, local copies, waits for them, and re-layouts, body(): lax.scan(grad_step, jnp.zeros(head_shape, jnp.float32), blocked_all)  177 us
    all_gather x1, waiting for transfers between devices, body(): lax.all_gather(w_down, 'wt', axis=1, tiled=True)  116 us
    all_gather x1, waiting for transfers between devices, body(): lax.all_gather(w_gate, 'wt', axis=2, tiled=True)  116 us
    reduce_scatter x1, waiting for transfers between devices, body(): lax.psum_scatter(grad_q_w, 'wt', scatter_dimension=0, tiled=True)  98 us
  transfers between devices with their start and end apart: 19, of which 16 were waited for; matrix products, arithmetic and copies ran while one was open for 9% of the time, Pallas kernels for 0%

commit v1 on v0

v1 whole, which is shorter than its diff:
```python
import functools

import jax
import jax.numpy as jnp
from jax import lax
from jax.experimental import pallas as pl
from jax.experimental.pallas import tpu as pltpu
from jax.sharding import Mesh, PartitionSpec as P

HEADS = 24
KV_HEADS = 8
HEAD_DIM = 64
SCALE = HEAD_DIM ** -0.5
PAIRS = KV_HEADS // 2
EPSILON = 1e-06
NEG_LARGE = -1e30
VMEM_BYTES = 56 * 1024 * 1024
BF = jnp.bfloat16
F32 = jnp.float32

VMEM = pl.BlockSpec(memory_space=pltpu.VMEM)
SMEM = pl.BlockSpec(memory_space=pltpu.SMEM)
ANY = pl.BlockSpec(memory_space=pl.ANY)


def params():
    return pltpu.CompilerParams(vmem_limit_bytes=VMEM_BYTES)


def cost(flops, nbytes, trans=0):
    return pl.CostEstimate(flops=int(flops), bytes_accessed=int(nbytes), transcendentals=int(trans))


def shape(dims, dtype):
    return jax.ShapeDtypeStruct(tuple(dims), dtype)


def nn(a, b):
    return lax.dot_general(a, b, (((1,), (0,)), ((), ())), preferred_element_type=F32)


def nt(a, b):
    return lax.dot_general(a, b, (((1,), (1,)), ((), ())), preferred_element_type=F32)


def tn(a, b):
    return lax.dot_general(a, b, (((0,), (0,)), ((), ())), preferred_element_type=F32)


def inv_root(values):
    return lax.rsqrt(jnp.mean(values * values, axis=-1, keepdims=True) + EPSILON)


def swap(v, axis):
    return lax.ppermute(v, axis, [(0, 1), (1, 0)])


def to_y(v, d):
    n = lax.axis_size("y")
    return lax.ppermute(v, "y", [(i, (i + d) % n) for i in range(n)])


def from_y(v, d):
    n = lax.axis_size("y")
    return lax.ppermute(v, "y", [((i + d) % n, i) for i in range(n)])


def to_plane(v, dy, dx):
    n = lax.axis_size("y")
    if dy == 0:
        return swap(v, "x")
    if dx == 0:
        return to_y(v, dy)
    perm = [(2 * i + k, 2 * ((i + dy) % n) + (k ^ dx)) for i in range(n) for k in range(2)]
    return lax.ppermute(v, ("y", "x"), perm)


def z_move(v, d):
    n = lax.axis_size("z")
    return lax.ppermute(v, "z", [(i, i + d) for i in range(n) if 0 <= i + d < n])


def plane_gather(a, b):
    n = lax.axis_size("y")
    xa, xb = swap(a, "x"), swap(b, "x")
    got = {(0, 1): (xa, xb)}
    for d in range(1, n):
        ya, yb = from_y(a, d), from_y(b, d)
        got[(d, 0)] = (ya, yb)
        got[(d, 1)] = (from_y(xa, d), swap(yb, "x"))
    return got


def add_low(*terms):
    total = terms[0].astype(F32)
    for term in terms[1:]:
        total = total + term.astype(F32)
    return total.astype(terms[0].dtype)


def z_sum(v, z):
    n = lax.axis_size("z")
    if n == 4:
        inner = add_low(v, lax.ppermute(v, "z", [(0, 1), (3, 2)]))
        whole = add_low(inner, lax.ppermute(inner, "z", [(1, 2), (2, 1)]))
        outer = lax.ppermute(whole, "z", [(1, 0), (2, 3)])
        return jnp.where((z == 0) | (z == 3), outer, whole)
    bit = 1
    while bit < n:
        v = add_low(v, lax.ppermute(v, "z", [(i, i ^ bit) for i in range(n)]))
        bit *= 2
    return v


def plane_reduce(mine, other, y, x):
    n = lax.axis_size("y")
    rows = mine.shape[0] // (2 * n)
    h = rows // 2
    got = swap(other, "core")

    def block(dy, dx, part):
        place = (lax.rem(y + dy, n) * 2 + (x if dx == 0 else 1 - x)) * rows + part * h
        one = lax.dynamic_slice_in_dim(mine, place, h, 0)
        two = lax.dynamic_slice_in_dim(got, place, h, 0)
        return one.astype(F32) + two.astype(F32)

    sent_a = swap(jnp.stack([block(dy, 1, 0) for dy in range(n)]).astype(BF), "x")
    sent_b = [
        to_y(jnp.stack([block(d, 0, 1), block(d, 1, 1)]).astype(BF), d) for d in range(1, n)
    ]
    part_a = [block(dy, 0, 0) + sent_a[dy].astype(F32) for dy in range(n)]
    part_b = [
        block(0, dx, 1) + sum(got_b[dx].astype(F32) for got_b in sent_b) for dx in range(2)
    ]
    total_a = part_a[0]
    for d in range(1, n):
        total_a = total_a + to_y(part_a[d].astype(BF), d).astype(F32)
    total_b = part_b[0] + swap(part_b[1].astype(BF), "x").astype(F32)
    return total_a.astype(BF), total_b.astype(BF)


def whole_grad(mine, other, y, x, z, core):
    parts = []
    for part in plane_reduce(mine, other, y, x):
        part = z_sum(part, z)
        beside = swap(part, "core")
        parts.append((part, beside))
    a, b = parts
    own = jnp.concatenate([a[0], b[0]], axis=0).astype(F32)
    beside = jnp.concatenate([a[1], b[1]], axis=0).astype(F32)
    return jnp.where(
        core == 0,
        jnp.concatenate([own, beside], axis=1),
        jnp.concatenate([beside, own], axis=1),
    )


class Gathered:
    def __init__(self, own, halves, core_axis_halves):
        self.pieces = own + halves + core_axis_halves
        self.arrays = [piece[0] for piece in self.pieces]
        self.places = [piece[1:] for piece in self.pieces]


def gather_weight(own_full, own_a, own_b, half_width):
    rows = own_a.shape[0]
    own = [(array, (0, 0), 0, first) for array, first in own_full]
    mine, beside = [], []
    for where, (a, b) in plane_gather(own_a, own_b).items():
        for array, row in ((a, 0), (b, rows)):
            mine.append((array, where, row, "mine"))
            beside.append((swap(array, "core"), where, row, "other"))
    return Gathered(own, mine, beside)


def start_load(refs, places, dst, sems, ids, ny, shard, half_width):
    core, y, x = ids[1], ids[2], ids[3]
    copies = []
    for k, (ref, ((dy, dx), row, column)) in enumerate(zip(refs, places)):
        owner = lax.rem(y + dy, ny) * 2 + (x if dx == 0 else 1 - x)
        if column == "mine":
            column = core * half_width
        elif column == "other":
            column = (1 - core) * half_width
        if not isinstance(column, int):
            column = pl.multiple_of(column, 128)
        first = pl.multiple_of(owner * shard + row, 16)
        copy = pltpu.make_async_copy(
            ref,
            dst.at[pl.ds(first, ref.shape[0]), pl.ds(column, ref.shape[1])],
            sems.at[k],
        )
        copy.start()
        copies.append(copy)
    return copies


def gathered_matmul(lhs, weight, ids, ny, shard, width):
    count = len(weight.arrays)
    depth = 2 * ny * shard

    def kernel(ids_ref, lhs_ref, *refs):
        pieces, out_ref, held, sems = refs[:count], refs[count], refs[count + 1], refs[count + 2]
        for copy in start_load(pieces, weight.places, held, sems, ids_ref, ny, shard, width // 2):
            copy.wait()
        out_ref[...] = nn(lhs_ref[...], held[...]).astype(BF)

    return pl.pallas_call(
        kernel,
        out_shape=shape((lhs.shape[0], width), BF),
        in_specs=[SMEM, VMEM] + [ANY] * count,
        out_specs=VMEM,
        scratch_shapes=[pltpu.VMEM((depth, width), BF), pltpu.SemaphoreType.DMA((count,))],
        compiler_params=params(),
        cost_estimate=cost(2 * lhs.shape[0] * depth * width, 2 * depth * width + 2 * lhs.size),
        name="project",
    )(ids, lhs, *weight.arrays)


def load_keys(nz, half, ids, refs, kv, sems):
    z = ids[0]
    own, beside = refs[0], refs[1]
    slot = 2 * half

    def place(index, second):
        return kv.at[pl.ds(pl.multiple_of(index * slot + second * half, half), half)]

    always = []
    for k, ref in enumerate((own, beside)):
        always.append(pltpu.make_async_copy(ref.at[pl.ds(0, half)], place(0, k), sems.at[2 * k]))
        always.append(
            pltpu.make_async_copy(ref.at[pl.ds(half, half)], place(z + 1, k), sems.at[2 * k + 1])
        )
    for copy in always:
        copy.start()
    guarded = []
    for d in range(1, nz):
        group = refs[2 + 4 * (d - 1) : 2 + 4 * d]
        base = 4 + 4 * (d - 1)
        low = [pltpu.make_async_copy(group[k], place(d, k), sems.at[base + k]) for k in range(2)]
        high = [
            pltpu.make_async_copy(group[2 + k], place(z + 1 + d, k), sems.at[base + 2 + k])
            for k in range(2)
        ]
        guarded.append((d <= z, low))
        guarded.append((z + d < nz, high))
    for needed, copies in guarded:

        @pl.when(needed)
        def _():
            for copy in copies:
                copy.start()

    for copy in always:
        copy.wait()
    for needed, copies in guarded:

        @pl.when(needed)
        def _():
            for copy in copies:
                copy.wait()


def slot_range(nz, ids, tile):
    z, core = ids[0], ids[1]
    if tile == 0:
        return 0, z + 1
    last = (z == nz - 1) & (core == 1)
    return jnp.where(last, 0, z + 1), nz + 1


def fill_masks(nz, half, ids, seg_col, seg_row, masks):
    z, core = ids[0], ids[1]
    blocks = 4 * nz
    own = 2 * z + core
    for tile in range(2):
        query_block = own if tile == 0 else blocks - 1 - own
        query_at = pl.multiple_of(query_block * half, half)
        query_seg = seg_row[:, pl.ds(query_at, half)]
        query_pos = query_at + lax.broadcasted_iota(jnp.int32, (1, half), 1)
        first, end = slot_range(nz, ids, tile)

        def fill(index, unused):
            for second in range(2):
                side = core if second == 0 else 1 - core
                key_block = jnp.where(
                    index <= z, 2 * (z - index) + side, blocks - 1 - (2 * (index - 1) + side)
                )
                key_at = pl.multiple_of(key_block * half, half)
                key_seg = seg_col[pl.ds(key_at, half), :]
                key_pos = key_at + lax.broadcasted_iota(jnp.int32, (half, 1), 0)
                allowed = (key_seg == query_seg) & (key_pos <= query_pos)
                masks[tile, index, second * half : (second + 1) * half, :] = jnp.where(
                    allowed, 0.0, NEG_LARGE
                )
            return unused

        lax.fori_loop(first, end, fill, 0)


def split_heads(tile_rows, scale=None):
    half = tile_rows.shape[0]
    if scale is not None:
        tile_rows = tile_rows * jnp.asarray(scale, tile_rows.dtype)
    lane = lax.broadcasted_iota(jnp.int32, (half, 128), 1)
    zero = jnp.zeros((half, 128), tile_rows.dtype)
    t0, t1, t2 = (tile_rows[:, 128 * k : 128 * k + 128] for k in range(3))

    def low(t):
        return jnp.where(lane < 64, t, zero)

    def high(t):
        return jnp.where(lane >= 64, t, zero)

    straight = jnp.concatenate([low(t0), low(t1), high(t1), high(t2)], axis=0)
    crossed = jnp.concatenate([high(t0), low(t2)], axis=0)
    return straight, crossed


def join_heads(straight_t, crossed_t, half):
    def head(t, k, upper):
        return t[64 * upper : 64 * upper + 64, half * k : half * k + half]

    tiles = (
        (head(straight_t, 0, 0), head(crossed_t, 0, 1)),
        (head(straight_t, 1, 0), head(straight_t, 2, 1)),
        (head(crossed_t, 1, 0), head(straight_t, 3, 1)),
    )
    return jnp.concatenate([jnp.concatenate(t, axis=0).T for t in tiles], axis=1)


def cross(v):
    return jnp.concatenate([v[:, 64:], v[:, :64]], axis=1)


def attention_forward(q, keys, seg_col, seg_row, ids, nz):
    rows = q.shape[0]
    half = rows // 2
    slots = nz + 1
    count = len(keys)
    slot = 2 * half
    lanes = 6 * half

    def kernel(ids_ref, q_ref, col_ref, row_ref, *refs):
        key_refs = refs[:count]
        out_ref, lse_ref, kv, scores, masks, sems = refs[count:]
        fill_masks(nz, half, ids_ref, col_ref, row_ref, masks)
        load_keys(nz, half, ids_ref, key_refs, kv, sems)
        for tile in range(2):
            first, end = slot_range(nz, ids_ref, tile)
            for pair in range(PAIRS):
                straight, crossed = split_heads(
                    q_ref[tile * half : (tile + 1) * half, 384 * pair : 384 * pair + 384], SCALE
                )

                def score(index, peak):
                    at = pl.ds(pl.multiple_of(index * slot, slot), slot)
                    k = kv[at, 128 * pair : 128 * pair + 128]
                    mask = masks[tile, index]
                    s = jnp.concatenate([nt(k, straight), nt(cross(k), crossed)], axis=1)
                    s = s + jnp.concatenate([mask] * 6, axis=1)
                    scores[index] = s
                    return jnp.maximum(peak, jnp.max(s, axis=0, keepdims=True))

                peak = lax.fori_loop(
                    first, end, score, jnp.full((1, lanes), NEG_LARGE, F32)
                )

                def mix(index, carry):
                    mass, out_s, out_c = carry
                    at = pl.ds(pl.multiple_of(index * slot, slot), slot)
                    v = kv[at, 512 + 128 * pair : 512 + 128 * pair + 128]
                    p = jnp.exp(scores[index] - peak)
                    mass = mass + jnp.sum(p, axis=0, keepdims=True)
                    p = p.astype(BF)
                    v_t = v.T
                    out_s = out_s + nn(v_t, p[:, : 4 * half])
                    out_c = out_c + nn(
                        jnp.concatenate([v_t[64:], v_t[:64]], axis=0), p[:, 4 * half :]
                    )
                    return mass, out_s, out_c

                mass, out_s, out_c = lax.fori_loop(
                    first,
                    end,
                    mix,
                    (
                        jnp.zeros((1, lanes), F32),
                        jnp.zeros((128, 4 * half), F32),
                        jnp.zeros((128, 2 * half), F32),
                    ),
                )
                share = 1.0 / mass
                out_s = out_s * share[:, : 4 * half]
                out_c = out_c * share[:, 4 * half :]
                out_ref[tile * half : (tile + 1) * half, 384 * pair : 384 * pair + 384] = (
                    join_heads(out_s, out_c, half).astype(BF)
                )
                spot = tile * PAIRS + pair
                lse_ref[spot : spot + 1, :] = peak + jnp.log(mass)

    pairs = slots * slot * half * HEADS
    return pl.pallas_call(
        kernel,
        out_shape=(shape(q.shape, BF), shape((2 * PAIRS, lanes), F32)),
        in_specs=[SMEM, VMEM, VMEM, VMEM] + [ANY] * count,
        out_specs=(VMEM, VMEM),
        scratch_shapes=[
            pltpu.VMEM((slots * slot, 1024), BF),
            pltpu.VMEM((slots, slot, lanes), F32),
            pltpu.VMEM((2, slots, slot, half), F32),
            pltpu.SemaphoreType.DMA((4 * nz,)),
        ],
        compiler_params=params(),
        cost_estimate=cost(8 * 256 * pairs, 2 * slots * slot * 1024, pairs),
        name="attend",
    )(ids, q, seg_col, seg_row, *keys)


def attention_backward(q, keys, seg_col, seg_row, attended, grad_att, lse, ids, nz):
    rows = q.shape[0]
    half = rows // 2
    slots = nz + 1
    count = len(keys)
    slot = 2 * half
    lanes = 6 * half

    def kernel(ids_ref, q_ref, col_ref, row_ref, att_ref, grad_ref, lse_ref, *refs):
        key_refs = refs[:count]
        dq_ref, mine_ref, other_ref, kv, dkv, masks, sems = refs[count:]
        fill_masks(nz, half, ids_ref, col_ref, row_ref, masks)
        dkv[...] = jnp.zeros_like(dkv)
        load_keys(nz, half, ids_ref, key_refs, kv, sems)
        for tile in range(2):
            first, end = slot_range(nz, ids_ref, tile)
            for pair in range(PAIRS):
                here = (slice(tile * half, (tile + 1) * half), slice(384 * pair, 384 * pair + 384))
                q_s, q_c = split_heads(q_ref[here], SCALE)
                g_s, g_c = split_heads(grad_ref[here])
                product = grad_ref[here].astype(F32) * att_ref[here].astype(F32)
                turned = [product[:, 128 * k : 128 * k + 128].T for k in range(3)]
                lower = [jnp.sum(t[:64], axis=0, keepdims=True) for t in turned]
                upper = [jnp.sum(t[64:], axis=0, keepdims=True) for t in turned]
                delta = jnp.concatenate(
                    [lower[0], lower[1], upper[1], upper[2], upper[0], lower[2]], axis=1
                )
                spot = tile * PAIRS + pair
                total = lse_ref[spot : spot + 1, :]

                def step(index, carry):
                    dq_s, dq_c = carry
                    at = pl.ds(pl.multiple_of(index * slot, slot), slot)
                    k_lanes = slice(128 * pair, 128 * pair + 128)
                    v_lanes = slice(512 + 128 * pair, 512 + 128 * pair + 128)
                    k, v = kv[at, k_lanes], kv[at, v_lanes]
                    mask = masks[tile, index]
                    s = jnp.concatenate([nt(k, q_s), nt(cross(k), q_c)], axis=1)
                    p = jnp.exp(s + jnp.concatenate([mask] * 6, axis=1) - total)
                    dp = jnp.concatenate([nt(v, g_s), nt(cross(v), g_c)], axis=1)
                    ds = (p * (dp - delta)).astype(BF)
                    p = p.astype(BF)
                    dkv[at, v_lanes] += nn(p[:, : 4 * half], g_s) + cross(
                        nn(p[:, 4 * half :], g_c)
                    )
                    dkv[at, k_lanes] += nn(ds[:, : 4 * half], q_s) + cross(
                        nn(ds[:, 4 * half :], q_c)
                    )
                    k_t = k.T
                    dq_s = dq_s + nn(k_t, ds[:, : 4 * half])
                    dq_c = dq_c + nn(
                        jnp.concatenate([k_t[64:], k_t[:64]], axis=0), ds[:, 4 * half :]
                    )
                    return dq_s, dq_c

                dq_s, dq_c = lax.fori_loop(
                    first,
                    end,
                    step,
                    (jnp.zeros((128, 4 * half), F32), jnp.zeros((128, 2 * half), F32)),
                )
                dq_ref[here] = (SCALE * join_heads(dq_s, dq_c, half)).astype(BF)
        for index in range(slots):
            mine_ref[index] = dkv[index * slot : index * slot + half, :].astype(BF)
            other_ref[index] = dkv[index * slot + half : (index + 1) * slot, :].astype(BF)

    pairs = slots * slot * half * HEADS
    return pl.pallas_call(
        kernel,
        out_shape=(
            shape(q.shape, BF),
            shape((slots, half, 1024), BF),
            shape((slots, half, 1024), BF),
        ),
        in_specs=[SMEM] + [VMEM] * 6 + [ANY] * count,
        out_specs=(VMEM,) * 3,
        scratch_shapes=[
            pltpu.VMEM((slots * slot, 1024), BF),
            pltpu.VMEM((slots * slot, 1024), F32),
            pltpu.VMEM((2, slots, slot, half), F32),
            pltpu.SemaphoreType.DMA((4 * nz,)),
        ],
        compiler_params=params(),
        cost_estimate=cost(20 * 256 * pairs, 2 * slots * slot * 1024, pairs),
        name="attend_back",
    )(ids, q, seg_col, seg_row, attended, grad_att, lse, *keys)


def out_project(tokens, attended, gain, weight, ids, ny, shard):
    rows, width = tokens.shape
    count = len(weight.arrays)

    def kernel(ids_ref, tokens_ref, att_ref, gain_ref, *refs):
        pieces = refs[:count]
        resid_ref, norm_ref, held, sems = refs[count:]
        for copy in start_load(pieces, weight.places, held, sems, ids_ref, ny, shard, width // 2):
            copy.wait()
        resid = tokens_ref[...].astype(F32) + nn(att_ref[...], held[...])
        resid_ref[...] = resid
        norm_ref[...] = (resid * inv_root(resid) * gain_ref[...].astype(F32)).astype(BF)

    return pl.pallas_call(
        kernel,
        out_shape=(shape((rows, width), F32), shape((rows, width), BF)),
        in_specs=[SMEM] + [VMEM] * 3 + [ANY] * count,
        out_specs=(VMEM, VMEM),
        scratch_shapes=[pltpu.VMEM((width, width), BF), pltpu.SemaphoreType.DMA((count,))],
        compiler_params=params(),
        cost_estimate=cost(2 * rows * width * width, 2 * width * width + 10 * rows * width),
        name="out_project",
    )(ids, tokens, attended, gain, *weight.arrays)


def out_back(resid, cotangent, gain, terms, weight, ids, ny, shard):
    rows, width = resid.shape
    count = len(weight.arrays)
    term_count = len(terms)

    def kernel(ids_ref, resid_ref, cot_ref, gain_ref, *refs):
        term_refs, pieces = refs[:term_count], refs[term_count : term_count + count]
        gres_ref, branch_ref, gatt_ref, ggain_ref, held, sems = refs[term_count + count :]
        copies = start_load(pieces, weight.places, held, sems, ids_ref, ny, shard, width // 2)
        grad_norm = term_refs[0][...].astype(F32)
        for ref in term_refs[1:]:
            grad_norm = grad_norm + ref[...].astype(F32)
        resid = resid_ref[...]
        root = inv_root(resid)
        s = resid * root
        ggain_ref[...] = jnp.sum(grad_norm * s, axis=0, keepdims=True)
        t = grad_norm * gain_ref[...].astype(F32)
        gres = cot_ref[...].astype(F32) + root * (
            t - s * jnp.mean(t * s, axis=-1, keepdims=True)
        )
        gres_ref[...] = gres
        branch = gres.astype(BF)
        branch_ref[...] = branch
        for copy in copies:
            copy.wait()
        gatt_ref[...] = nt(branch, held[...]).astype(BF)

    return pl.pallas_call(
        kernel,
        out_shape=(
            shape((rows, width), F32),
            shape((rows, width), BF),
            shape((rows, width), BF),
            shape((1, width), F32),
        ),
        in_specs=[SMEM] + [VMEM] * (3 + term_count) + [ANY] * count,
        out_specs=(VMEM,) * 4,
        scratch_shapes=[pltpu.VMEM((width, width), BF), pltpu.SemaphoreType.DMA((count,))],
        compiler_params=params(),
        cost_estimate=cost(2 * rows * width * width, 2 * width * width + 20 * rows * width),
        name="out_back",
    )(ids, resid, cotangent, gain, *terms, *weight.arrays)


def in_back(tokens, gres, gain, dq, dkv, weight_q, weight_kv, ids, ny, shard):
    rows, width = tokens.shape
    kv_width = dkv.shape[1]
    count_q, count_kv = len(weight_q.arrays), len(weight_kv.arrays)

    def kernel(ids_ref, tokens_ref, gres_ref, gain_ref, dq_ref, dkv_ref, *refs):
        q_pieces, kv_pieces = refs[:count_q], refs[count_q : count_q + count_kv]
        out_ref, ggain_ref, held_q, held_kv, sems_q, sems_kv = refs[count_q + count_kv :]
        copies = start_load(
            kv_pieces, weight_kv.places, held_kv, sems_kv, ids_ref, ny, shard, kv_width // 2
        ) + start_load(q_pieces, weight_q.places, held_q, sems_q, ids_ref, ny, shard, width // 2)
        for copy in copies:
            copy.wait()
        grad_norm = nt(dq_ref[...], held_q[...]) + nt(dkv_ref[...], held_kv[...])
        x = tokens_ref[...].astype(F32)
        root = inv_root(x)
        s = x * root
        ggain_ref[...] = jnp.sum(grad_norm * s, axis=0, keepdims=True)
        t = grad_norm * gain_ref[...].astype(F32)
        out_ref[...] = gres_ref[...] + root * (t - s * jnp.mean(t * s, axis=-1, keepdims=True))

    return pl.pallas_call(
        kernel,
        out_shape=(shape((rows, width), F32), shape((1, width), F32)),
        in_specs=[SMEM] + [VMEM] * 5 + [ANY] * (count_q + count_kv),
        out_specs=(VMEM, VMEM),
        scratch_shapes=[
            pltpu.VMEM((width, width), BF),
            pltpu.VMEM((width, kv_width), BF),
            pltpu.SemaphoreType.DMA((count_q,)),
            pltpu.SemaphoreType.DMA((count_kv,)),
        ],
        compiler_params=params(),
        cost_estimate=cost(
            2 * rows * width * (width + kv_width), 2 * width * (width + kv_width) + 12 * rows * width
        ),
        name="in_back",
    )(ids, tokens, gres, gain, dq, dkv, *weight_q.arrays, *weight_kv.arrays)


def expert_block(normed, cots, coeff, w_gate, w_up, w_down, out_dtype):
    experts, width, units = w_gate.shape
    half = normed[0].shape[0]
    rows = 2 * half

    def kernel(na, nb, ca, cb, coeff_ref, wg_ref, wu_ref, wd_ref, hid_ref, gg_ref, gu_ref,
               mix_ref, gnf_ref, n_all, c_all, mix, gnf):
        e = pl.program_id(0)

        @pl.when(e == 0)
        def _():
            n_all[:half] = na[...]
            n_all[half:] = nb[...]
            c_all[:half] = ca[...]
            c_all[half:] = cb[...]

        wg, wu, wd = wg_ref[0], wu_ref[0], wd_ref[0]
        rows_in, cot = n_all[...], c_all[...]
        lane = lax.broadcasted_iota(jnp.int32, coeff_ref.shape, 1)
        weight = jnp.sum(jnp.where(lane == e, coeff_ref[...], 0.0), axis=1, keepdims=True)
        gate = nn(rows_in, wg)
        up = nn(rows_in, wu)
        back = nt(cot, wd) * weight
        sigma = jax.nn.sigmoid(gate)
        silu = gate * sigma
        hidden = (silu * up * weight).astype(BF)
        grad_gate = (back * up * sigma * (1.0 + gate * (1.0 - sigma))).astype(BF)
        grad_up = (back * silu).astype(BF)
        hid_ref[...] = hidden
        gg_ref[...] = grad_gate
        gu_ref[...] = grad_up
        more = nt(grad_gate, wg) + nt(grad_up, wu)
        out = nn(hidden, wd)

        @pl.when(e == 0)
        def _():
            gnf[...] = more
            mix[...] = out

        @pl.when(e > 0)
        def _():
            gnf[...] += more
            mix[...] += out

        @pl.when(e == experts - 1)
        def _():
            gnf_ref[...] = gnf[...].astype(gnf_ref.dtype)
            mix_ref[...] = mix[...].astype(mix_ref.dtype)

    whole = pl.BlockSpec((half, width), lambda e: (0, 0))
    keep = pl.BlockSpec((rows, width), lambda e: (0, 0))
    unit = pl.BlockSpec((rows, units), lambda e: (0, e))
    return pl.pallas_call(
        kernel,
        grid=(experts,),
        out_shape=(shape((rows, experts * units), BF),) * 3
        + (shape((rows, width), out_dtype),) * 2,
        in_specs=[whole] * 4
        + [
            pl.BlockSpec(coeff.shape, lambda e: (0, 0)),
            pl.BlockSpec((1, width, units), lambda e: (e, 0, 0)),
            pl.BlockSpec((1, width, units), lambda e: (e, 0, 0)),
            pl.BlockSpec((1, units, width), lambda e: (e, 0, 0)),
        ],
        out_specs=(unit, unit, unit, keep, keep),
        scratch_shapes=[pltpu.VMEM((rows, width), BF)] * 2 + [pltpu.VMEM((rows, width), F32)] * 2,
        compiler_params=params(),
        cost_estimate=cost(
            12 * rows * width * experts * units, 6 * experts * width * units + 10 * rows * width
        ),
        name="experts",
    )(*normed, *cots, coeff, w_gate, w_up, w_down)


def expert_grads(first, normed, cots, hidden, grad_gate, grad_up, experts):
    blocks = len(hidden)
    half, width = normed[0].shape
    rows = hidden[0].shape[0]
    units = hidden[0].shape[1] // experts
    pieces = 2 * blocks

    def kernel(first_ref, *refs):
        n_refs, c_refs = refs[:pieces], refs[pieces : 2 * pieces]
        at = 2 * pieces
        h_refs, gg_refs, gu_refs = (
            refs[at : at + blocks],
            refs[at + blocks : at + 2 * blocks],
            refs[at + 2 * blocks : at + 3 * blocks],
        )
        og_ref, ou_ref, od_ref, n_all, c_all, sems = refs[at + 3 * blocks :]

        @pl.when(pl.program_id(0) == 0)
        def _():
            copies = []
            for k in range(pieces):
                to = pl.ds(k * half, half)
                copies.append(pltpu.make_async_copy(n_refs[k], n_all.at[to], sems.at[0, k]))
                copies.append(pltpu.make_async_copy(c_refs[k], c_all.at[to], sems.at[1, k]))
            for copy in copies:
                copy.start()
            for copy in copies:
                copy.wait()

        grads = jnp.concatenate(
            [
                jnp.concatenate([ref[...] for ref in gg_refs], axis=0),
                jnp.concatenate([ref[...] for ref in gu_refs], axis=0),
            ],
            axis=1,
        )
        both = tn(n_all[...], grads)
        og_ref[0] = both[:, :units].astype(BF)
        ou_ref[0] = both[:, units:].astype(BF)
        hid = jnp.concatenate([ref[...] for ref in h_refs], axis=0)
        od_ref[0] = tn(hid, c_all[...]).astype(BF)

    unit = pl.BlockSpec((rows, units), lambda e, first: (0, first[0] + e))
    grid_spec = pltpu.PrefetchScalarGridSpec(
        num_scalar_prefetch=1,
        grid=(experts // 2,),
        in_specs=[ANY] * (2 * pieces) + [unit] * (3 * blocks),
        out_specs=(
            pl.BlockSpec((1, width, units), lambda e, first: (e, 0, 0)),
            pl.BlockSpec((1, width, units), lambda e, first: (e, 0, 0)),
            pl.BlockSpec((1, units, width), lambda e, first: (e, 0, 0)),
        ),
        scratch_shapes=[
            pltpu.VMEM((blocks * rows, width), BF),
            pltpu.VMEM((blocks * rows, width), BF),
            pltpu.SemaphoreType.DMA((2, pieces)),
        ],
    )
    count = experts // 2
    return pl.pallas_call(
        kernel,
        grid_spec=grid_spec,
        out_shape=(
            shape((count, width, units), BF),
            shape((count, width, units), BF),
            shape((count, units, width), BF),
        ),
        compiler_params=params(),
        cost_estimate=cost(
            6 * blocks * rows * width * units * count,
            4 * blocks * rows * width + 6 * count * units * width,
        ),
        name="expert_grads",
    )(first, *normed, *cots, *hidden, *grad_gate, *grad_up)


def spread_halves(mine, beside, core):
    count, a, b = mine.shape

    def kernel(core_ref, mine_ref, beside_ref, out_ref):
        is_mine = pl.program_id(0) // count == core_ref[0]

        @pl.when(is_mine)
        def _():
            out_ref[...] = mine_ref[...].astype(F32)

        @pl.when(jnp.logical_not(is_mine))
        def _():
            out_ref[...] = beside_ref[...].astype(F32)

    block = (1, a, b)
    source = pl.BlockSpec(block, lambda e, core: (lax.rem(e, count), 0, 0))
    return pl.pallas_call(
        kernel,
        grid_spec=pltpu.PrefetchScalarGridSpec(
            num_scalar_prefetch=1,
            grid=(2 * count,),
            in_specs=[source, source],
            out_specs=pl.BlockSpec(block, lambda e, core: (e, 0, 0)),
        ),
        out_shape=shape((2 * count, a, b), F32),
        compiler_params=params(),
        cost_estimate=cost(0, 16 * count * a * b),
        name="spread",
    )(core, mine, beside)


def body(
    tokens,
    segments,
    routes,
    route_weights,
    gain_attn,
    w_query,
    w_key,
    w_value,
    w_out,
    gain_ffn,
    w_gate,
    w_up,
    w_down,
    cotangent,
):
    tokens, cotangent = tokens[0], cotangent[0]
    rows, width = tokens.shape
    half = rows // 2
    nz, ny = lax.axis_size("z"), lax.axis_size("y")
    z, core, y, x = (lax.axis_index(a) for a in ("z", "core", "y", "x"))
    ids = jnp.stack([z, core, y, x]).astype(jnp.int32)
    shard = w_query.shape[0]
    sh = shard // 2
    experts = w_gate.shape[0]
    kv_width = w_key.shape[1] + w_value.shape[1]
    hw = width // 2
    plane = [(dy, dx) for dy in range(ny) for dx in range(2)]
    seg_row = segments
    seg_col = segments.reshape(-1, 1)

    gains = jnp.stack([gain_attn, gain_ffn])
    owners = {}
    for dy, dx in plane:
        got = gains if (dy, dx) == (0, 0) else to_plane(gains, dy, dx)
        owner = lax.rem(y - dy + ny, ny) * 2 + (x if dx == 0 else 1 - x)
        owners[(dy, dx)] = (owner, got)
    slot = jnp.arange(2 * ny, dtype=jnp.int32)[None, :, None]
    all_gains = sum(
        jnp.where(slot == owner, got[:, None, :], jnp.zeros((), BF))
        for owner, got in owners.values()
    ).reshape(2, 1, width)
    gain_a, gain_f = all_gains[0], all_gains[1]

    kv_half = jnp.where(core == 0, w_key, w_value)
    weight_kv = gather_weight(
        [(w_key, 0), (w_value, kv_width // 2)], kv_half[:sh], kv_half[sh:], kv_width // 2
    )

    def column_half(w, row, count):
        return lax.dynamic_slice(w, (row, core * (w.shape[1] // 2)), (count, w.shape[1] // 2))

    weight_q = gather_weight(
        [(w_query, 0)], column_half(w_query, 0, sh), column_half(w_query, sh, sh), hw
    )
    weight_o = gather_weight(
        [(w_out, 0)], column_half(w_out, 0, sh), column_half(w_out, sh, sh), hw
    )

    x_f = tokens.astype(F32)
    normed = (x_f * inv_root(x_f) * gain_a.astype(F32)).astype(BF)
    kv = gathered_matmul(normed, weight_kv, ids, ny, shard, kv_width)
    keys = [kv, swap(kv, "core")]
    for d in range(1, nz):
        low, high = z_move(kv[:half], d), z_move(kv[half:], -d)
        keys += [low, swap(low, "core"), high, swap(high, "core")]
    queries = gathered_matmul(normed, weight_q, ids, ny, shard, width)
    attended, lse = attention_forward(queries, keys, seg_col, seg_row, ids, nz)
    resid, normed_f = out_project(tokens, attended, gain_f, weight_o, ids, ny, shard)

    chosen = routes[0][:, :, None] == jnp.arange(experts, dtype=jnp.int32)[None, None, :]
    coeff = jnp.sum(jnp.where(chosen, route_weights[0][:, :, None], 0.0), axis=1)
    coeffs = {(dy, dx): to_plane(coeff, -dy % ny, dx) for dy, dx in plane if (dy, dx) != (0, 0)}
    coeffs[(0, 0)] = coeff
    cots = plane_gather(cotangent[:half], cotangent[half:])
    cots[(0, 0)] = (cotangent[:half], cotangent[half:])
    norms = plane_gather(normed_f[:half], normed_f[half:])
    norms[(0, 0)] = (normed_f[:half], normed_f[half:])
    order = sorted(plane, key=lambda p: (p[0] != 0) + (p[1] != 0))
    hidden, grad_gate, grad_up, mixes, grad_norms = [], [], [], [], []
    for where in order:
        own = where == (0, 0)
        h, gg, gu, mix, gnf = expert_block(
            norms[where], cots[where], coeffs[where], w_gate, w_up, w_down, F32 if own else BF
        )
        hidden.append(h)
        grad_gate.append(gg)
        grad_up.append(gu)
        mixes.append(mix if own else to_plane(mix, *where))
        grad_norms.append(gnf if own else to_plane(gnf, *where))
    flat_norms = [piece for where in order for piece in norms[where]]
    flat_cots = [piece for where in order for piece in cots[where]]
    count = experts // 2

    def half_grads(which):
        first = (which * count).astype(jnp.int32).reshape(1)
        return expert_grads(first, flat_norms, flat_cots, hidden, grad_gate, grad_up, experts)

    far, near = half_grads(1 - core), half_grads(core)
    expert_totals = []
    for one, two in zip(near, far):
        got = swap(two, "core")
        parts, besides = [], []
        for e in range(count):
            part = z_sum(add_low(one[e], got[e]), z)
            parts.append(part)
            besides.append(swap(part, "core"))
        expert_totals.append(
            spread_halves(
                jnp.stack(parts), jnp.stack(besides), core.astype(jnp.int32).reshape(1)
            )
        )
    result = resid
    for mix in mixes:
        result = result + mix.astype(F32)

    gres, branch, grad_att, ggain_f = out_back(
        resid, cotangent, gain_f, grad_norms, weight_o, ids, ny, shard
    )

    def columns(v, which):
        n = v.shape[1] // 2
        return lax.dynamic_slice(v, (0, which * n), (v.shape[0], n))

    def weight_grad(left, right):
        return tuple(tn(left, columns(right, which)).astype(BF) for which in (core, 1 - core))

    grad_wo = whole_grad(*weight_grad(attended, branch), y, x, z, core)
    dq, dkv_mine, dkv_other = attention_backward(
        queries, keys, seg_col, seg_row, attended, grad_att, lse, ids, nz
    )
    parts = add_low(dkv_mine, swap(dkv_other, "core"))
    low = parts[0].astype(F32)
    high = lax.dynamic_index_in_dim(parts, z + 1, 0, keepdims=False).astype(F32)
    for d in range(1, nz):
        low = low + z_move(parts[d], -d).astype(F32)
        far_high = lax.dynamic_index_in_dim(
            parts, jnp.minimum(z + 1 + d, nz), 0, keepdims=False
        )
        high = high + z_move(far_high, d).astype(F32)
    dkv = jnp.concatenate([low, high], axis=0).astype(BF)
    grad_wq = whole_grad(*weight_grad(normed, dq), y, x, z, core)
    grad_wkv = whole_grad(*weight_grad(normed, dkv), y, x, z, core)
    grad_tokens, ggain_a = in_back(
        tokens, gres, gain_a, dq, dkv, weight_q, weight_kv, ids, ny, shard
    )

    ggains = jnp.concatenate([ggain_a, ggain_f], axis=0)
    ggains = ggains + swap(ggains, "core")
    ggains = ggains.reshape(2, 2 * ny, shard)

    def gain_block(dy, dx):
        place = lax.rem(y + dy, ny) * 2 + (x if dx == 0 else 1 - x)
        return lax.dynamic_index_in_dim(ggains, place, 1, keepdims=False)

    total = gain_block(0, 0)
    for dy, dx in plane[1:]:
        total = total + to_plane(gain_block(dy, dx), dy, dx)
    total = z_sum(total, z)
    kv_cut = w_key.shape[1]
    return (
        result.astype(BF)[None],
        grad_tokens[None],
        total[0],
        grad_wq,
        grad_wkv[:, :kv_cut],
        grad_wkv[:, kv_cut:],
        grad_wo,
        total[1],
        *expert_totals,
    )


def solution(mesh):
    ctx, wt = mesh.shape["ctx"], mesh.shape["wt"]
    fine = Mesh(mesh.devices.reshape(ctx // 2, 2, wt // 2, 2), ("z", "core", "y", "x"))
    c, w = ("z", "core"), ("y", "x")
    rows = P(w, c, None)
    return jax.shard_map(
        body,
        mesh=fine,
        in_specs=(
            rows,
            P(w, None),
            rows,
            rows,
            P(w),
            P(w, None),
            P(w, None),
            P(w, None),
            P(w, None),
            P(w),
            P(None, None, w),
            P(None, None, w),
            P(None, w, None),
            rows,
        ),
        out_specs=(
            rows,
            rows,
            P(w),
            P(w, None),
            P(w, None),
            P(w, None),
            P(w, None),
            P(w),
            P(None, None, w),
            P(None, None, w),
            P(None, w, None),
        ),
        check_vma=False,
    )
```

time: 2660 us -> 785 us (0.30)
  waiting for transfers between devices: 1880 us -> 326 us
  matrix products: 328 us -> 8.75 us
  local copies, waits for them, and re-layouts: 303 us -> 16.8 us
  starting transfers between devices: 0.76 us -> 209 us
  Pallas kernels: 0 us -> 165 us
  blocking collectives: 47.7 us -> 0 us
  other arithmetic: 74.8 us -> 46.3 us
    reduce_scatter x9 -> x0, waiting for transfers between devices: 1000 us -> none  [the longest x1 225 us: body(): lax.psum_scatter(grad_up_w, 'wt', scatter_dimension=2, tiled=True)]
    psum x1 -> x0, waiting for transfers between devices: 456 us -> none  [body(): lax.psum((shard_ga, shard_q, shard_k, shard_v, shard_o, shard_gf, shard_g...]
    all_gather x9 -> x0, waiting for transfers between devices: 415 us -> none  [the longest x1 116 us: body(): lax.all_gather(w_down, 'wt', axis=1, tiled=True)]
    ppermute x0 -> x153, waiting for transfers between devices: none -> 326 us  [the longest x13 161 us: z_sum(): outer = lax.ppermute(whole, 'z', [(1, 0), (2, 3)])]
    dot_general x57 -> x6, matrix products: 328 us -> 8.75 us  [tn(): lax.dot_general(a, b, (((0,), (0,)), ((), ())), preferred_element_type=F32)]
    ppermute x0 -> x153, starting transfers between devices: none -> 209 us  [the longest x12 62.9 us: z_move(): lax.ppermute(v, 'z', [(i, i + d) for i in range(n) if 0 <= i + d < n])]
    dynamic_update_slice x16 -> x0, local copies, waits for them, and re-layouts: 177 us -> none  [body(): lax.scan(grad_step, jnp.zeros(head_shape, jnp.float32), blocked_all)]
    pallas_call x0 -> x16, Pallas kernels: none -> 165 us  [the longest x4 51.6 us: expert_block(): pl.pallas_call(kernel, grid=(experts,), out_shape=(shape((rows, experts *...]
  transfers between devices with their start and end apart: 19 -> 153, of which waited for: 16 -> 44; matrix products, arithmetic and copies ran while one was open for 9% -> 8% of each run, Pallas kernels for 0% -> 21%
where the time goes in v1:
time: 785 us; the launch traced here: 775 us
  waiting for transfers between devices  326 us (42%)
  starting transfers between devices  209 us (27%)
  Pallas kernels  165 us (21%)
  other arithmetic  46.3 us (6%)
  local copies, waits for them, and re-layouts  16.8 us (2%)
  matrix products  8.75 us (1%)
    ppermute x13, waiting for transfers between devices, z_sum(): outer = lax.ppermute(whole, 'z', [(1, 0), (2, 3)])  161 us
    ppermute x12, starting transfers between devices, z_move(): lax.ppermute(v, 'z', [(i, i + d) for i in range(n) if 0 <= i + d < n])  62.9 us
    ppermute x13, waiting for transfers between devices, z_sum(): inner = add_low(v, lax.ppermute(v, 'z', [(0, 1), (3, 2)]))  56.7 us
    ppermute x71, waiting for transfers between devices, swap(): return lax.ppermute(v, axis, [(0, 1), (1, 0)])  54.8 us
    pallas_call x4, Pallas kernels, expert_block(): pl.pallas_call(kernel, grid=(experts,), out_shape=(shape((rows, experts *...  51.6 us
    ppermute x13, starting transfers between devices, z_sum(): inner = add_low(v, lax.ppermute(v, 'z', [(0, 1), (3, 2)]))  40.5 us
    ppermute x71, starting transfers between devices, swap(): return lax.ppermute(v, axis, [(0, 1), (1, 0)])  38.6 us
    pallas_call x2, Pallas kernels, expert_grads(): pl.pallas_call(kernel, grid_spec=grid_spec, out_shape=(shape((count, widt...  22.2 us
  transfers between devices with their start and end apart: 153, of which 44 were waited for; matrix products, arithmetic and copies ran while one was open for 8% of the time, Pallas kernels for 21%

profile of v1, /device:TPU:0, one launch (start us, length us, event | category | flops | bytes accessed | tf_op | source)
XLA Modules:
  0.0 774.8 jit_solution(17647976050530160400)
XLA Ops:
  80.3 8.1 %collective-permute-start.36 = (bf16[128,1024]{1,0:T(8,128)(2,1)S(1)}, bf16[128,1024]{1,0:T(8,128)(2,1)}, u32[]{:S(2)}, u32[]{:S(2)}) collective-permute-start(bf16[128,1024]{1,0:T(8,128)(2,1)S(1)} %get-tuple-element.137), channel_id=1, source_target_pairs={{0,24},{1,25},{2,26},{3,27},{4,28},{5,29},{6,30},{7,31}} | collective-permute-start | bytes 786440 | tf_op jit(solution)/shard_map/ppermute | solution.py:80
  96.3 11.2 %collective-permute-done.38.refs_12_ = bf16[128,1024]{1,0:T(8,128)(2,1)} collective-permute-done((bf16[128,1024]{1,0:T(8,128)(2,1)S(1)}, bf16[128,1024]{1,0:T(8,128)(2,1)}, u32[]{:S(2)}, u32[]{:S(2)}) %collective-permute-start.38) | collective-permute-done | bytes 262176 | tf_op jit(solution)/shard_map/ppermute | solution.py:80
  120.4 17.7 %attend.1 = (bf16[256,1536]{1,0:T(8,128)(2,1)}, f32[8,768]{1,0:T(8,128)}) custom-call(s32[4]{0:T(128)} %pad_add_fusion.ids_ref, bf16[256,1536]{1,0:T(8,128)(2,1)} %project.2.q_ref, s32[2048,1]{1,0:T(8,128)} %copy.31.col_ref, s32[1,2048]{1,0:T(1,128)} %row_ref.3, bf16[256,1024]{1,0:T(8,128)(2,1)} %project.3.refs_0_, bf16[256,1024]{1,0:T(8,128)(2,1)} %copy-done.77, ...), custom_call_target="tpu_custom_call" | custom-call | flops 8053063680 | bytes 2621440 | tf_op jit(solution)/shard_map/attend/pallas_call | solution.py:403
  152.0 13.3 %experts.4 = (bf16[256,1024]{1,0:T(8,128)(2,1)}, bf16[256,1024]{1,0:T(8,128)(2,1)}, bf16[256,1024]{1,0:T(8,128)(2,1)}, f32[256,1536]{1,0:T(8,128)}, f32[256,1536]{1,0:T(8,128)}) custom-call(bf16[128,1536]{1,0:T(8,128)(2,1)} %copy-done.63, bf16[128,1536]{1,0:T(8,128)(2,1)} %copy-done.62, bf16[128,1536]{1,0:T(8,128)(2,1)} %copy-done.60, ...), custom_call_target="tpu_custom_call" | custom-call | flops 4831838208 | bytes 13369344 | tf_op jit(solution)/shard_map/experts/pallas_call | solution.py:669
  170.5 7.3 collective-permute-done.58.na.refs_4_
  178.5 12.7 %experts.6 = (bf16[256,1024]{1,0:T(8,128)(2,1)}, bf16[256,1024]{1,0:T(8,128)(2,1)}, bf16[256,1024]{1,0:T(8,128)(2,1)}, bf16[256,1536]{1,0:T(8,128)(2,1)}, bf16[256,1536]{1,0:T(8,128)(2,1)}) custom-call(bf16[128,1536]{1,0:T(8,128)(2,1)} %copy-done.81, bf16[128,1536]{1,0:T(8,128)(2,1)} %copy-done.80, bf16[128,1536]{1,0:T(8,128)(2,1)} %copy-done.79, ...), custom_call_target="tpu_custom_call" | custom-call | flops 4831838208 | bytes 13369344 | tf_op jit(solution)/shard_map/experts/pallas_call | solution.py:669
  198.1 7.4 collective-permute-done.53.nb.refs_3_
  206.7 12.9 %experts.5 = (bf16[256,1024]{1,0:T(8,128)(2,1)}, bf16[256,1024]{1,0:T(8,128)(2,1)}, bf16[256,1024]{1,0:T(8,128)(2,1)}, bf16[256,1536]{1,0:T(8,128)(2,1)}, bf16[256,1536]{1,0:T(8,128)(2,1)}) custom-call(bf16[128,1536]{1,0:T(8,128)(2,1)} %copy-done.84, bf16[128,1536]{1,0:T(8,128)(2,1)} %copy-done.85, bf16[128,1536]{1,0:T(8,128)(2,1)} %copy-done.82, ...), custom_call_target="tpu_custom_call" | custom-call | flops 4831838208 | bytes 13369344 | tf_op jit(solution)/shard_map/experts/pallas_call | solution.py:669
  226.0 12.7 %experts.7 = (bf16[256,1024]{1,0:T(8,128)(2,1)}, bf16[256,1024]{1,0:T(8,128)(2,1)}, bf16[256,1024]{1,0:T(8,128)(2,1)}, bf16[256,1536]{1,0:T(8,128)(2,1)}, bf16[256,1536]{1,0:T(8,128)(2,1)}) custom-call(bf16[128,1536]{1,0:T(8,128)(2,1)} %copy-done.89, bf16[128,1536]{1,0:T(8,128)(2,1)} %copy-done.88, bf16[128,1536]{1,0:T(8,128)(2,1)} %copy-done.87, ...), custom_call_target="tpu_custom_call" | custom-call | flops 4831838208 | bytes 13369344 | tf_op jit(solution)/shard_map/experts/pallas_call | solution.py:669
  240.3 11.1 %expert_grads.3 = (bf16[2,1536,256]{2,1,0:T(8,128)(2,1)}, bf16[2,1536,256]{2,1,0:T(8,128)(2,1)}, bf16[2,256,1536]{2,1,0:T(8,128)(2,1)}) custom-call(s32[1]{0:T(128)} %bitcast.46.first_ref, bf16[128,1536]{1,0:T(8,128)(2,1)} %copy-done.63, bf16[128,1536]{1,0:T(8,128)(2,1)} %copy-done.62, bf16[128,1536]{1,0:T(8,128)(2,1)} %copy-done.84, ...), custom_call_target="tpu_custom_call" | custom-call | flops 4831838208 | bytes 11010048 | tf_op jit(solution)/shard_map/expert_grads/pallas_call | solution.py:750
  251.5 11.1 %expert_grads.2 = (bf16[2,1536,256]{2,1,0:T(8,128)(2,1)}, bf16[2,1536,256]{2,1,0:T(8,128)(2,1)}, bf16[2,256,1536]{2,1,0:T(8,128)(2,1)}) custom-call(s32[1]{0:T(128)} %bitcast.45.first_ref, bf16[128,1536]{1,0:T(8,128)(2,1)} %copy-done.63, bf16[128,1536]{1,0:T(8,128)(2,1)} %copy-done.62, bf16[128,1536]{1,0:T(8,128)(2,1)} %copy-done.84, ...), custom_call_target="tpu_custom_call" | custom-call | flops 4831838208 | bytes 11010048 | tf_op jit(solution)/shard_map/expert_grads/pallas_call | solution.py:750
  264.0 12.3 %collective-permute-done.72.refs_3_ = bf16[256,1536]{1,0:T(8,128)(2,1)S(1)} collective-permute-done((bf16[256,1536]{1,0:T(8,128)(2,1)}, bf16[256,1536]{1,0:T(8,128)(2,1)S(1)}, u32[]{:S(2)}, u32[]{:S(2)}) %collective-permute-start.72) | collective-permute-done | bytes 786464 | tf_op jit(solution)/shard_map/ppermute | solution.py:75
  277.2 7.5 out_back.1
  284.8 21.8 %attend_back.1 = (bf16[256,1536]{1,0:T(8,128)(2,1)}, bf16[5,128,1024]{2,1,0:T(8,128)(2,1)}, bf16[5,128,1024]{2,1,0:T(8,128)(2,1)}) custom-call(s32[4]{0:T(128)} %pad_add_fusion.ids_ref, bf16[256,1536]{1,0:T(8,128)(2,1)} %project.2.q_ref, s32[2048,1]{1,0:T(8,128)} %copy.31.col_ref, s32[1,2048]{1,0:T(1,128)} %row_ref.3, ...), custom_call_target="tpu_custom_call" | custom-call | flops 20132659200 | bytes 2621440 | tf_op jit(solution)/shard_map/attend_back/pallas_call | solution.py:487
  329.6 8.2 %collective-permute-done.130 = bf16[1536,256]{1,0:T(8,128)(2,1)S(1)} collective-permute-done((bf16[1536,256]{1,0:T(8,128)(2,1)S(1)}, bf16[1536,256]{1,0:T(8,128)(2,1)S(1)}, u32[]{:S(2)}, u32[]{:S(2)}) %collective-permute-start.130) | collective-permute-done | bytes 786464 | tf_op jit(solution)/shard_map/ppermute | solution.py:104
  340.2 14.5 %collective-permute-done.127 = bf16[1536,256]{1,0:T(8,128)(2,1)S(1)} collective-permute-done((bf16[1536,256]{1,0:T(8,128)(2,1)S(1)}, bf16[1536,256]{1,0:T(8,128)(2,1)S(1)}, u32[]{:S(2)}, u32[]{:S(2)}) %collective-permute-start.127) | collective-permute-done | bytes 786464 | tf_op jit(solution)/shard_map/ppermute | solution.py:104
  354.6 20.4 %collective-permute-start.79 = (bf16[128,1024]{1,0:T(8,128)(2,1)S(1)}, bf16[128,1024]{1,0:T(8,128)(2,1)S(1)}, u32[]{:S(2)}, u32[]{:S(2)}) collective-permute-start(bf16[128,1024]{1,0:T(8,128)(2,1)S(1)} %get-tuple-element.123), channel_id=1, source_target_pairs={{0,24},{1,25},{2,26},{3,27},{4,28},{5,29},{6,30},{7,31}} | collective-permute-start | bytes 786440 | tf_op jit(solution)/shard_map/ppermute | solution.py:80
  376.1 16.8 %collective-permute-start.78 = (bf16[128,1024]{1,0:T(8,128)(2,1)S(1)}, bf16[128,1024]{1,0:T(8,128)(2,1)S(1)}, u32[]{:S(2)}, u32[]{:S(2)}) collective-permute-start(bf16[128,1024]{1,0:T(8,128)(2,1)S(1)} %get-tuple-element.124), channel_id=1, source_target_pairs={{0,16},{8,24},{1,17},{9,25},{2,18},{10,26},{3,19},{11,27},{4,20},{... | collective-permute-start | bytes 786440 | tf_op jit(solution)/shard_map/ppermute | solution.py:80
  410.9 9.2 %in_back.1 = (f32[256,1536]{1,0:T(8,128)}, f32[1,1536]{1,0:T(1,128)}) custom-call(s32[4]{0:T(128)} %pad_add_fusion.ids_ref, bf16[256,1536]{1,0:T(8,128)(2,1)} %bitcast.176, f32[256,1536]{1,0:T(8,128)} %get-tuple-element.61.gres_ref, bf16[1,1536]{1,0:T(2,128)(2,1)} %bitcast.192, bf16[256,1536]{1,0:T(8,128)(2,1)} %get-tuple-element.64.dq_ref, ...), custom_call_target="tpu_custom_call" | custom-call | flops 2013265920 | bytes 12582912 | tf_op jit(solution)/shard_map/in_back/pallas_call | solution.py:598
  425.4 13.5 %collective-permute-done.148 = bf16[256,1536]{1,0:T(8,128)(2,1)} collective-permute-done((bf16[256,1536]{1,0:T(8,128)(2,1)}, bf16[256,1536]{1,0:T(8,128)(2,1)}, u32[]{:S(2)}, u32[]{:S(2)}) %collective-permute-start.148) | collective-permute-done | bytes 786464 | tf_op jit(solution)/shard_map/ppermute | solution.py:104
  443.2 12.1 %collective-permute-done.145 = bf16[256,1536]{1,0:T(8,128)(2,1)} collective-permute-done((bf16[256,1536]{1,0:T(8,128)(2,1)}, bf16[256,1536]{1,0:T(8,128)(2,1)}, u32[]{:S(2)}, u32[]{:S(2)}) %collective-permute-start.145) | collective-permute-done | bytes 786464 | tf_op jit(solution)/shard_map/ppermute | solution.py:104
  464.8 25.1 %collective-permute-done.86 = f32[2,384]{1,0:T(2,128)S(1)} collective-permute-done((f32[2,384]{1,0:T(2,128)S(1)}, f32[2,384]{1,0:T(2,128)S(1)}, u32[]{:S(2)}, u32[]{:S(2)}) %collective-permute-start.86) | collective-permute-done | bytes 3104 | tf_op jit(solution)/shard_map/ppermute | solution.py:106
  501.1 10.6 %collective-permute-done.88 = bf16[2,192,768]{2,1,0:T(8,128)(2,1)S(1)} collective-permute-done((bf16[2,192,768]{2,1,0:T(8,128)(2,1)S(1)}, bf16[2,192,768]{2,1,0:T(8,128)(2,1)S(1)}, u32[]{:S(2)}, u32[]{:S(2)}) %collective-permute-start.88) | collective-permute-done | bytes 589856 | tf_op jit(solution)/shard_map/ppermute | solution.py:55
  514.4 9.5 %collective-permute-done.114 = bf16[2,192,768]{2,1,0:T(8,128)(2,1)S(1)} collective-permute-done((bf16[2,192,768]{2,1,0:T(8,128)(2,1)S(1)}, bf16[2,192,768]{2,1,0:T(8,128)(2,1)S(1)}, u32[]{:S(2)}, u32[]{:S(2)}) %collective-permute-start.114) | collective-permute-done | bytes 589856 | tf_op jit(solution)/shard_map/ppermute | solution.py:55
  525.6 35.8 %collective-permute-done.132 = bf16[1536,256]{1,0:T(8,128)(2,1)S(1)} collective-permute-done((bf16[1536,256]{1,0:T(8,128)(2,1)S(1)}, bf16[1536,256]{1,0:T(8,128)(2,1)S(1)}, u32[]{:S(2)}, u32[]{:S(2)}) %collective-permute-start.132) | collective-permute-done | bytes 786464 | tf_op jit(solution)/shard_map/ppermute | solution.py:106
  562.9 17.8 %collective-permute-done.129 = bf16[1536,256]{1,0:T(8,128)(2,1)S(1)} collective-permute-done((bf16[1536,256]{1,0:T(8,128)(2,1)S(1)}, bf16[1536,256]{1,0:T(8,128)(2,1)S(1)}, u32[]{:S(2)}, u32[]{:S(2)}) %collective-permute-start.129) | collective-permute-done | bytes 786464 | tf_op jit(solution)/shard_map/ppermute | solution.py:106
  582.1 15.5 %collective-permute-done.141 = bf16[1536,256]{1,0:T(8,128)(2,1)S(1)} collective-permute-done((bf16[1536,256]{1,0:T(8,128)(2,1)S(1)}, bf16[1536,256]{1,0:T(8,128)(2,1)S(1)}, u32[]{:S(2)}, u32[]{:S(2)}) %collective-permute-start.141) | collective-permute-done | bytes 786464 | tf_op jit(solution)/shard_map/ppermute | solution.py:106
  598.8 15.6 %collective-permute-done.138 = bf16[1536,256]{1,0:T(8,128)(2,1)S(1)} collective-permute-done((bf16[1536,256]{1,0:T(8,128)(2,1)S(1)}, bf16[1536,256]{1,0:T(8,128)(2,1)S(1)}, u32[]{:S(2)}, u32[]{:S(2)}) %collective-permute-start.138) | collective-permute-done | bytes 786464 | tf_op jit(solution)/shard_map/ppermute | solution.py:106
  616.9 14.3 %collective-permute-done.150 = bf16[256,1536]{1,0:T(8,128)(2,1)S(1)} collective-permute-done((bf16[256,1536]{1,0:T(8,128)(2,1)S(1)}, bf16[256,1536]{1,0:T(8,128)(2,1)S(1)}, u32[]{:S(2)}, u32[]{:S(2)}) %collective-permute-start.150) | collective-permute-done | bytes 786464 | tf_op jit(solution)/shard_map/ppermute | solution.py:106
  632.5 13.2 %collective-permute-done.147 = bf16[256,1536]{1,0:T(8,128)(2,1)S(1)} collective-permute-done((bf16[256,1536]{1,0:T(8,128)(2,1)S(1)}, bf16[256,1536]{1,0:T(8,128)(2,1)S(1)}, u32[]{:S(2)}, u32[]{:S(2)}) %collective-permute-start.147) | collective-permute-done | bytes 786464 | tf_op jit(solution)/shard_map/ppermute | solution.py:106
  726.2 7.1 collective-permute-start.108
  742.9 11.3 %collective-permute-done.105 = bf16[192,512]{1,0:T(8,128)(2,1)S(1)} collective-permute-done((bf16[192,512]{1,0:T(8,128)(2,1)S(1)}, bf16[192,512]{1,0:T(8,128)(2,1)S(1)}, u32[]{:S(2)}, u32[]{:S(2)}) %collective-permute-start.105) | collective-permute-done | bytes 196640 | tf_op jit(solution)/shard_map/ppermute | solution.py:106
  (600 shorter events, 334.1 us)
Async XLA Ops:
  219.6 86.9 %collective-permute-start.63 = (bf16[256,1536]{1,0:T(8,128)(2,1)S(1)}, bf16[256,1536]{1,0:T(8,128)(2,1)S(1)}, u32[]{:S(2)}, u32[]{:S(2)}) collective-permute-start(bf16[256,1536]{1,0:T(8,128)(2,1)S(1)} %copy-done.74), channel_id=1, source_target_pairs={{0,2},{2,0},{1,3},{3,1},{4,6},{6,4},{5,7},{7,5},{8,10},{10,8},{9,1... | collective-permute-start | bytes 2359304 | tf_op jit(solution)/shard_map/ppermute | solution.py:60
  220.6 86.0 %collective-permute-start.57 = (bf16[256,1536]{1,0:T(8,128)(2,1)}, bf16[256,1536]{1,0:T(8,128)(2,1)S(1)}, u32[]{:S(2)}, u32[]{:S(2)}) collective-permute-start(bf16[256,1536]{1,0:T(8,128)(2,1)} %get-tuple-element.54), channel_id=1, source_target_pairs={{0,1},{1,0},{2,3},{3,2},{4,5},{5,4},{6,7},{7,6},{8,9},{9,8},{10,11... | collective-permute-start | bytes 2359304 | tf_op jit(solution)/shard_map/ppermute | solution.py:55
  221.6 41.0 %collective-permute-start.70 = (bf16[256,1536]{1,0:T(8,128)(2,1)}, bf16[256,1536]{1,0:T(8,128)(2,1)S(1)}, u32[]{:S(2)}, u32[]{:S(2)}) collective-permute-start(bf16[256,1536]{1,0:T(8,128)(2,1)} %get-tuple-element.58), channel_id=1, source_target_pairs={{0,1},{1,0},{2,3},{3,2},{4,5},{5,4},{6,7},{7,6},{8,9},{9,8},{10,11... | collective-permute-start | bytes 2359304 | tf_op jit(solution)/shard_map/ppermute | solution.py:55
  222.6 41.4 %collective-permute-start.71 = (bf16[256,1536]{1,0:T(8,128)(2,1)S(1)}, bf16[256,1536]{1,0:T(8,128)(2,1)S(1)}, u32[]{:S(2)}, u32[]{:S(2)}) collective-permute-start(bf16[256,1536]{1,0:T(8,128)(2,1)S(1)} %copy-done.75), channel_id=1, source_target_pairs={{0,2},{2,0},{1,3},{3,1},{4,6},{6,4},{5,7},{7,5},{8,10},{10,8},{9,1... | collective-permute-start | bytes 2359304 | tf_op jit(solution)/shard_map/ppermute | solution.py:60
  238.7 37.6 %collective-permute-start.72 = (bf16[256,1536]{1,0:T(8,128)(2,1)}, bf16[256,1536]{1,0:T(8,128)(2,1)S(1)}, u32[]{:S(2)}, u32[]{:S(2)}) collective-permute-start(bf16[256,1536]{1,0:T(8,128)(2,1)} %get-tuple-element.60), channel_id=1, source_target_pairs={{0,3},{1,2},{2,1},{3,0},{4,7},{5,6},{6,5},{7,4},{8,11},{9,10},{10,... | collective-permute-start | bytes 2359304 | tf_op jit(solution)/shard_map/ppermute | solution.py:75
  262.6 44.6 %collective-permute-start.69 = (bf16[256,1536]{1,0:T(8,128)(2,1)S(1)}, bf16[256,1536]{1,0:T(8,128)(2,1)S(1)}, u32[]{:S(2)}, u32[]{:S(2)}) collective-permute-start(bf16[256,1536]{1,0:T(8,128)(2,1)S(1)} %copy-done.76), channel_id=1, source_target_pairs={{0,3},{1,2},{2,1},{3,0},{4,7},{5,6},{6,5},{7,4},{8,11},{9,10},{10,... | collective-permute-start | bytes 2359304 | tf_op jit(solution)/shard_map/ppermute | solution.py:75
  264.0 52.1 %collective-permute-start.126 = (bf16[2,1536,256]{2,1,0:T(8,128)(2,1)}, bf16[2,1536,256]{2,1,0:T(8,128)(2,1)}, u32[]{:S(2)}, u32[]{:S(2)}) collective-permute-start(bf16[2,1536,256]{2,1,0:T(8,128)(2,1)} %get-tuple-element.84), channel_id=1, source_target_pairs={{0,4},{4,0},{1,5},{5,1},{2,6},{6,2},{3,7},{7,3},{8,12},{12,8},{9,1... | collective-permute-start | bytes 4718600 | tf_op jit(solution)/shard_map/ppermute | solution.py:55
  276.3 45.0 %collective-permute-start.135 = (bf16[2,1536,256]{2,1,0:T(8,128)(2,1)}, bf16[2,1536,256]{2,1,0:T(8,128)(2,1)}, u32[]{:S(2)}, u32[]{:S(2)}) collective-permute-start(bf16[2,1536,256]{2,1,0:T(8,128)(2,1)} %get-tuple-element.86), channel_id=1, source_target_pairs={{0,4},{4,0},{1,5},{5,1},{2,6},{6,2},{3,7},{7,3},{8,12},{12,8},{9,1... | collective-permute-start | bytes 4718600 | tf_op jit(solution)/shard_map/ppermute | solution.py:55
  320.0 34.7 %collective-permute-start.127 = (bf16[1536,256]{1,0:T(8,128)(2,1)S(1)}, bf16[1536,256]{1,0:T(8,128)(2,1)S(1)}, u32[]{:S(2)}, u32[]{:S(2)}) collective-permute-start(bf16[1536,256]{1,0:T(8,128)(2,1)S(1)} %get-tuple-element.109), channel_id=1, source_target_pairs={{0,8},{24,16},{1,9},{25,17},{2,10},{26,18},{3,11},{27,19},{4,12},{... | collective-permute-start | bytes 2359304 | tf_op jit(solution)/shard_map/ppermute | solution.py:104
  323.2 52.9 %collective-permute-start.139 = (bf16[1536,256]{1,0:T(8,128)(2,1)S(1)}, bf16[1536,256]{1,0:T(8,128)(2,1)S(1)}, u32[]{:S(2)}, u32[]{:S(2)}) collective-permute-start(bf16[1536,256]{1,0:T(8,128)(2,1)S(1)} %get-tuple-element.108), channel_id=1, source_target_pairs={{0,8},{24,16},{1,9},{25,17},{2,10},{26,18},{3,11},{27,19},{4,12},{... | collective-permute-start | bytes 2359304 | tf_op jit(solution)/shard_map/ppermute | solution.py:104
  327.0 69.1 %collective-permute-start.76 = (bf16[128,1024]{1,0:T(8,128)(2,1)S(1)}, bf16[128,1024]{1,0:T(8,128)(2,1)S(1)}, u32[]{:S(2)}, u32[]{:S(2)}) collective-permute-start(bf16[128,1024]{1,0:T(8,128)(2,1)S(1)} %get-tuple-element.126), channel_id=1, source_target_pairs={{24,0},{25,1},{26,2},{27,3},{28,4},{29,5},{30,6},{31,7}} | collective-permute-start | bytes 786440 | tf_op jit(solution)/shard_map/ppermute | solution.py:80
  328.3 70.2 %collective-permute-start.75 = (bf16[128,1024]{1,0:T(8,128)(2,1)S(1)}, bf16[128,1024]{1,0:T(8,128)(2,1)S(1)}, u32[]{:S(2)}, u32[]{:S(2)}) collective-permute-start(bf16[128,1024]{1,0:T(8,128)(2,1)S(1)} %get-tuple-element.127), channel_id=1, source_target_pairs={{16,0},{24,8},{17,1},{25,9},{18,2},{26,10},{19,3},{27,11},{20,4},{... | collective-permute-start | bytes 786440 | tf_op jit(solution)/shard_map/ppermute | solution.py:80
  337.8 60.7 %collective-permute-start.74 = (bf16[128,1024]{1,0:T(8,128)(2,1)S(1)}, bf16[128,1024]{1,0:T(8,128)(2,1)S(1)}, u32[]{:S(2)}, u32[]{:S(2)}) collective-permute-start(bf16[128,1024]{1,0:T(8,128)(2,1)S(1)} %get-tuple-element.122), channel_id=1, source_target_pairs={{8,0},{16,8},{24,16},{9,1},{17,9},{25,17},{10,2},{18,10},{26,18},{... | collective-permute-start | bytes 786440 | tf_op jit(solution)/shard_map/ppermute | solution.py:80
  354.6 49.6 %collective-permute-start.79 = (bf16[128,1024]{1,0:T(8,128)(2,1)S(1)}, bf16[128,1024]{1,0:T(8,128)(2,1)S(1)}, u32[]{:S(2)}, u32[]{:S(2)}) collective-permute-start(bf16[128,1024]{1,0:T(8,128)(2,1)S(1)} %get-tuple-element.123), channel_id=1, source_target_pairs={{0,24},{1,25},{2,26},{3,27},{4,28},{5,29},{6,30},{7,31}} | collective-permute-start | bytes 786440 | tf_op jit(solution)/shard_map/ppermute | solution.py:80
  398.4 93.8 %collective-permute-start.87 = (bf16[1536,768]{1,0:T(8,128)(2,1)}, bf16[1536,768]{1,0:T(8,128)(2,1)}, u32[]{:S(2)}, u32[]{:S(2)}) collective-permute-start(bf16[1536,768]{1,0:T(8,128)(2,1)} %convolution_convert_fusion.2), channel_id=1, source_target_pairs={{0,4},{4,0},{1,5},{5,1},{2,6},{6,2},{3,7},{7,3},{8,12},{12,8},{9,1... | collective-permute-start | bytes 7077896 | tf_op jit(solution)/shard_map/ppermute | solution.py:55
  404.2 34.7 %collective-permute-start.148 = (bf16[256,1536]{1,0:T(8,128)(2,1)}, bf16[256,1536]{1,0:T(8,128)(2,1)}, u32[]{:S(2)}, u32[]{:S(2)}) collective-permute-start(bf16[256,1536]{1,0:T(8,128)(2,1)} %get-tuple-element.106), channel_id=1, source_target_pairs={{0,8},{24,16},{1,9},{25,17},{2,10},{26,18},{3,11},{27,19},{4,12},{... | collective-permute-start | bytes 2359304 | tf_op jit(solution)/shard_map/ppermute | solution.py:104
  406.4 49.0 %collective-permute-start.145 = (bf16[256,1536]{1,0:T(8,128)(2,1)}, bf16[256,1536]{1,0:T(8,128)(2,1)}, u32[]{:S(2)}, u32[]{:S(2)}) collective-permute-start(bf16[256,1536]{1,0:T(8,128)(2,1)} %get-tuple-element.105), channel_id=1, source_target_pairs={{0,8},{24,16},{1,9},{25,17},{2,10},{26,18},{3,11},{27,19},{4,12},{... | collective-permute-start | bytes 2359304 | tf_op jit(solution)/shard_map/ppermute | solution.py:104
  441.2 54.3 %collective-permute-start.113 = (bf16[1536,768]{1,0:T(8,128)(2,1)S(1)}, bf16[1536,768]{1,0:T(8,128)(2,1)S(1)}, u32[]{:S(2)}, u32[]{:S(2)}) collective-permute-start(bf16[1536,768]{1,0:T(8,128)(2,1)S(1)} %copy-done.4), channel_id=1, source_target_pairs={{0,4},{4,0},{1,5},{5,1},{2,6},{6,2},{3,7},{7,3},{8,12},{12,8},{9,1... | collective-permute-start | bytes 7077896 | tf_op jit(solution)/shard_map/ppermute | solution.py:55
  441.3 49.9 %collective-permute-start.131 = (bf16[1536,256]{1,0:T(8,128)(2,1)}, bf16[1536,256]{1,0:T(8,128)(2,1)S(1)}, u32[]{:S(2)}, u32[]{:S(2)}) collective-permute-start(bf16[1536,256]{1,0:T(8,128)(2,1)} %add_convert_fusion.14), channel_id=1, source_target_pairs={{8,16},{16,8},{9,17},{17,9},{10,18},{18,10},{11,19},{19,11},{12,20... | collective-permute-start | bytes 2359304 | tf_op jit(solution)/shard_map/ppermute | solution.py:105
  442.5 51.7 %collective-permute-start.128 = (bf16[1536,256]{1,0:T(8,128)(2,1)}, bf16[1536,256]{1,0:T(8,128)(2,1)S(1)}, u32[]{:S(2)}, u32[]{:S(2)}) collective-permute-start(bf16[1536,256]{1,0:T(8,128)(2,1)} %add_convert_fusion.17), channel_id=1, source_target_pairs={{8,16},{16,8},{9,17},{17,9},{10,18},{18,10},{11,19},{19,11},{12,20... | collective-permute-start | bytes 2359304 | tf_op jit(solution)/shard_map/ppermute | solution.py:105
  495.2 154.5 %collective-permute-start.100 = (bf16[1536,512]{1,0:T(8,128)(2,1)S(1)}, bf16[1536,512]{1,0:T(8,128)(2,1)S(1)}, u32[]{:S(2)}, u32[]{:S(2)}) collective-permute-start(bf16[1536,512]{1,0:T(8,128)(2,1)S(1)} %convolution_convert_fusion.4), channel_id=1, source_target_pairs={{0,4},{4,0},{1,5},{5,1},{2,6},{6,2},{3,7},{7,3},{8,12},{12,8},{9,1... | collective-permute-start | bytes 4718600 | tf_op jit(solution)/shard_map/ppermute | solution.py:55
  498.1 63.3 %collective-permute-start.132 = (bf16[1536,256]{1,0:T(8,128)(2,1)S(1)}, bf16[1536,256]{1,0:T(8,128)(2,1)S(1)}, u32[]{:S(2)}, u32[]{:S(2)}) collective-permute-start(bf16[1536,256]{1,0:T(8,128)(2,1)S(1)} %add_convert_fusion.13), channel_id=1, source_target_pairs={{8,0},{16,24},{9,1},{17,25},{10,2},{18,26},{11,3},{19,27},{12,4},{... | collective-permute-start | bytes 2359304 | tf_op jit(solution)/shard_map/ppermute | solution.py:106
  499.6 81.0 %collective-permute-start.129 = (bf16[1536,256]{1,0:T(8,128)(2,1)S(1)}, bf16[1536,256]{1,0:T(8,128)(2,1)S(1)}, u32[]{:S(2)}, u32[]{:S(2)}) collective-permute-start(bf16[1536,256]{1,0:T(8,128)(2,1)S(1)} %add_convert_fusion.16), channel_id=1, source_target_pairs={{8,0},{16,24},{9,1},{17,25},{10,2},{18,26},{11,3},{19,27},{12,4},{... | collective-permute-start | bytes 2359304 | tf_op jit(solution)/shard_map/ppermute | solution.py:106
  511.7 85.8 %collective-permute-start.141 = (bf16[1536,256]{1,0:T(8,128)(2,1)S(1)}, bf16[1536,256]{1,0:T(8,128)(2,1)S(1)}, u32[]{:S(2)}, u32[]{:S(2)}) collective-permute-start(bf16[1536,256]{1,0:T(8,128)(2,1)S(1)} %add_convert_fusion.7), channel_id=1, source_target_pairs={{8,0},{16,24},{9,1},{17,25},{10,2},{18,26},{11,3},{19,27},{12,4},{... | collective-permute-start | bytes 2359304 | tf_op jit(solution)/shard_map/ppermute | solution.py:106
  524.0 90.4 %collective-permute-start.138 = (bf16[1536,256]{1,0:T(8,128)(2,1)S(1)}, bf16[1536,256]{1,0:T(8,128)(2,1)S(1)}, u32[]{:S(2)}, u32[]{:S(2)}) collective-permute-start(bf16[1536,256]{1,0:T(8,128)(2,1)S(1)} %add_convert_fusion.10), channel_id=1, source_target_pairs={{8,0},{16,24},{9,1},{17,25},{10,2},{18,26},{11,3},{19,27},{12,4},{... | collective-permute-start | bytes 2359304 | tf_op jit(solution)/shard_map/ppermute | solution.py:106
  561.5 69.8 %collective-permute-start.150 = (bf16[256,1536]{1,0:T(8,128)(2,1)S(1)}, bf16[256,1536]{1,0:T(8,128)(2,1)S(1)}, u32[]{:S(2)}, u32[]{:S(2)}) collective-permute-start(bf16[256,1536]{1,0:T(8,128)(2,1)S(1)} %add_convert_fusion.1), channel_id=1, source_target_pairs={{8,0},{16,24},{9,1},{17,25},{10,2},{18,26},{11,3},{19,27},{12,4},{... | collective-permute-start | bytes 2359304 | tf_op jit(solution)/shard_map/ppermute | solution.py:106
  580.7 65.1 %collective-permute-start.147 = (bf16[256,1536]{1,0:T(8,128)(2,1)S(1)}, bf16[256,1536]{1,0:T(8,128)(2,1)S(1)}, u32[]{:S(2)}, u32[]{:S(2)}) collective-permute-start(bf16[256,1536]{1,0:T(8,128)(2,1)S(1)} %add_convert_fusion.4), channel_id=1, source_target_pairs={{8,0},{16,24},{9,1},{17,25},{10,2},{18,26},{11,3},{19,27},{12,4},{... | collective-permute-start | bytes 2359304 | tf_op jit(solution)/shard_map/ppermute | solution.py:106
  597.5 52.3 %collective-permute-start.89 = (bf16[192,768]{1,0:T(8,128)(2,1)S(1)}, bf16[192,768]{1,0:T(8,128)(2,1)S(1)}, u32[]{:S(2)}, u32[]{:S(2)}) collective-permute-start(bf16[192,768]{1,0:T(8,128)(2,1)S(1)} %get-tuple-element.100), channel_id=1, source_target_pairs={{0,2},{2,0},{1,3},{3,1},{4,6},{6,4},{5,7},{7,5},{8,10},{10,8},{9,1... | collective-permute-start | bytes 884744 | tf_op jit(solution)/shard_map/ppermute | solution.py:60
  614.4 36.0 %collective-permute-start.93 = (bf16[2,192,768]{2,1,0:T(8,128)(2,1)S(1)}, bf16[2,192,768]{2,1,0:T(8,128)(2,1)S(1)}, u32[]{:S(2)}, u32[]{:S(2)}) collective-permute-start(bf16[2,192,768]{2,1,0:T(8,128)(2,1)S(1)} %pad_maximum_fusion.8), channel_id=1, source_target_pairs={{0,2},{2,0},{1,3},{3,1},{4,6},{6,4},{5,7},{7,5},{8,10},{10,8},{9,1... | collective-permute-start | bytes 1769480 | tf_op jit(solution)/shard_map/ppermute | solution.py:60
  649.8 32.1 %collective-permute-start.133 = (bf16[1536,256]{1,0:T(8,128)(2,1)S(1)}, bf16[1536,256]{1,0:T(8,128)(2,1)S(1)}, u32[]{:S(2)}, u32[]{:S(2)}) collective-permute-start(bf16[1536,256]{1,0:T(8,128)(2,1)S(1)} %broadcast_select_fusion.5), channel_id=1, source_target_pairs={{0,4},{4,0},{1,5},{5,1},{2,6},{6,2},{3,7},{7,3},{8,12},{12,8},{9,1... | collective-permute-start | bytes 2359304 | tf_op jit(solution)/shard_map/ppermute | solution.py:55
  682.0 32.6 %collective-permute-start.102 = (bf16[192,512]{1,0:T(8,128)(2,1)S(1)}, bf16[192,512]{1,0:T(8,128)(2,1)S(1)}, u32[]{:S(2)}, u32[]{:S(2)}) collective-permute-start(bf16[192,512]{1,0:T(8,128)(2,1)S(1)} %get-tuple-element.113), channel_id=1, source_target_pairs={{0,2},{2,0},{1,3},{3,1},{4,6},{6,4},{5,7},{7,5},{8,10},{10,8},{9,1... | collective-permute-start | bytes 589832 | tf_op jit(solution)/shard_map/ppermute | solution.py:60
  685.3 32.2 %collective-permute-start.95 = (bf16[192,768]{1,0:T(8,128)(2,1)S(1)}, bf16[192,768]{1,0:T(8,128)(2,1)S(1)}, u32[]{:S(2)}, u32[]{:S(2)}) collective-permute-start(bf16[192,768]{1,0:T(8,128)(2,1)S(1)} %fusion.18), channel_id=1, source_target_pairs={{0,8},{24,16},{1,9},{25,17},{2,10},{26,18},{3,11},{27,19},{4,12},{... | collective-permute-start | bytes 884744 | tf_op jit(solution)/shard_map/ppermute | solution.py:104
  (216 other events, 3299.1 us)

commit v2 on v1

--- a/solution.py
+++ b/solution.py
@@ -1,5 +1,3 @@
-import functools
-
 import jax
 import jax.numpy as jnp
 from jax import lax
@@ -78,17 +76,6 @@
 def z_move(v, d):
     n = lax.axis_size("z")
     return lax.ppermute(v, "z", [(i, i + d) for i in range(n) if 0 <= i + d < n])
-
-
-def plane_gather(a, b):
-    n = lax.axis_size("y")
-    xa, xb = swap(a, "x"), swap(b, "x")
-    got = {(0, 1): (xa, xb)}
-    for d in range(1, n):
-        ya, yb = from_y(a, d), from_y(b, d)
-        got[(d, 0)] = (ya, yb)
-        got[(d, 1)] = (from_y(xa, d), swap(yb, "x"))
-    return got
 
 
 def add_low(*terms):
@@ -136,58 +123,48 @@
     for d in range(1, n):
         total_a = total_a + to_y(part_a[d].astype(BF), d).astype(F32)
     total_b = part_b[0] + swap(part_b[1].astype(BF), "x").astype(F32)
-    return total_a.astype(BF), total_b.astype(BF)
-
-
-def whole_grad(mine, other, y, x, z, core):
-    parts = []
-    for part in plane_reduce(mine, other, y, x):
-        part = z_sum(part, z)
-        beside = swap(part, "core")
-        parts.append((part, beside))
-    a, b = parts
-    own = jnp.concatenate([a[0], b[0]], axis=0).astype(F32)
-    beside = jnp.concatenate([a[1], b[1]], axis=0).astype(F32)
-    return jnp.where(
-        core == 0,
-        jnp.concatenate([own, beside], axis=1),
-        jnp.concatenate([beside, own], axis=1),
-    )
+    return jnp.concatenate([total_a.astype(BF), total_b.astype(BF)], axis=0)
+
+
+def whole_grads(mine, other, count, y, x, z, core):
+    parts = plane_reduce(mine, other, y, x)
+    n = parts.shape[1] // count
+    outs = []
+    for k in range(count):
+        own = z_sum(parts[:, k * n : (k + 1) * n], z)
+        beside = swap(own, "core").astype(F32)
+        own = own.astype(F32)
+        outs.append(
+            jnp.where(
+                core == 0,
+                jnp.concatenate([own, beside], axis=1),
+                jnp.concatenate([beside, own], axis=1),
+            )
+        )
+    return outs
 
 
 class Gathered:
-    def __init__(self, own, halves, core_axis_halves):
-        self.pieces = own + halves + core_axis_halves
-        self.arrays = [piece[0] for piece in self.pieces]
-        self.places = [piece[1:] for piece in self.pieces]
-
-
-def gather_weight(own_full, own_a, own_b, half_width):
-    rows = own_a.shape[0]
-    own = [(array, (0, 0), 0, first) for array, first in own_full]
-    mine, beside = [], []
-    for where, (a, b) in plane_gather(own_a, own_b).items():
-        for array, row in ((a, 0), (b, rows)):
-            mine.append((array, where, row, "mine"))
-            beside.append((swap(array, "core"), where, row, "other"))
-    return Gathered(own, mine, beside)
+    def __init__(self, arrays, places):
+        self.arrays = arrays
+        self.places = places
 
 
 def start_load(refs, places, dst, sems, ids, ny, shard, half_width):
     core, y, x = ids[1], ids[2], ids[3]
     copies = []
-    for k, (ref, ((dy, dx), row, column)) in enumerate(zip(refs, places)):
-        owner = lax.rem(y + dy, ny) * 2 + (x if dx == 0 else 1 - x)
+    for k, (which, (row0, rows, col0, cols), owner, row, column) in enumerate(places):
+        if owner is not None:
+            dy, dx = owner
+            row = (lax.rem(y + dy, ny) * 2 + (x if dx == 0 else 1 - x)) * shard + row
+            row = pl.multiple_of(row, 16)
         if column == "mine":
-            column = core * half_width
+            column = pl.multiple_of(core * half_width, 128)
         elif column == "other":
-            column = (1 - core) * half_width
-        if not isinstance(column, int):
-            column = pl.multiple_of(column, 128)
-        first = pl.multiple_of(owner * shard + row, 16)
+            column = pl.multiple_of((1 - core) * half_width, 128)
         copy = pltpu.make_async_copy(
-            ref,
-            dst.at[pl.ds(first, ref.shape[0]), pl.ds(column, ref.shape[1])],
+            refs[which].at[pl.ds(row0, rows), pl.ds(col0, cols)],
+            dst.at[pl.ds(row, rows), pl.ds(column, cols)],
             sems.at[k],
         )
         copy.start()
@@ -195,8 +172,56 @@
     return copies
 
 
+def gather_first(w_key, w_value, core):
+    ny = lax.axis_size("y")
+    rows, cols = w_key.shape
+    h = rows // 2
+    own = jnp.where(core == 0, w_key, w_value)
+    from_x = swap(own, "x")
+    pieces, where = [from_x], [((0, 1), 0)]
+    sides = [from_y(own, d) for d in range(1, ny)]
+    for d, side in enumerate(sides, 1):
+        pieces.append(side)
+        where.append(((d, 0), 0))
+    for d, side in enumerate(sides, 1):
+        pieces += [from_y(from_x[:h], d), swap(side[h:], "x")]
+        where += [((d, 1), 0), ((d, 1), h)]
+    mine = jnp.concatenate(pieces, axis=0)
+    other = swap(mine, "core")
+    places = [
+        (0, (0, rows, 0, cols), (0, 0), 0, 0),
+        (1, (0, rows, 0, cols), (0, 0), 0, cols),
+    ]
+    at = 0
+    for piece, (owner, row) in zip(pieces, where):
+        count = piece.shape[0]
+        places.append((2, (at, count, 0, cols), owner, row, "mine"))
+        places.append((3, (at, count, 0, cols), owner, row, "other"))
+        at += count
+    return Gathered([w_key, w_value, mine, other], places)
+
+
+def gather_rest(w_query, w_out, core):
+    ny = lax.axis_size("y")
+    rows, cols = w_query.shape
+    n = cols // 2
+    half = jnp.concatenate(
+        [lax.dynamic_slice(w, (0, core * n), (rows, n)) for w in (w_query, w_out)], axis=1
+    )
+    gathered = lax.all_gather(half, ("core", "y", "x"), axis=0, tiled=True)
+    weights = []
+    for k in range(2):
+        places = [
+            (0, ((c * 2 * ny + w) * rows, rows, k * n, n), None, w * rows, c * n)
+            for c in range(2)
+            for w in range(2 * ny)
+        ]
+        weights.append(Gathered([gathered], places))
+    return weights
+
+
 def gathered_matmul(lhs, weight, ids, ny, shard, width):
-    count = len(weight.arrays)
+    count, moves = len(weight.arrays), len(weight.places)
     depth = 2 * ny * shard
 
     def kernel(ids_ref, lhs_ref, *refs):
@@ -210,7 +235,7 @@
         out_shape=shape((lhs.shape[0], width), BF),
         in_specs=[SMEM, VMEM] + [ANY] * count,
         out_specs=VMEM,
-        scratch_shapes=[pltpu.VMEM((depth, width), BF), pltpu.SemaphoreType.DMA((count,))],
+        scratch_shapes=[pltpu.VMEM((depth, width), BF), pltpu.SemaphoreType.DMA((moves,))],
         compiler_params=params(),
         cost_estimate=cost(2 * lhs.shape[0] * depth * width, 2 * depth * width + 2 * lhs.size),
         name="project",
@@ -219,46 +244,26 @@
 
 def load_keys(nz, half, ids, refs, kv, sems):
     z = ids[0]
-    own, beside = refs[0], refs[1]
     slot = 2 * half
 
     def place(index, second):
         return kv.at[pl.ds(pl.multiple_of(index * slot + second * half, half), half)]
 
-    always = []
-    for k, ref in enumerate((own, beside)):
-        always.append(pltpu.make_async_copy(ref.at[pl.ds(0, half)], place(0, k), sems.at[2 * k]))
-        always.append(
-            pltpu.make_async_copy(ref.at[pl.ds(half, half)], place(z + 1, k), sems.at[2 * k + 1])
+    copies = []
+    for second in range(2):
+        own, came = refs[second], refs[2 + second]
+        copies.append(pltpu.make_async_copy(own.at[pl.ds(0, half)], place(0, second), sems.at[second, 0]))
+        copies.append(
+            pltpu.make_async_copy(own.at[pl.ds(half, half)], place(z + 1, second), sems.at[second, nz])
         )
-    for copy in always:
+        for d in range(1, nz):
+            index = jnp.where(d <= z, d, z + 1 + nz - d)
+            copies.append(
+                pltpu.make_async_copy(came.at[d - 1], place(index, second), sems.at[second, d])
+            )
+    for copy in copies:
         copy.start()
-    guarded = []
-    for d in range(1, nz):
-        group = refs[2 + 4 * (d - 1) : 2 + 4 * d]
-        base = 4 + 4 * (d - 1)
-        low = [pltpu.make_async_copy(group[k], place(d, k), sems.at[base + k]) for k in range(2)]
-        high = [
-            pltpu.make_async_copy(group[2 + k], place(z + 1 + d, k), sems.at[base + 2 + k])
-            for k in range(2)
-        ]
-        guarded.append((d <= z, low))
-        guarded.append((z + d < nz, high))
-    for needed, copies in guarded:
-
-        @pl.when(needed)
-        def _():
-            for copy in copies:
-                copy.start()
-
-    for copy in always:
-        copy.wait()
-    for needed, copies in guarded:
-
-        @pl.when(needed)
-        def _():
-            for copy in copies:
-                copy.wait()
+    return copies
 
 
 def slot_range(nz, ids, tile):
@@ -344,8 +349,10 @@
     def kernel(ids_ref, q_ref, col_ref, row_ref, *refs):
         key_refs = refs[:count]
         out_ref, lse_ref, kv, scores, masks, sems = refs[count:]
+        copies = load_keys(nz, half, ids_ref, key_refs, kv, sems)
         fill_masks(nz, half, ids_ref, col_ref, row_ref, masks)
-        load_keys(nz, half, ids_ref, key_refs, kv, sems)
+        for copy in copies:
+            copy.wait()
         for tile in range(2):
             first, end = slot_range(nz, ids_ref, tile)
             for pair in range(PAIRS):
@@ -409,7 +416,7 @@
             pltpu.VMEM((slots * slot, 1024), BF),
             pltpu.VMEM((slots, slot, lanes), F32),
             pltpu.VMEM((2, slots, slot, half), F32),
-            pltpu.SemaphoreType.DMA((4 * nz,)),
+            pltpu.SemaphoreType.DMA((2, nz + 1)),
         ],
         compiler_params=params(),
         cost_estimate=cost(8 * 256 * pairs, 2 * slots * slot * 1024, pairs),
@@ -428,9 +435,11 @@
     def kernel(ids_ref, q_ref, col_ref, row_ref, att_ref, grad_ref, lse_ref, *refs):
         key_refs = refs[:count]
         dq_ref, mine_ref, other_ref, kv, dkv, masks, sems = refs[count:]
+        copies = load_keys(nz, half, ids_ref, key_refs, kv, sems)
         fill_masks(nz, half, ids_ref, col_ref, row_ref, masks)
         dkv[...] = jnp.zeros_like(dkv)
-        load_keys(nz, half, ids_ref, key_refs, kv, sems)
+        for copy in copies:
+            copy.wait()
         for tile in range(2):
             first, end = slot_range(nz, ids_ref, tile)
             for pair in range(PAIRS):
@@ -497,17 +506,17 @@
             pltpu.VMEM((slots * slot, 1024), BF),
             pltpu.VMEM((slots * slot, 1024), F32),
             pltpu.VMEM((2, slots, slot, half), F32),
-            pltpu.SemaphoreType.DMA((4 * nz,)),
+            pltpu.SemaphoreType.DMA((2, nz + 1)),
         ],
         compiler_params=params(),
-        cost_estimate=cost(20 * 256 * pairs, 2 * slots * slot * 1024, pairs),
+        cost_estimate=cost(300 * 256 * pairs, 2 * slots * slot * 1024, pairs),
         name="attend_back",
     )(ids, q, seg_col, seg_row, attended, grad_att, lse, *keys)
 
 
 def out_project(tokens, attended, gain, weight, ids, ny, shard):
     rows, width = tokens.shape
-    count = len(weight.arrays)
+    count, moves = len(weight.arrays), len(weight.places)
 
     def kernel(ids_ref, tokens_ref, att_ref, gain_ref, *refs):
         pieces = refs[:count]
@@ -516,28 +525,28 @@
             copy.wait()
         resid = tokens_ref[...].astype(F32) + nn(att_ref[...], held[...])
         resid_ref[...] = resid
-        norm_ref[...] = (resid * inv_root(resid) * gain_ref[...].astype(F32)).astype(BF)
+        norm_ref[...] = (resid * inv_root(resid) * gain_ref[...]).astype(BF)
 
     return pl.pallas_call(
         kernel,
         out_shape=(shape((rows, width), F32), shape((rows, width), BF)),
         in_specs=[SMEM] + [VMEM] * 3 + [ANY] * count,
         out_specs=(VMEM, VMEM),
-        scratch_shapes=[pltpu.VMEM((width, width), BF), pltpu.SemaphoreType.DMA((count,))],
+        scratch_shapes=[pltpu.VMEM((width, width), BF), pltpu.SemaphoreType.DMA((moves,))],
         compiler_params=params(),
         cost_estimate=cost(2 * rows * width * width, 2 * width * width + 10 * rows * width),
         name="out_project",
     )(ids, tokens, attended, gain, *weight.arrays)
 
 
-def out_back(resid, cotangent, gain, terms, weight, ids, ny, shard):
+def out_back(resid, cotangent, gain, terms, weight, ids, ny, shard, after=()):
     rows, width = resid.shape
-    count = len(weight.arrays)
+    count, moves = len(weight.arrays), len(weight.places)
     term_count = len(terms)
 
     def kernel(ids_ref, resid_ref, cot_ref, gain_ref, *refs):
         term_refs, pieces = refs[:term_count], refs[term_count : term_count + count]
-        gres_ref, branch_ref, gatt_ref, ggain_ref, held, sems = refs[term_count + count :]
+        gres_ref, branch_ref, gatt_ref, ggain_ref, held, sems = refs[term_count + count + len(after) :]
         copies = start_load(pieces, weight.places, held, sems, ids_ref, ny, shard, width // 2)
         grad_norm = term_refs[0][...].astype(F32)
         for ref in term_refs[1:]:
@@ -546,7 +555,7 @@
         root = inv_root(resid)
         s = resid * root
         ggain_ref[...] = jnp.sum(grad_norm * s, axis=0, keepdims=True)
-        t = grad_norm * gain_ref[...].astype(F32)
+        t = grad_norm * gain_ref[...]
         gres = cot_ref[...].astype(F32) + root * (
             t - s * jnp.mean(t * s, axis=-1, keepdims=True)
         )
@@ -565,23 +574,23 @@
             shape((rows, width), BF),
             shape((1, width), F32),
         ),
-        in_specs=[SMEM] + [VMEM] * (3 + term_count) + [ANY] * count,
+        in_specs=[SMEM] + [VMEM] * (3 + term_count) + [ANY] * (count + len(after)),
         out_specs=(VMEM,) * 4,
-        scratch_shapes=[pltpu.VMEM((width, width), BF), pltpu.SemaphoreType.DMA((count,))],
+        scratch_shapes=[pltpu.VMEM((width, width), BF), pltpu.SemaphoreType.DMA((moves,))],
         compiler_params=params(),
         cost_estimate=cost(2 * rows * width * width, 2 * width * width + 20 * rows * width),
         name="out_back",
-    )(ids, resid, cotangent, gain, *terms, *weight.arrays)
-
-
-def in_back(tokens, gres, gain, dq, dkv, weight_q, weight_kv, ids, ny, shard):
+    )(ids, resid, cotangent, gain, *terms, *weight.arrays, *after)
+
+
+def in_back(tokens, gres, gain, dq, dkv, weight_q, weight_kv, ids, ny, shard, after=()):
     rows, width = tokens.shape
     kv_width = dkv.shape[1]
     count_q, count_kv = len(weight_q.arrays), len(weight_kv.arrays)
 
     def kernel(ids_ref, tokens_ref, gres_ref, gain_ref, dq_ref, dkv_ref, *refs):
         q_pieces, kv_pieces = refs[:count_q], refs[count_q : count_q + count_kv]
-        out_ref, ggain_ref, held_q, held_kv, sems_q, sems_kv = refs[count_q + count_kv :]
+        out_ref, ggain_ref, held_q, held_kv, sems_q, sems_kv = refs[count_q + count_kv + len(after) :]
         copies = start_load(
             kv_pieces, weight_kv.places, held_kv, sems_kv, ids_ref, ny, shard, kv_width // 2
         ) + start_load(q_pieces, weight_q.places, held_q, sems_q, ids_ref, ny, shard, width // 2)
@@ -592,46 +601,45 @@
         root = inv_root(x)
         s = x * root
         ggain_ref[...] = jnp.sum(grad_norm * s, axis=0, keepdims=True)
-        t = grad_norm * gain_ref[...].astype(F32)
+        t = grad_norm * gain_ref[...]
         out_ref[...] = gres_ref[...] + root * (t - s * jnp.mean(t * s, axis=-1, keepdims=True))
 
     return pl.pallas_call(
         kernel,
         out_shape=(shape((rows, width), F32), shape((1, width), F32)),
-        in_specs=[SMEM] + [VMEM] * 5 + [ANY] * (count_q + count_kv),
+        in_specs=[SMEM] + [VMEM] * 5 + [ANY] * (count_q + count_kv + len(after)),
         out_specs=(VMEM, VMEM),
         scratch_shapes=[
             pltpu.VMEM((width, width), BF),
             pltpu.VMEM((width, kv_width), BF),
-            pltpu.SemaphoreType.DMA((count_q,)),
-            pltpu.SemaphoreType.DMA((count_kv,)),
+            pltpu.SemaphoreType.DMA((len(weight_q.places),)),
+            pltpu.SemaphoreType.DMA((len(weight_kv.places),)),
         ],
         compiler_params=params(),
         cost_estimate=cost(
             2 * rows * width * (width + kv_width), 2 * width * (width + kv_width) + 12 * rows * width
         ),
         name="in_back",
-    )(ids, tokens, gres, gain, dq, dkv, *weight_q.arrays, *weight_kv.arrays)
-
-
-def expert_block(normed, cots, coeff, w_gate, w_up, w_down, out_dtype):
+    )(ids, tokens, gres, gain, dq, dkv, *weight_q.arrays, *weight_kv.arrays, *after)
+
+
+def expert_block(block_ids, blocks, cot_all, coeffs, w_gate, w_up, w_down, out_dtype, after=()):
     experts, width, units = w_gate.shape
-    half = normed[0].shape[0]
-    rows = 2 * half
-
-    def kernel(na, nb, ca, cb, coeff_ref, wg_ref, wu_ref, wd_ref, hid_ref, gg_ref, gu_ref,
-               mix_ref, gnf_ref, n_all, c_all, mix, gnf):
+    pieces = [p for block in blocks for p in block]
+    count, many, extra = len(pieces), len(blocks), len(after)
+    size = coeffs[0].shape[0]
+    rows = many * size
+
+    def kernel(id_ref, *refs):
+        n_refs, refs = refs[:count], refs[count:]
+        c_refs, refs = refs[:many], refs[many:]
+        (coeff_ref, wg_ref, wu_ref, wd_ref), refs = refs[:4], refs[4 + extra :]
+        (hid_ref, gg_ref, gu_ref), refs = refs[:3], refs[3:]
+        mix_refs, gnf_refs, (mix, gnf) = refs[:many], refs[many : 2 * many], refs[2 * many :]
         e = pl.program_id(0)
-
-        @pl.when(e == 0)
-        def _():
-            n_all[:half] = na[...]
-            n_all[half:] = nb[...]
-            c_all[:half] = ca[...]
-            c_all[half:] = cb[...]
-
         wg, wu, wd = wg_ref[0], wu_ref[0], wd_ref[0]
-        rows_in, cot = n_all[...], c_all[...]
+        rows_in = jnp.concatenate([ref[...] for ref in n_refs], axis=0)
+        cot = jnp.concatenate([ref[...] for ref in c_refs], axis=0)
         lane = lax.broadcasted_iota(jnp.int32, coeff_ref.shape, 1)
         weight = jnp.sum(jnp.where(lane == e, coeff_ref[...], 0.0), axis=1, keepdims=True)
         gate = nn(rows_in, wg)
@@ -660,58 +668,83 @@
 
         @pl.when(e == experts - 1)
         def _():
-            gnf_ref[...] = gnf[...].astype(gnf_ref.dtype)
-            mix_ref[...] = mix[...].astype(mix_ref.dtype)
-
-    whole = pl.BlockSpec((half, width), lambda e: (0, 0))
-    keep = pl.BlockSpec((rows, width), lambda e: (0, 0))
-    unit = pl.BlockSpec((rows, units), lambda e: (0, e))
-    return pl.pallas_call(
+            for k in range(many):
+                here = slice(k * size, (k + 1) * size)
+                gnf_refs[k][...] = gnf[here].astype(out_dtype)
+                mix_refs[k][...] = mix[here].astype(out_dtype)
+
+    keep = pl.BlockSpec((size, width), lambda e, s: (0, 0))
+    unit = pl.BlockSpec((rows, units), lambda e, s: (0, e))
+    outs = pl.pallas_call(
         kernel,
-        grid=(experts,),
+        grid_spec=pltpu.PrefetchScalarGridSpec(
+            num_scalar_prefetch=1,
+            grid=(experts,),
+            in_specs=[pl.BlockSpec(p.shape, lambda e, s: (0, 0)) for p in pieces]
+            + [pl.BlockSpec((size, width), lambda e, s, k=k: (s[k], 0)) for k in range(many)]
+            + [
+                pl.BlockSpec((rows, experts), lambda e, s: (0, 0)),
+                pl.BlockSpec((1, width, units), lambda e, s: (e, 0, 0)),
+                pl.BlockSpec((1, width, units), lambda e, s: (e, 0, 0)),
+                pl.BlockSpec((1, units, width), lambda e, s: (e, 0, 0)),
+            ]
+            + [ANY] * extra,
+            out_specs=(unit,) * 3 + (keep,) * (2 * many),
+            scratch_shapes=[pltpu.VMEM((rows, width), F32)] * 2,
+        ),
         out_shape=(shape((rows, experts * units), BF),) * 3
-        + (shape((rows, width), out_dtype),) * 2,
-        in_specs=[whole] * 4
-        + [
-            pl.BlockSpec(coeff.shape, lambda e: (0, 0)),
-            pl.BlockSpec((1, width, units), lambda e: (e, 0, 0)),
-            pl.BlockSpec((1, width, units), lambda e: (e, 0, 0)),
-            pl.BlockSpec((1, units, width), lambda e: (e, 0, 0)),
-        ],
-        out_specs=(unit, unit, unit, keep, keep),
-        scratch_shapes=[pltpu.VMEM((rows, width), BF)] * 2 + [pltpu.VMEM((rows, width), F32)] * 2,
+        + (shape((size, width), out_dtype),) * (2 * many),
         compiler_params=params(),
         cost_estimate=cost(
             12 * rows * width * experts * units, 6 * experts * width * units + 10 * rows * width
         ),
         name="experts",
-    )(*normed, *cots, coeff, w_gate, w_up, w_down)
-
-
-def expert_grads(first, normed, cots, hidden, grad_gate, grad_up, experts):
-    blocks = len(hidden)
-    half, width = normed[0].shape
-    rows = hidden[0].shape[0]
+    )(
+        block_ids,
+        *pieces,
+        *[cot_all] * many,
+        jnp.concatenate(coeffs, axis=0),
+        w_gate,
+        w_up,
+        w_down,
+        *after,
+    )
+    return outs[:3], outs[3 : 3 + many], outs[3 + many :]
+
+
+def expert_grads(block_ids, pieces, cot_all, hidden, grad_gate, grad_up, experts, size):
+    groups = len(hidden)
+    width = cot_all.shape[1]
     units = hidden[0].shape[1] // experts
-    pieces = 2 * blocks
-
-    def kernel(first_ref, *refs):
-        n_refs, c_refs = refs[:pieces], refs[pieces : 2 * pieces]
-        at = 2 * pieces
+    count = len(pieces)
+    blocks = block_ids.shape[0]
+    rows = blocks * size
+
+    def kernel(id_ref, *refs):
+        n_refs, c_ref = refs[:count], refs[count]
+        at = count + 1
         h_refs, gg_refs, gu_refs = (
-            refs[at : at + blocks],
-            refs[at + blocks : at + 2 * blocks],
-            refs[at + 2 * blocks : at + 3 * blocks],
+            refs[at : at + groups],
+            refs[at + groups : at + 2 * groups],
+            refs[at + 2 * groups : at + 3 * groups],
         )
-        og_ref, ou_ref, od_ref, n_all, c_all, sems = refs[at + 3 * blocks :]
+        out_ref, n_all, c_all, n_sems, c_sems = refs[at + 3 * groups :]
 
         @pl.when(pl.program_id(0) == 0)
         def _():
-            copies = []
-            for k in range(pieces):
-                to = pl.ds(k * half, half)
-                copies.append(pltpu.make_async_copy(n_refs[k], n_all.at[to], sems.at[0, k]))
-                copies.append(pltpu.make_async_copy(c_refs[k], c_all.at[to], sems.at[1, k]))
+            copies, row = [], 0
+            for k, ref in enumerate(n_refs):
+                copies.append(
+                    pltpu.make_async_copy(ref, n_all.at[pl.ds(row, ref.shape[0])], n_sems.at[k])
+                )
+                row += ref.shape[0]
+            for k in range(blocks):
+                start = pl.multiple_of(id_ref[k] * size, size)
+                copies.append(
+                    pltpu.make_async_copy(
+                        c_ref.at[pl.ds(start, size)], c_all.at[pl.ds(k * size, size)], c_sems.at[k]
+                    )
+                )
             for copy in copies:
                 copy.start()
             for copy in copies:
@@ -724,75 +757,86 @@
             ],
             axis=1,
         )
-        both = tn(n_all[...], grads)
-        og_ref[0] = both[:, :units].astype(BF)
-        ou_ref[0] = both[:, units:].astype(BF)
+        out_ref[:, : 2 * units] = tn(n_all[...], grads).astype(BF)
         hid = jnp.concatenate([ref[...] for ref in h_refs], axis=0)
-        od_ref[0] = tn(hid, c_all[...]).astype(BF)
-
-    unit = pl.BlockSpec((rows, units), lambda e, first: (0, first[0] + e))
+        out_ref[:, 2 * units :] = tn(c_all[...], hid).astype(BF)
+
     grid_spec = pltpu.PrefetchScalarGridSpec(
         num_scalar_prefetch=1,
-        grid=(experts // 2,),
-        in_specs=[ANY] * (2 * pieces) + [unit] * (3 * blocks),
-        out_specs=(
-            pl.BlockSpec((1, width, units), lambda e, first: (e, 0, 0)),
-            pl.BlockSpec((1, width, units), lambda e, first: (e, 0, 0)),
-            pl.BlockSpec((1, units, width), lambda e, first: (e, 0, 0)),
-        ),
+        grid=(experts,),
+        in_specs=[ANY] * (count + 1)
+        + [
+            pl.BlockSpec((one.shape[0], units), lambda e, s: (0, e))
+            for group in (hidden, grad_gate, grad_up)
+            for one in group
+        ],
+        out_specs=pl.BlockSpec((width, 3 * units), lambda e, s: (e, 0)),
         scratch_shapes=[
-            pltpu.VMEM((blocks * rows, width), BF),
-            pltpu.VMEM((blocks * rows, width), BF),
-            pltpu.SemaphoreType.DMA((2, pieces)),
+            pltpu.VMEM((rows, width), BF),
+            pltpu.VMEM((rows, width), BF),
+            pltpu.SemaphoreType.DMA((count,)),
+            pltpu.SemaphoreType.DMA((blocks,)),
         ],
     )
-    count = experts // 2
     return pl.pallas_call(
         kernel,
         grid_spec=grid_spec,
-        out_shape=(
-            shape((count, width, units), BF),
-            shape((count, width, units), BF),
-            shape((count, units, width), BF),
-        ),
+        out_shape=shape((experts * width, 3 * units), BF),
         compiler_params=params(),
         cost_estimate=cost(
-            6 * blocks * rows * width * units * count,
-            4 * blocks * rows * width + 6 * count * units * width,
+            6 * rows * width * units * experts, 4 * rows * width + 6 * experts * units * width
         ),
         name="expert_grads",
-    )(first, *normed, *cots, *hidden, *grad_gate, *grad_up)
-
-
-def spread_halves(mine, beside, core):
-    count, a, b = mine.shape
-
-    def kernel(core_ref, mine_ref, beside_ref, out_ref):
-        is_mine = pl.program_id(0) // count == core_ref[0]
-
-        @pl.when(is_mine)
-        def _():
-            out_ref[...] = mine_ref[...].astype(F32)
-
-        @pl.when(jnp.logical_not(is_mine))
-        def _():
-            out_ref[...] = beside_ref[...].astype(F32)
-
-    block = (1, a, b)
-    source = pl.BlockSpec(block, lambda e, core: (lax.rem(e, count), 0, 0))
+    )(block_ids, *pieces, cot_all, *hidden, *grad_gate, *grad_up)
+
+
+def spread_grads(grads, experts):
+    width, units = grads.shape[0] // experts, grads.shape[1] // 3
+
+    def kernel(in_ref, gate_ref, up_ref, down_ref):
+        gate_ref[0] = in_ref[:, :units].astype(F32)
+        up_ref[0] = in_ref[:, units : 2 * units].astype(F32)
+        down_ref[0] = in_ref[:, 2 * units :].astype(F32).T
+
+    side = pl.BlockSpec((1, width, units), lambda e: (e, 0, 0))
     return pl.pallas_call(
         kernel,
-        grid_spec=pltpu.PrefetchScalarGridSpec(
-            num_scalar_prefetch=1,
-            grid=(2 * count,),
-            in_specs=[source, source],
-            out_specs=pl.BlockSpec(block, lambda e, core: (e, 0, 0)),
-        ),
-        out_shape=shape((2 * count, a, b), F32),
+        grid=(experts,),
+        out_shape=(shape((experts, width, units), F32),) * 2
+        + (shape((experts, units, width), F32),),
+        in_specs=[pl.BlockSpec((width, 3 * units), lambda e: (e, 0))],
+        out_specs=(side, side, pl.BlockSpec((1, units, width), lambda e: (e, 0, 0))),
         compiler_params=params(),
-        cost_estimate=cost(0, 16 * count * a * b),
-        name="spread",
-    )(core, mine, beside)
+        cost_estimate=cost(0, 6 * grads.size),
+        name="spread_grads",
+    )(grads)
+
+
+def weight_grads(ids, pairs, after=()):
+    depth = pairs[0][0].shape[1]
+    halves = [right.shape[1] // 2 for _, right in pairs]
+    width = sum(halves)
+    rows = pairs[0][0].shape[0]
+
+    def kernel(ids_ref, *refs):
+        mine_ref, other_ref = refs[2 * len(pairs) + len(after) :]
+        core, at = ids_ref[1], 0
+        for k, n in enumerate(halves):
+            left, right = refs[2 * k][...], refs[2 * k + 1]
+            for out_ref, side in ((mine_ref, core), (other_ref, 1 - core)):
+                columns = right[:, pl.ds(pl.multiple_of(side * n, 128), n)]
+                out_ref[:, at : at + n] = tn(left, columns).astype(BF)
+            at += n
+
+    return pl.pallas_call(
+        kernel,
+        out_shape=(shape((depth, width), BF),) * 2,
+        in_specs=[SMEM] + [VMEM] * (2 * len(pairs)) + [ANY] * len(after),
+        out_specs=(VMEM,) * 2,
+        compiler_params=params(),
+        cost_estimate=cost(4 * rows * depth * width, 4 * depth * width),
+        name="weight_grads",
+    )(ids, *[v for pair in pairs for v in pair], *after)
 
 
 def body(
@@ -818,128 +862,127 @@
     z, core, y, x = (lax.axis_index(a) for a in ("z", "core", "y", "x"))
     ids = jnp.stack([z, core, y, x]).astype(jnp.int32)
     shard = w_query.shape[0]
-    sh = shard // 2
     experts = w_gate.shape[0]
     kv_width = w_key.shape[1] + w_value.shape[1]
-    hw = width // 2
     plane = [(dy, dx) for dy in range(ny) for dx in range(2)]
     seg_row = segments
     seg_col = segments.reshape(-1, 1)
 
-    gains = jnp.stack([gain_attn, gain_ffn])
+    chosen = routes[0][:, :, None] == jnp.arange(experts, dtype=jnp.int32)[None, None, :]
+    coeff = jnp.sum(jnp.where(chosen, route_weights[0][:, :, None], 0.0), axis=1)
+    small = jnp.concatenate(
+        [coeff.reshape(-1), gain_attn.astype(F32), gain_ffn.astype(F32)]
+    ).reshape(-1, 128)
+    coeffs = {}
+    slot = jnp.arange(2 * ny, dtype=jnp.int32)[None, :, None]
+    gains = jnp.zeros((2, 2 * ny, shard), F32)
     owners = {}
     for dy, dx in plane:
-        got = gains if (dy, dx) == (0, 0) else to_plane(gains, dy, dx)
-        owner = lax.rem(y - dy + ny, ny) * 2 + (x if dx == 0 else 1 - x)
-        owners[(dy, dx)] = (owner, got)
-    slot = jnp.arange(2 * ny, dtype=jnp.int32)[None, :, None]
-    all_gains = sum(
-        jnp.where(slot == owner, got[:, None, :], jnp.zeros((), BF))
-        for owner, got in owners.values()
-    ).reshape(2, 1, width)
-    gain_a, gain_f = all_gains[0], all_gains[1]
-
-    kv_half = jnp.where(core == 0, w_key, w_value)
-    weight_kv = gather_weight(
-        [(w_key, 0), (w_value, kv_width // 2)], kv_half[:sh], kv_half[sh:], kv_width // 2
-    )
-
-    def column_half(w, row, count):
-        return lax.dynamic_slice(w, (row, core * (w.shape[1] // 2)), (count, w.shape[1] // 2))
-
-    weight_q = gather_weight(
-        [(w_query, 0)], column_half(w_query, 0, sh), column_half(w_query, sh, sh), hw
-    )
-    weight_o = gather_weight(
-        [(w_out, 0)], column_half(w_out, 0, sh), column_half(w_out, sh, sh), hw
-    )
+        got = small if (dy, dx) == (0, 0) else to_plane(small, -dy % ny, dx)
+        got = got.reshape(-1)
+        owner = lax.rem(y + dy, ny) * 2 + (x if dx == 0 else 1 - x)
+        owners[(dy, dx)] = owner.astype(jnp.int32).reshape(1)
+        coeffs[(dy, dx)] = got[: rows * experts].reshape(rows, experts)
+        pair = got[rows * experts :].reshape(2, 1, shard)
+        gains = gains + jnp.where(slot == owner, pair, 0.0)
+    gain_a, gain_f = gains[0].reshape(1, width), gains[1].reshape(1, width)
+
+    weight_kv = gather_first(w_key, w_value, core)
+    weight_q, weight_o = gather_rest(w_query, w_out, core)
+    cot_all = lax.all_gather(cotangent, ("y", "x"), axis=0, tiled=True)
 
     x_f = tokens.astype(F32)
-    normed = (x_f * inv_root(x_f) * gain_a.astype(F32)).astype(BF)
+    normed = (x_f * inv_root(x_f) * gain_a).astype(BF)
     kv = gathered_matmul(normed, weight_kv, ids, ny, shard, kv_width)
-    keys = [kv, swap(kv, "core")]
+    beside = swap(kv, "core")
+    came = []
     for d in range(1, nz):
-        low, high = z_move(kv[:half], d), z_move(kv[half:], -d)
-        keys += [low, swap(low, "core"), high, swap(high, "core")]
+        start = jnp.where(z + d < nz, 0, half)
+        piece = lax.dynamic_slice_in_dim(kv, start, half, 0)
+        came.append(lax.ppermute(piece, "z", [(i, (i + d) % nz) for i in range(nz)]))
+    came = jnp.stack(came)
+    keys = [kv, beside, came, swap(came, "core")]
     queries = gathered_matmul(normed, weight_q, ids, ny, shard, width)
     attended, lse = attention_forward(queries, keys, seg_col, seg_row, ids, nz)
     resid, normed_f = out_project(tokens, attended, gain_f, weight_o, ids, ny, shard)
 
-    chosen = routes[0][:, :, None] == jnp.arange(experts, dtype=jnp.int32)[None, None, :]
-    coeff = jnp.sum(jnp.where(chosen, route_weights[0][:, :, None], 0.0), axis=1)
-    coeffs = {(dy, dx): to_plane(coeff, -dy % ny, dx) for dy, dx in plane if (dy, dx) != (0, 0)}
-    coeffs[(0, 0)] = coeff
-    cots = plane_gather(cotangent[:half], cotangent[half:])
-    cots[(0, 0)] = (cotangent[:half], cotangent[half:])
-    norms = plane_gather(normed_f[:half], normed_f[half:])
-    norms[(0, 0)] = (normed_f[:half], normed_f[half:])
-    order = sorted(plane, key=lambda p: (p[0] != 0) + (p[1] != 0))
-    hidden, grad_gate, grad_up, mixes, grad_norms = [], [], [], [], []
-    for where in order:
-        own = where == (0, 0)
-        h, gg, gu, mix, gnf = expert_block(
-            norms[where], cots[where], coeffs[where], w_gate, w_up, w_down, F32 if own else BF
+    from_x = swap(normed_f, "x")
+    norms = {(0, 0): [normed_f], (0, 1): [from_x]}
+    for d in range(1, ny):
+        side = from_y(normed_f, d)
+        norms[(d, 0)] = [side]
+        norms[(d, 1)] = [from_y(from_x[:half], d), swap(side[half:], "x")]
+    groups = [
+        [(0, 0)],
+        [(0, 1)] + [(d, 0) for d in range(1, ny)],
+        [(d, 1) for d in range(1, ny)],
+    ]
+    hidden, grad_gate, grad_up, mixes, grad_norms, after = [], [], [], [], [], ()
+    for group in groups:
+        own = group == [(0, 0)]
+        (h, gg, gu), mix, gnf = expert_block(
+            jnp.concatenate([owners[where] for where in group]),
+            [norms[where] for where in group],
+            cot_all,
+            [coeffs[where] for where in group],
+            w_gate,
+            w_up,
+            w_down,
+            F32 if own else BF,
+            after,
         )
+        after = (h,)
         hidden.append(h)
         grad_gate.append(gg)
         grad_up.append(gu)
-        mixes.append(mix if own else to_plane(mix, *where))
-        grad_norms.append(gnf if own else to_plane(gnf, *where))
-    flat_norms = [piece for where in order for piece in norms[where]]
-    flat_cots = [piece for where in order for piece in cots[where]]
-    count = experts // 2
-
-    def half_grads(which):
-        first = (which * count).astype(jnp.int32).reshape(1)
-        return expert_grads(first, flat_norms, flat_cots, hidden, grad_gate, grad_up, experts)
-
-    far, near = half_grads(1 - core), half_grads(core)
-    expert_totals = []
-    for one, two in zip(near, far):
-        got = swap(two, "core")
-        parts, besides = [], []
-        for e in range(count):
-            part = z_sum(add_low(one[e], got[e]), z)
-            parts.append(part)
-            besides.append(swap(part, "core"))
-        expert_totals.append(
-            spread_halves(
-                jnp.stack(parts), jnp.stack(besides), core.astype(jnp.int32).reshape(1)
-            )
-        )
+        for where, one, two in zip(group, mix, gnf):
+            mixes.append(one if own else to_plane(one, *where))
+            grad_norms.append(two if own else to_plane(two, *where))
+    order = [where for group in groups for where in group]
+    expert_parts = expert_grads(
+        jnp.concatenate([owners[where] for where in order]),
+        [piece for where in order for piece in norms[where]],
+        cot_all,
+        hidden,
+        grad_gate,
+        grad_up,
+        experts,
+        rows,
+    )
+    expert_shard = lax.psum_scatter(
+        expert_parts, ("z", "core"), scatter_dimension=0, tiled=True
+    )
     result = resid
     for mix in mixes:
         result = result + mix.astype(F32)
+    result = result.astype(BF)
 
     gres, branch, grad_att, ggain_f = out_back(
-        resid, cotangent, gain_f, grad_norms, weight_o, ids, ny, shard
-    )
-
-    def columns(v, which):
-        n = v.shape[1] // 2
-        return lax.dynamic_slice(v, (0, which * n), (v.shape[0], n))
-
-    def weight_grad(left, right):
-        return tuple(tn(left, columns(right, which)).astype(BF) for which in (core, 1 - core))
-
-    grad_wo = whole_grad(*weight_grad(attended, branch), y, x, z, core)
+        resid, cotangent, gain_f, grad_norms, weight_o, ids, ny, shard, (expert_parts,)
+    )
     dq, dkv_mine, dkv_other = attention_backward(
         queries, keys, seg_col, seg_row, attended, grad_att, lse, ids, nz
     )
+    oq = weight_grads(ids, [(attended, branch), (normed, dq)])
+    dkv_mine = lax.optimization_barrier((dkv_mine, oq[0]))[0]
     parts = add_low(dkv_mine, swap(dkv_other, "core"))
     low = parts[0].astype(F32)
     high = lax.dynamic_index_in_dim(parts, z + 1, 0, keepdims=False).astype(F32)
     for d in range(1, nz):
-        low = low + z_move(parts[d], -d).astype(F32)
-        far_high = lax.dynamic_index_in_dim(
-            parts, jnp.minimum(z + 1 + d, nz), 0, keepdims=False
-        )
-        high = high + z_move(far_high, d).astype(F32)
+        index = jnp.where(d <= z, d, z + 1 + nz - d)
+        piece = lax.dynamic_index_in_dim(parts, index, 0, keepdims=False)
+        got = lax.ppermute(piece, "z", [((i + d) % nz, i) for i in range(nz)]).astype(F32)
+        low = low + jnp.where(z + d < nz, got, 0.0)
+        high = high + jnp.where(z + d < nz, 0.0, got)
     dkv = jnp.concatenate([low, high], axis=0).astype(BF)
-    grad_wq = whole_grad(*weight_grad(normed, dq), y, x, z, core)
-    grad_wkv = whole_grad(*weight_grad(normed, dkv), y, x, z, core)
+    expert_shard = lax.optimization_barrier((expert_shard, dkv))[0]
+    expert_totals = spread_grads(
+        lax.all_gather(expert_shard, ("z", "core"), axis=0, tiled=True), experts
+    )
+    grad_wo, grad_wq = whole_grads(*oq, 2, y, x, z, core)
+    (grad_wkv,) = whole_grads(*weight_grads(ids, [(normed, dkv)]), 1, y, x, z, core)
     grad_tokens, ggain_a = in_back(
-        tokens, gres, gain_a, dq, dkv, weight_q, weight_kv, ids, ny, shard
+        tokens, gres, gain_a, dq, dkv, weight_q, weight_kv, ids, ny, shard, (result,)
     )
 
     ggains = jnp.concatenate([ggain_a, ggain_f], axis=0)
@@ -956,7 +999,7 @@
     total = z_sum(total, z)
     kv_cut = w_key.shape[1]
     return (
-        result.astype(BF)[None],
+        result[None],
         grad_tokens[None],
         total[0],
         grad_wq,

time: 785 us -> 550 us (0.70)
  starting transfers between devices: 209 us -> 90.7 us
  waiting for transfers between devices: 326 us -> 230 us
  other arithmetic: 46.3 us -> 28.9 us
  between operations: 3.13 us -> 15.3 us
  matrix products: 8.75 us -> 0 us
    ppermute x13 -> x4, waiting for transfers between devices: 161 us -> 16.1 us  [z_sum(): outer = lax.ppermute(whole, 'z', [(1, 0), (2, 3)])]
    ppermute x12 -> x6, starting transfers between devices: 62.9 us -> 16.6 us  [the longest x3 11.9 us: body(): lax.ppermute(piece, 'z', [((i + d) % nz, i) for i in range(nz)]).astype(F32)]
    ppermute x11 -> x8, waiting for transfers between devices: 4.94 us -> 51 us  [to_y(): return lax.ppermute(v, 'y', [(i, (i + d) % n) for i in range(n)])]
    ppermute x12 -> x6, waiting for transfers between devices: 20.4 us -> 56.1 us  [the longest x3 34.5 us: body(): lax.ppermute(piece, 'z', [((i + d) % nz, i) for i in range(nz)]).astype(F32)]
    ppermute x13 -> x4, waiting for transfers between devices: 56.7 us -> 22.3 us  [z_sum(): inner = add_low(v, lax.ppermute(v, 'z', [(0, 1), (3, 2)]))]
    reduce_scatter x0 -> x1, waiting for transfers between devices: none -> 27.7 us  [body(): lax.psum_scatter(expert_parts, ('z', 'core'), scatter_dimension=0, tiled=...]
    ppermute x71 -> x22, starting transfers between devices: 38.6 us -> 15.4 us  [swap(): return lax.ppermute(v, axis, [(0, 1), (1, 0)])]
    ppermute x71 -> x22, waiting for transfers between devices: 54.8 us -> 33.3 us  [swap(): return lax.ppermute(v, axis, [(0, 1), (1, 0)])]
  transfers between devices with their start and end apart: 153 -> 60, of which waited for: 44 -> 23; matrix products, arithmetic and copies ran while one was open for 8% -> 7% of each run, Pallas kernels for 21% -> 28%
where the time goes in v2:
time: 550 us; the launch traced here: 541 us
  waiting for transfers between devices  230 us (42%)
  Pallas kernels  160 us (29%)
  starting transfers between devices  90.7 us (16%)
  other arithmetic  28.9 us (5%)
  local copies, waits for them, and re-layouts  16.2 us (3%)
  between operations  15.3 us (3%)
    ppermute x8, waiting for transfers between devices, to_y(): return lax.ppermute(v, 'y', [(i, (i + d) % n) for i in range(n)])  51 us
    pallas_call x3, Pallas kernels, expert_block(): pl.pallas_call(kernel, grid_spec=pltpu.PrefetchScalarGridSpec(num_scalar_...  48.5 us
    ppermute x3, waiting for transfers between devices, body(): lax.ppermute(piece, 'z', [((i + d) % nz, i) for i in range(nz)]).astype(F32)  34.5 us
    ppermute x22, waiting for transfers between devices, swap(): return lax.ppermute(v, axis, [(0, 1), (1, 0)])  33.3 us
    reduce_scatter x1, waiting for transfers between devices, body(): lax.psum_scatter(expert_parts, ('z', 'core'), scatter_dimension=0, tiled=...  27.7 us
    ppermute x4, starting transfers between devices, z_sum(): inner = add_low(v, lax.ppermute(v, 'z', [(0, 1), (3, 2)]))  27.4 us
    ppermute x4, waiting for transfers between devices, z_sum(): inner = add_low(v, lax.ppermute(v, 'z', [(0, 1), (3, 2)]))  22.3 us
    ppermute x3, waiting for transfers between devices, body(): lax.ppermute(piece, 'z', [(i, (i + d) % nz) for i in range(nz)])  21.7 us
  transfers between devices with their start and end apart: 60, of which 23 were waited for; matrix products, arithmetic and copies ran while one was open for 7% of the time, Pallas kernels for 28%

profile of v2, /device:TPU:0, one launch (start us, length us, event | category | flops | bytes accessed | tf_op | source)
XLA Modules:
  0.0 541.4 jit_solution(15834226855802485525)
XLA Ops:
  19.2 11.4 %collective-permute-done.3 = bf16[384,512]{1,0:T(8,128)(2,1)S(1)} collective-permute-done((bf16[384,512]{1,0:T(8,128)(2,1)S(1)}, bf16[384,512]{1,0:T(8,128)(2,1)S(1)}, u32[]{:S(2)}, u32[]{:S(2)}) %collective-permute-start.3) | collective-permute-done | bytes 393248 | tf_op jit(solution)/shard_map/ppermute | solution.py:53
  34.9 5.8 %collective-permute-done.5 = bf16[192,512]{1,0:T(8,128)(2,1)S(1)} collective-permute-done((bf16[192,512]{1,0:T(8,128)(2,1)S(1)}, bf16[192,512]{1,0:T(8,128)(2,1)S(1)}, u32[]{:S(2)}, u32[]{:S(2)}) %collective-permute-start.5) | collective-permute-done | bytes 196640 | tf_op jit(solution)/shard_map/ppermute | solution.py:63
  46.6 4.8 project.3.refs_0_
  57.5 5.8 %collective-permute-done.11 = bf16[128,1024]{1,0:T(8,128)(2,1)S(1)} collective-permute-done((bf16[128,1024]{1,0:T(8,128)(2,1)S(1)}, bf16[128,1024]{1,0:T(8,128)(2,1)S(1)}, u32[]{:S(2)}, u32[]{:S(2)}) %collective-permute-start.11) | collective-permute-done | bytes 262176 | tf_op jit(solution)/shard_map/ppermute | solution.py:902
  63.3 15.8 %collective-permute-done.10 = bf16[128,1024]{1,0:T(8,128)(2,1)S(1)} collective-permute-done((bf16[128,1024]{1,0:T(8,128)(2,1)S(1)}, bf16[128,1024]{1,0:T(8,128)(2,1)S(1)}, u32[]{:S(2)}, u32[]{:S(2)}) %collective-permute-start.10) | collective-permute-done | bytes 262176 | tf_op jit(solution)/shard_map/ppermute | solution.py:902
  81.8 5.8 %project.2.q_ref = bf16[256,1536]{1,0:T(8,128)(2,1)} custom-call(s32[4]{0:T(128)} %pad_add_fusion.ids_ref, bf16[256,1536]{1,0:T(8,128)(2,1)} %fusion.2.lhs_ref.refs_2_.refs_0_, bf16[3072,1536]{1,0:T(8,128)(2,1)} %all-gather.5.cloned.1.call-done.refs_0_.refs_4_), custom_call_target="tpu_custom_call" | custom-call | flops 1207959552 | bytes 5505024 | tf_op jit(solution)/shard_map/project/pallas_call | solution.py:233
  89.3 16.9 %attend.1 = (bf16[256,1536]{1,0:T(8,128)(2,1)}, f32[8,768]{1,0:T(8,128)}) custom-call(s32[4]{0:T(128)} %pad_add_fusion.ids_ref, bf16[256,1536]{1,0:T(8,128)(2,1)} %project.2.q_ref, s32[2048,1]{1,0:T(8,128)} %copy.39.col_ref, s32[1,2048]{1,0:T(1,128)} %row_ref.3, bf16[256,1024]{1,0:T(8,128)(2,1)} %project.3.refs_0_, bf16[256,1024]{1,0:T(8,128)(2,1)} %copy-done.27, ...), custom_call_target="tpu_custom_call" | custom-call | flops 8053063680 | bytes 2621440 | tf_op jit(solution)/shard_map/attend/pallas_call | solution.py:410
  106.2 6.7 %out_project.1 = (f32[256,1536]{1,0:T(8,128)}, bf16[256,1536]{1,0:T(8,128)(2,1)}) custom-call(s32[4]{0:T(128)} %pad_add_fusion.ids_ref, bf16[256,1536]{1,0:T(8,128)(2,1)} %bitcast.116, bf16[256,1536]{1,0:T(8,128)(2,1)} %get-tuple-element.50.att_ref.refs_0_, f32[1,1536]{1,0:T(1,128)} %bitcast.123, bf16[3072,1536]{1,0:T(8,128)(2,1)} %all-gather.5.cloned.1.call-done.refs_0_.refs_4_), custom_call_target="tpu_custom_call" | custom-call | flops 1207959552 | bytes 8650752 | tf_op jit(solution)/shard_map/out_project/pallas_call | solution.py:530
  119.1 15.6 %all-gather.9.cloned.1.call-done = bf16[1,1024,1536]{2,1,0:T(8,128)(2,1)} async-done(((bf16[1,256,1536]{2,1,0:T(8,128)(2,1)}), bf16[1,1024,1536]{2,1,0:T(8,128)(2,1)}) %all-gather.9.cloned.1.call-update) | async-done | bytes 3145744 | tf_op jit(solution)/shard_map/all_gather | solution.py:892
  134.7 13.6 %experts.3 = (bf16[256,1024]{1,0:T(8,128)(2,1)}, bf16[256,1024]{1,0:T(8,128)(2,1)}, bf16[256,1024]{1,0:T(8,128)(2,1)}, f32[256,1536]{1,0:T(8,128)}, f32[256,1536]{1,0:T(8,128)}) custom-call(s32[1]{0:T(128)} %bitcast.13.id_ref, bf16[256,1536]{1,0:T(8,128)(2,1)} %get-tuple-element.52.refs_0_, bf16[1024,1536]{1,0:T(8,128)(2,1)} %bitcast.132, ...), custom_call_target="tpu_custom_call" | custom-call | flops 4831838208 | bytes 13369344 | tf_op jit(solution)/shard_map/experts/pallas_call | solution.py:678
  150.7 22.2 %experts.4 = (bf16[512,1024]{1,0:T(8,128)(2,1)}, bf16[512,1024]{1,0:T(8,128)(2,1)}, bf16[512,1024]{1,0:T(8,128)(2,1)}, bf16[256,1536]{1,0:T(8,128)(2,1)}, bf16[2...) custom-call(s32[2]{0:T(128)} %pad_add_fusion.1.id_ref, bf16[256,1536]{1,0:T(8,128)(2,1)} %copy-done.16, ...), custom_call_target="tpu_custom_call" | custom-call | flops 9663676416 | bytes 17301504 | tf_op jit(solution)/shard_map/experts/pallas_call | solution.py:678
  175.8 12.7 %experts.5 = (bf16[256,1024]{1,0:T(8,128)(2,1)}, bf16[256,1024]{1,0:T(8,128)(2,1)}, bf16[256,1024]{1,0:T(8,128)(2,1)}, bf16[256,1536]{1,0:T(8,128)(2,1)}, bf16[256,1536]{1,0:T(8,128)(2,1)}) custom-call(s32[1]{0:T(128)} %bitcast.17.id_ref, bf16[128,1536]{1,0:T(8,128)(2,1)} %copy-done.28, bf16[128,1536]{1,0:T(8,128)(2,1)} %copy-done.29, ...), custom_call_target="tpu_custom_call" | custom-call | flops 4831838208 | bytes 13369344 | tf_op jit(solution)/shard_map/experts/pallas_call | solution.py:678
  190.1 17.3 %expert_grads.1.refs_5_ = bf16[6144,768]{1,0:T(8,128)(2,1)} custom-call(s32[4]{0:T(128)} %pad_add_fusion.2.id_ref, bf16[256,1536]{1,0:T(8,128)(2,1)} %get-tuple-element.52.refs_0_, bf16[256,1536]{1,0:T(8,128)(2,1)} %copy-done.16, bf16[256,1536]{1,0:T(8,128)(2,1)} %copy-done.17, bf16[128,1536]{1,0:T(8,128)(2,1)} %copy-done.28, bf16[128,1536]{1,0:T(8,128)(2,1)} %copy-done.29, ...), custom_call_target="tpu_custom_call" | custom-call | flops 9663676416 | bytes 15728640 | tf_op jit(solution)/shard_map/expert_grads/pallas_call | solution.py:781
  210.4 7.9 %out_back.1 = (f32[256,1536]{1,0:T(8,128)}, bf16[256,1536]{1,0:T(8,128)(2,1)}, bf16[256,1536]{1,0:T(8,128)(2,1)}, f32[1,1536]{1,0:T(1,128)}) custom-call(s32[4]{0:T(128)} %pad_add_fusion.ids_ref, f32[256,1536]{1,0:T(8,128)} %get-tuple-element.51.resid_ref, bf16[256,1536]{1,0:T(8,128)(2,1)} %bitcast.119, f32[1,1536]{1,0:T(1,128)} %bitcast.124, ...), custom_call_target="tpu_custom_call" | custom-call | flops 1207959552 | bytes 12582912 | tf_op jit(solution)/shard_map/out_back/pallas_call | solution.py:569
  218.3 21.1 %attend_back.1 = (bf16[256,1536]{1,0:T(8,128)(2,1)}, bf16[5,128,1024]{2,1,0:T(8,128)(2,1)}, bf16[5,128,1024]{2,1,0:T(8,128)(2,1)}) custom-call(s32[4]{0:T(128)} %pad_add_fusion.ids_ref, bf16[256,1536]{1,0:T(8,128)(2,1)} %project.2.q_ref, s32[2048,1]{1,0:T(8,128)} %copy.39.col_ref, s32[1,2048]{1,0:T(1,128)} %row_ref.3, ...), custom_call_target="tpu_custom_call" | custom-call | flops 301989888000 | bytes 2621440 | tf_op jit(solution)/shard_map/attend_back/pallas_call | solution.py:496
  239.5 8.0 %weight_grads.2 = (bf16[1536,1536]{1,0:T(8,128)(2,1)}, bf16[1536,1536]{1,0:T(8,128)(2,1)}) custom-call(s32[4]{0:T(128)} %pad_add_fusion.ids_ref, bf16[256,1536]{1,0:T(8,128)(2,1)} %get-tuple-element.50.att_ref.refs_0_, bf16[256,1536]{1,0:T(8,128)(2,1)} %get-tuple-element.75.refs_1_, bf16[256,1536]{1,0:T(8,128)(2,1)} %fusion.2.lhs_ref.refs_2_.refs_0_, ...), custom_call_target="tpu_custom_call" | custom-call | flops 2415919104 | bytes 9437184 | tf_op jit(solution)/shard_map/weight_grads/pallas_call | solution.py:831
  248.2 11.3 %collective-permute-start.24 = (bf16[128,1024]{1,0:T(8,128)(2,1)S(1)}, bf16[128,1024]{1,0:T(8,128)(2,1)S(1)}, u32[]{:S(2)}, u32[]{:S(2)}) collective-permute-start(bf16[128,1024]{1,0:T(8,128)(2,1)S(1)} %get-tuple-element.117), channel_id=1, source_target_pairs={{8,0},{16,8},{24,16},{0,24},{9,1},{17,9},{25,17},{1,25},{10,2},{18... | collective-permute-start | bytes 786440 | tf_op jit(solution)/shard_map/ppermute | solution.py:974
  260.1 11.7 %collective-permute-done.24 = bf16[128,1024]{1,0:T(8,128)(2,1)S(1)} collective-permute-done((bf16[128,1024]{1,0:T(8,128)(2,1)S(1)}, bf16[128,1024]{1,0:T(8,128)(2,1)S(1)}, u32[]{:S(2)}, u32[]{:S(2)}) %collective-permute-start.24) | collective-permute-done | bytes 262176 | tf_op jit(solution)/shard_map/ppermute | solution.py:974
  271.8 18.7 %collective-permute-done.25 = bf16[128,1024]{1,0:T(8,128)(2,1)S(1)} collective-permute-done((bf16[128,1024]{1,0:T(8,128)(2,1)S(1)}, bf16[128,1024]{1,0:T(8,128)(2,1)S(1)}, u32[]{:S(2)}, u32[]{:S(2)}) %collective-permute-start.25) | collective-permute-done | bytes 262176 | tf_op jit(solution)/shard_map/ppermute | solution.py:974
  295.7 27.7 %reduce-scatter.2.cloned.1.call-done = bf16[768,768]{1,0:T(8,128)(2,1)} async-done(((bf16[6144,768]{1,0:T(8,128)(2,1)}), bf16[768,768]{1,0:T(8,128)(2,1)}) %reduce-scatter.2.cloned.1.call-update) | async-done | bytes 1179664 | tf_op jit(solution)/shard_map/reduce_scatter | solution.py:952
  342.1 38.7 %collective-permute-done.37 = bf16[2,192,1536]{2,1,0:T(8,128)(2,1)} collective-permute-done((bf16[2,192,1536]{2,1,0:T(8,128)(2,1)}, bf16[2,192,1536]{2,1,0:T(8,128)(2,1)}, u32[]{:S(2)}, u32[]{:S(2)}) %collective-permute-start.37) | collective-permute-done | bytes 1179680 | tf_op jit(solution)/shard_map/ppermute | solution.py:58
  386.1 10.7 %collective-permute-done.16 = bf16[256,1536]{1,0:T(8,128)(2,1)S(1)} collective-permute-done((bf16[256,1536]{1,0:T(8,128)(2,1)}, bf16[256,1536]{1,0:T(8,128)(2,1)S(1)}, u32[]{:S(2)}, u32[]{:S(2)}) %collective-permute-start.16) | collective-permute-done | bytes 786464 | tf_op jit(solution)/shard_map/ppermute | solution.py:58
  399.8 9.2 %in_back.1 = (f32[256,1536]{1,0:T(8,128)}, f32[1,1536]{1,0:T(1,128)}) custom-call(s32[4]{0:T(128)} %pad_add_fusion.ids_ref, bf16[256,1536]{1,0:T(8,128)(2,1)} %bitcast.117, f32[256,1536]{1,0:T(8,128)} %get-tuple-element.70.gres_ref, f32[1,1536]{1,0:T(1,128)} %bitcast.125, bf16[256,1536]{1,0:T(8,128)(2,1)} %get-tuple-element.73.refs_3_.dq_ref, ...), custom_call_target="tpu_custom_call" | custom-call | flops 2013265920 | bytes 12582912 | tf_op jit(solution)/shard_map/in_back/pallas_call | solution.py:607
  412.3 11.7 %collective-permute-done.35 = bf16[2,192,1536]{2,1,0:T(8,128)(2,1)S(1)} collective-permute-done((bf16[2,192,1536]{2,1,0:T(8,128)(2,1)S(1)}, bf16[2,192,1536]{2,1,0:T(8,128)(2,1)S(1)}, u32[]{:S(2)}, u32[]{:S(2)}) %collective-permute-start.35) | collective-permute-done | bytes 1179680 | tf_op jit(solution)/shard_map/ppermute | solution.py:53
  436.2 8.2 %collective-permute-start.48 = (bf16[384,512]{1,0:T(8,128)(2,1)S(1)}, bf16[384,512]{1,0:T(8,128)(2,1)S(1)}, u32[]{:S(2)}, u32[]{:S(2)}) collective-permute-start(bf16[384,512]{1,0:T(8,128)(2,1)S(1)} %pad_maximum_fusion.8), channel_id=1, source_target_pairs={{0,8},{24,16},{1,9},{25,17},{2,10},{26,18},{3,11},{27,19},{4,12},{... | collective-permute-start | bytes 1179656 | tf_op jit(solution)/shard_map/ppermute | solution.py:91
  446.1 4.1 collective-permute-start.39
  453.7 11.3 %collective-permute-done.39 = bf16[384,768]{1,0:T(8,128)(2,1)S(1)} collective-permute-done((bf16[384,768]{1,0:T(8,128)(2,1)S(1)}, bf16[384,768]{1,0:T(8,128)(2,1)S(1)}, u32[]{:S(2)}, u32[]{:S(2)}) %collective-permute-start.39) | collective-permute-done | bytes 589856 | tf_op jit(solution)/shard_map/ppermute | solution.py:91
  465.9 9.7 %collective-permute-done.52 = bf16[384,768]{1,0:T(8,128)(2,1)S(1)} collective-permute-done((bf16[384,768]{1,0:T(8,128)(2,1)S(1)}, bf16[384,768]{1,0:T(8,128)(2,1)S(1)}, u32[]{:S(2)}, u32[]{:S(2)}) %collective-permute-start.52) | collective-permute-done | bytes 589856 | tf_op jit(solution)/shard_map/ppermute | solution.py:91
  484.4 13.7 %collective-permute-start.31 = (f32[2,384]{1,0:T(2,128)S(1)}, f32[2,384]{1,0:T(2,128)S(1)}, u32[]{:S(2)}, u32[]{:S(2)}) collective-permute-start(f32[2,384]{1,0:T(2,128)S(1)} %fusion.33), channel_id=1, source_target_pairs={{0,8},{24,16},{1,9},{25,17},{2,10},{26,18},{3,11},{27,19},{4,12},{... | collective-permute-start | bytes 9224 | tf_op jit(solution)/shard_map/ppermute | solution.py:91
  501.6 7.3 %collective-permute-done.41 = bf16[384,768]{1,0:T(8,128)(2,1)S(1)} collective-permute-done((bf16[384,768]{1,0:T(8,128)(2,1)S(1)}, bf16[384,768]{1,0:T(8,128)(2,1)S(1)}, u32[]{:S(2)}, u32[]{:S(2)}) %collective-permute-start.41) | collective-permute-done | bytes 589856 | tf_op jit(solution)/shard_map/ppermute | solution.py:93
  509.0 8.8 %collective-permute-done.54 = bf16[384,768]{1,0:T(8,128)(2,1)S(1)} collective-permute-done((bf16[384,768]{1,0:T(8,128)(2,1)S(1)}, bf16[384,768]{1,0:T(8,128)(2,1)S(1)}, u32[]{:S(2)}, u32[]{:S(2)}) %collective-permute-start.54) | collective-permute-done | bytes 589856 | tf_op jit(solution)/shard_map/ppermute | solution.py:93
  523.9 10.5 %spread_grads.1 = (f32[4,1536,256]{2,1,0:T(8,128)}, f32[4,1536,256]{2,1,0:T(8,128)}, f32[4,256,1536]{2,1,0:T(8,128)}) custom-call(bf16[6144,768]{1,0:T(8,128)(2,1)} %all-gather.7.cloned.1.call-done.in_ref), custom_call_target="tpu_custom_call" | custom-call | bytes 28311552 | tf_op jit(solution)/shard_map/spread_grads/pallas_call | solution.py:802
  (262 shorter events, 121.3 us)
Async XLA Ops:
  7.2 74.6 %all-gather.5.cloned.1.call-start = ((), (), s32[]{:S(2)}) async-start(), calls=%async_computation.1 | async-start | bytes 10616832 | tf_op jit(solution)/shard_map/all_gather | solution.py:211
  9.7 125.0 %all-gather.9.cloned.1.call-start = ((), (), s32[]{:S(2)}) async-start(), calls=%async_computation.4 | async-start | bytes 3932160 | tf_op jit(solution)/shard_map/all_gather | solution.py:892
  10.7 32.9 %collective-permute-start.2 = (f32[14,128]{1,0:T(8,128)S(1)}, f32[14,128]{1,0:T(8,128)S(1)}, u32[]{:S(2)}, u32[]{:S(2)}) collective-permute-start(f32[14,128]{1,0:T(8,128)S(1)} %maximum_bitcast_fusion), channel_id=1, source_target_pairs={{0,3},{1,2},{2,1},{3,0},{4,7},{5,6},{6,5},{7,4},{8,11},{9,10},{10,... | collective-permute-start | bytes 21512 | tf_op jit(solution)/shard_map/ppermute | solution.py:73
  14.6 29.0 %collective-permute-start.1 = (f32[14,128]{1,0:T(8,128)S(1)}, f32[14,128]{1,0:T(8,128)S(1)}, u32[]{:S(2)}, u32[]{:S(2)}) collective-permute-start(f32[14,128]{1,0:T(8,128)S(1)} %maximum_bitcast_fusion), channel_id=1, source_target_pairs={{0,2},{2,0},{1,3},{3,1},{4,6},{6,4},{5,7},{7,5},{8,10},{10,8},{9,1... | collective-permute-start | bytes 21512 | tf_op jit(solution)/shard_map/ppermute | solution.py:58
  15.2 28.5 %collective-permute-start = (f32[14,128]{1,0:T(8,128)S(1)}, f32[14,128]{1,0:T(8,128)S(1)}, u32[]{:S(2)}, u32[]{:S(2)}) collective-permute-start(f32[14,128]{1,0:T(8,128)S(1)} %maximum_bitcast_fusion), channel_id=1, source_target_pairs={{0,1},{1,0},{2,3},{3,2},{4,5},{5,4},{6,7},{7,6},{8,9},{9,8},{10,11... | collective-permute-start | bytes 21512 | tf_op jit(solution)/shard_map/ppermute | solution.py:53
  18.8 304.6 %reduce-scatter.2.cloned.1.call-start = ((), (), s32[]{:S(2)}) async-start(), calls=%async_computation.2 | async-start | bytes 10616832 | tf_op jit(solution)/shard_map/reduce_scatter | solution.py:952
  56.5 22.6 %collective-permute-start.10 = (bf16[128,1024]{1,0:T(8,128)(2,1)S(1)}, bf16[128,1024]{1,0:T(8,128)(2,1)S(1)}, u32[]{:S(2)}, u32[]{:S(2)}) collective-permute-start(bf16[128,1024]{1,0:T(8,128)(2,1)S(1)} %get-tuple-element.122), channel_id=1, source_target_pairs={{0,16},{8,24},{16,0},{24,8},{1,17},{9,25},{17,1},{25,9},{2,18},{10... | collective-permute-start | bytes 786440 | tf_op jit(solution)/shard_map/ppermute | solution.py:902
  56.5 22.6 %collective-permute-start.9 = (bf16[128,1024]{1,0:T(8,128)(2,1)S(1)}, bf16[128,1024]{1,0:T(8,128)(2,1)S(1)}, u32[]{:S(2)}, u32[]{:S(2)}) collective-permute-start(bf16[128,1024]{1,0:T(8,128)(2,1)S(1)} %get-tuple-element.120), channel_id=1, source_target_pairs={{0,8},{8,16},{16,24},{24,0},{1,9},{9,17},{17,25},{25,1},{2,10},{10... | collective-permute-start | bytes 786440 | tf_op jit(solution)/shard_map/ppermute | solution.py:902
  113.0 35.3 %collective-permute-start.13 = (bf16[256,1536]{1,0:T(8,128)(2,1)}, bf16[256,1536]{1,0:T(8,128)(2,1)S(1)}, u32[]{:S(2)}, u32[]{:S(2)}) collective-permute-start(bf16[256,1536]{1,0:T(8,128)(2,1)} %get-tuple-element.52.refs_0_), channel_id=1, source_target_pairs={{0,1},{1,0},{2,3},{3,2},{4,5},{5,4},{6,7},{7,6},{8,9},{9,8},{10,11... | collective-permute-start | bytes 2359304 | tf_op jit(solution)/shard_map/ppermute | solution.py:53
  114.7 35.1 %collective-permute-start.14 = (bf16[256,1536]{1,0:T(8,128)(2,1)}, bf16[256,1536]{1,0:T(8,128)(2,1)S(1)}, u32[]{:S(2)}, u32[]{:S(2)}) collective-permute-start(bf16[256,1536]{1,0:T(8,128)(2,1)} %get-tuple-element.52.refs_0_), channel_id=1, source_target_pairs={{2,0},{0,2},{3,1},{1,3},{6,4},{4,6},{7,5},{5,7},{10,8},{8,10},{11,... | collective-permute-start | bytes 2359304 | tf_op jit(solution)/shard_map/ppermute | solution.py:63
  148.4 26.5 %collective-permute-start.17 = (bf16[128,1536]{1,0:T(8,128)(2,1)S(1)}, bf16[128,1536]{1,0:T(8,128)(2,1)S(1)}, u32[]{:S(2)}, u32[]{:S(2)}) collective-permute-start(bf16[128,1536]{1,0:T(8,128)(2,1)S(1)} %slice.126), channel_id=1, source_target_pairs={{2,0},{0,2},{3,1},{1,3},{6,4},{4,6},{7,5},{5,7},{10,8},{8,10},{11,... | collective-permute-start | bytes 1179656 | tf_op jit(solution)/shard_map/ppermute | solution.py:63
  149.8 25.1 %collective-permute-start.18 = (bf16[128,1536]{1,0:T(8,128)(2,1)S(1)}, bf16[128,1536]{1,0:T(8,128)(2,1)S(1)}, u32[]{:S(2)}, u32[]{:S(2)}) collective-permute-start(bf16[128,1536]{1,0:T(8,128)(2,1)S(1)} %slice.127), channel_id=1, source_target_pairs={{0,1},{1,0},{2,3},{3,2},{4,5},{5,4},{6,7},{7,6},{8,9},{9,8},{10,11... | collective-permute-start | bytes 1179656 | tf_op jit(solution)/shard_map/ppermute | solution.py:53
  172.9 34.8 %collective-permute-start.20 = (bf16[256,1536]{1,0:T(8,128)(2,1)}, bf16[256,1536]{1,0:T(8,128)(2,1)S(1)}, u32[]{:S(2)}, u32[]{:S(2)}) collective-permute-start(bf16[256,1536]{1,0:T(8,128)(2,1)} %get-tuple-element.60), channel_id=1, source_target_pairs={{0,1},{1,0},{2,3},{3,2},{4,5},{5,4},{6,7},{7,6},{8,9},{9,8},{10,11... | collective-permute-start | bytes 2359304 | tf_op jit(solution)/shard_map/ppermute | solution.py:53
  174.2 35.1 %collective-permute-start.21 = (bf16[256,1536]{1,0:T(8,128)(2,1)}, bf16[256,1536]{1,0:T(8,128)(2,1)S(1)}, u32[]{:S(2)}, u32[]{:S(2)}) collective-permute-start(bf16[256,1536]{1,0:T(8,128)(2,1)} %get-tuple-element.61), channel_id=1, source_target_pairs={{0,2},{2,0},{1,3},{3,1},{4,6},{6,4},{5,7},{7,5},{8,10},{10,8},{9,1... | collective-permute-start | bytes 2359304 | tf_op jit(solution)/shard_map/ppermute | solution.py:58
  188.5 20.8 %collective-permute-start.22 = (bf16[256,1536]{1,0:T(8,128)(2,1)}, bf16[256,1536]{1,0:T(8,128)(2,1)S(1)}, u32[]{:S(2)}, u32[]{:S(2)}) collective-permute-start(bf16[256,1536]{1,0:T(8,128)(2,1)} %get-tuple-element.62), channel_id=1, source_target_pairs={{0,3},{1,2},{2,1},{3,0},{4,7},{5,6},{6,5},{7,4},{8,11},{9,10},{10,... | collective-permute-start | bytes 2359304 | tf_op jit(solution)/shard_map/ppermute | solution.py:73
  207.5 316.4 %all-gather.7.cloned.1.call-start = ((), (), s32[]{:S(2)}) async-start(), calls=%async_computation.3 | async-start | bytes 10616832 | tf_op jit(solution)/shard_map/all_gather | solution.py:980
  248.2 23.6 %collective-permute-start.24 = (bf16[128,1024]{1,0:T(8,128)(2,1)S(1)}, bf16[128,1024]{1,0:T(8,128)(2,1)S(1)}, u32[]{:S(2)}, u32[]{:S(2)}) collective-permute-start(bf16[128,1024]{1,0:T(8,128)(2,1)S(1)} %get-tuple-element.117), channel_id=1, source_target_pairs={{8,0},{16,8},{24,16},{0,24},{9,1},{17,9},{25,17},{1,25},{10,2},{18... | collective-permute-start | bytes 786440 | tf_op jit(solution)/shard_map/ppermute | solution.py:974
  259.5 31.0 %collective-permute-start.25 = (bf16[128,1024]{1,0:T(8,128)(2,1)S(1)}, bf16[128,1024]{1,0:T(8,128)(2,1)S(1)}, u32[]{:S(2)}, u32[]{:S(2)}) collective-permute-start(bf16[128,1024]{1,0:T(8,128)(2,1)S(1)} %get-tuple-element.116), channel_id=1, source_target_pairs={{16,0},{24,8},{0,16},{8,24},{17,1},{25,9},{1,17},{9,25},{18,2},{26... | collective-permute-start | bytes 786440 | tf_op jit(solution)/shard_map/ppermute | solution.py:974
  259.5 35.1 %collective-permute-start.26 = (bf16[128,1024]{1,0:T(8,128)(2,1)S(1)}, bf16[128,1024]{1,0:T(8,128)(2,1)S(1)}, u32[]{:S(2)}, u32[]{:S(2)}) collective-permute-start(bf16[128,1024]{1,0:T(8,128)(2,1)S(1)} %get-tuple-element.115), channel_id=1, source_target_pairs={{24,0},{0,8},{8,16},{16,24},{25,1},{1,9},{9,17},{17,25},{26,2},{2,... | collective-permute-start | bytes 786440 | tf_op jit(solution)/shard_map/ppermute | solution.py:974
  334.9 46.0 %collective-permute-start.37 = (bf16[2,192,1536]{2,1,0:T(8,128)(2,1)}, bf16[2,192,1536]{2,1,0:T(8,128)(2,1)}, u32[]{:S(2)}, u32[]{:S(2)}) collective-permute-start(bf16[2,192,1536]{2,1,0:T(8,128)(2,1)} %pad_maximum_fusion.2), channel_id=1, source_target_pairs={{0,2},{2,0},{1,3},{3,1},{4,6},{6,4},{5,7},{7,5},{8,10},{10,8},{9,1... | collective-permute-start | bytes 3538952 | tf_op jit(solution)/shard_map/ppermute | solution.py:58
  336.9 59.9 %collective-permute-start.16 = (bf16[256,1536]{1,0:T(8,128)(2,1)}, bf16[256,1536]{1,0:T(8,128)(2,1)S(1)}, u32[]{:S(2)}, u32[]{:S(2)}) collective-permute-start(bf16[256,1536]{1,0:T(8,128)(2,1)} %get-tuple-element.56), channel_id=1, source_target_pairs={{0,2},{2,0},{1,3},{3,1},{4,6},{6,4},{5,7},{7,5},{8,10},{10,8},{9,1... | collective-permute-start | bytes 2359304 | tf_op jit(solution)/shard_map/ppermute | solution.py:58
  337.5 60.8 %collective-permute-start.15 = (bf16[256,1536]{1,0:T(8,128)(2,1)}, bf16[256,1536]{1,0:T(8,128)(2,1)S(1)}, u32[]{:S(2)}, u32[]{:S(2)}) collective-permute-start(bf16[256,1536]{1,0:T(8,128)(2,1)} %get-tuple-element.55), channel_id=1, source_target_pairs={{0,1},{1,0},{2,3},{3,2},{4,5},{5,4},{6,7},{7,6},{8,9},{9,8},{10,11... | collective-permute-start | bytes 2359304 | tf_op jit(solution)/shard_map/ppermute | solution.py:53
  339.0 59.3 %collective-permute-start.19 = (bf16[256,1536]{1,0:T(8,128)(2,1)}, bf16[256,1536]{1,0:T(8,128)(2,1)S(1)}, u32[]{:S(2)}, u32[]{:S(2)}) collective-permute-start(bf16[256,1536]{1,0:T(8,128)(2,1)} %get-tuple-element.58), channel_id=1, source_target_pairs={{0,3},{1,2},{2,1},{3,0},{4,7},{5,6},{6,5},{7,4},{8,11},{9,10},{10,... | collective-permute-start | bytes 2359304 | tf_op jit(solution)/shard_map/ppermute | solution.py:73
  340.6 68.4 %collective-permute-start.44 = (bf16[2,192,512]{2,1,0:T(8,128)(2,1)S(1)}, bf16[2,192,512]{2,1,0:T(8,128)(2,1)}, u32[]{:S(2)}, u32[]{:S(2)}) collective-permute-start(bf16[2,192,512]{2,1,0:T(8,128)(2,1)S(1)} %pad_maximum_fusion.6), channel_id=1, source_target_pairs={{0,1},{1,0},{2,3},{3,2},{4,5},{5,4},{6,7},{7,6},{8,9},{9,8},{10,11... | collective-permute-start | bytes 1179656 | tf_op jit(solution)/shard_map/ppermute | solution.py:53
  384.5 27.8 %collective-permute-start.38 = (bf16[192,1536]{1,0:T(8,128)(2,1)}, bf16[192,1536]{1,0:T(8,128)(2,1)}, u32[]{:S(2)}, u32[]{:S(2)}) collective-permute-start(bf16[192,1536]{1,0:T(8,128)(2,1)} %get-tuple-element.99), channel_id=1, source_target_pairs={{0,1},{1,0},{2,3},{3,2},{4,5},{5,4},{6,7},{7,6},{8,9},{9,8},{10,11... | collective-permute-start | bytes 1769480 | tf_op jit(solution)/shard_map/ppermute | solution.py:53
  396.8 27.3 %collective-permute-start.35 = (bf16[2,192,1536]{2,1,0:T(8,128)(2,1)S(1)}, bf16[2,192,1536]{2,1,0:T(8,128)(2,1)S(1)}, u32[]{:S(2)}, u32[]{:S(2)}) collective-permute-start(bf16[2,192,1536]{2,1,0:T(8,128)(2,1)S(1)} %pad_maximum_fusion.1), channel_id=1, source_target_pairs={{0,1},{1,0},{2,3},{3,2},{4,5},{5,4},{6,7},{7,6},{8,9},{9,8},{10,11... | collective-permute-start | bytes 3538952 | tf_op jit(solution)/shard_map/ppermute | solution.py:53
  431.0 20.6 %collective-permute-start.27 = (f32[2,1536]{1,0:T(2,128)S(1)}, f32[2,1536]{1,0:T(2,128)S(1)}, u32[]{:S(2)}, u32[]{:S(2)}) collective-permute-start(f32[2,1536]{1,0:T(2,128)S(1)} %pad_maximum_fusion.10), channel_id=1, source_target_pairs={{0,4},{4,0},{1,5},{5,1},{2,6},{6,2},{3,7},{7,3},{8,12},{12,8},{9,1... | collective-permute-start | bytes 36872 | tf_op jit(solution)/shard_map/ppermute | solution.py:53
  450.2 25.3 %collective-permute-start.52 = (bf16[384,768]{1,0:T(8,128)(2,1)S(1)}, bf16[384,768]{1,0:T(8,128)(2,1)S(1)}, u32[]{:S(2)}, u32[]{:S(2)}) collective-permute-start(bf16[384,768]{1,0:T(8,128)(2,1)S(1)} %get-tuple-element.118), channel_id=1, source_target_pairs={{0,8},{24,16},{1,9},{25,17},{2,10},{26,18},{3,11},{27,19},{4,12},{... | collective-permute-start | bytes 1769480 | tf_op jit(solution)/shard_map/ppermute | solution.py:91
  453.0 26.4 %collective-permute-start.49 = (bf16[384,512]{1,0:T(8,128)(2,1)S(1)}, bf16[384,512]{1,0:T(8,128)(2,1)S(1)}, u32[]{:S(2)}, u32[]{:S(2)}) collective-permute-start(bf16[384,512]{1,0:T(8,128)(2,1)S(1)} %add_convert_fusion.11), channel_id=1, source_target_pairs={{8,16},{16,8},{9,17},{17,9},{10,18},{18,10},{11,19},{19,11},{12,20... | collective-permute-start | bytes 1179656 | tf_op jit(solution)/shard_map/ppermute | solution.py:92
  480.1 21.2 %collective-permute-start.50 = (bf16[384,512]{1,0:T(8,128)(2,1)S(1)}, bf16[384,512]{1,0:T(8,128)(2,1)S(1)}, u32[]{:S(2)}, u32[]{:S(2)}) collective-permute-start(bf16[384,512]{1,0:T(8,128)(2,1)S(1)} %add_convert_fusion.10), channel_id=1, source_target_pairs={{8,0},{16,24},{9,1},{17,25},{10,2},{18,26},{11,3},{19,27},{12,4},{... | collective-permute-start | bytes 1179656 | tf_op jit(solution)/shard_map/ppermute | solution.py:93
  481.6 27.2 %collective-permute-start.41 = (bf16[384,768]{1,0:T(8,128)(2,1)S(1)}, bf16[384,768]{1,0:T(8,128)(2,1)S(1)}, u32[]{:S(2)}, u32[]{:S(2)}) collective-permute-start(bf16[384,768]{1,0:T(8,128)(2,1)S(1)} %add_convert_fusion.4), channel_id=1, source_target_pairs={{8,0},{16,24},{9,1},{17,25},{10,2},{18,26},{11,3},{19,27},{12,4},{... | collective-permute-start | bytes 1769480 | tf_op jit(solution)/shard_map/ppermute | solution.py:93
  483.1 34.8 %collective-permute-start.54 = (bf16[384,768]{1,0:T(8,128)(2,1)S(1)}, bf16[384,768]{1,0:T(8,128)(2,1)S(1)}, u32[]{:S(2)}, u32[]{:S(2)}) collective-permute-start(bf16[384,768]{1,0:T(8,128)(2,1)S(1)} %add_convert_fusion.2), channel_id=1, source_target_pairs={{8,0},{16,24},{9,1},{17,25},{10,2},{18,26},{11,3},{19,27},{12,4},{... | collective-permute-start | bytes 1769480 | tf_op jit(solution)/shard_map/ppermute | solution.py:93
  (58 other events, 539.1 us)
Sparse Core Ops, SparseCore 0:
  10.5 68.7 all-gather.4
  81.1 53.6 all-gather.8
  207.6 115.8 reduce-scatter.1
  324.9 93.7 all-gather.6

commit v3 on v2

--- a/solution.py
+++ b/solution.py
@@ -85,63 +85,49 @@
     return total.astype(terms[0].dtype)
 
 
-def z_sum(v, z):
+def plane_blocks(mine, other, y, x):
+    n = lax.axis_size("y")
+    rows = mine.shape[0] // (2 * n)
+    got = swap(other, "core")
+    blocks = {}
+    for dy in range(n):
+        for dx in range(2):
+            place = (lax.rem(y + dy, n) * 2 + (x if dx == 0 else 1 - x)) * rows
+            one = lax.dynamic_slice_in_dim(mine, place, rows, 0)
+            two = lax.dynamic_slice_in_dim(got, place, rows, 0)
+            blocks[(dy, dx)] = add_low(one, two)
+    return blocks
+
+
+def plane_total(blocks):
+    return add_low(
+        *[v if where == (0, 0) else to_plane(v, *where) for where, v in blocks.items()]
+    )
+
+
+def z_first(v):
+    n = lax.axis_size("z")
+    perm = [(0, 1), (3, 2)] if n == 4 else [(i, i ^ 1) for i in range(n)]
+    return add_low(v, lax.ppermute(v, "z", perm))
+
+
+def z_rest(v, z):
     n = lax.axis_size("z")
     if n == 4:
-        inner = add_low(v, lax.ppermute(v, "z", [(0, 1), (3, 2)]))
-        whole = add_low(inner, lax.ppermute(inner, "z", [(1, 2), (2, 1)]))
+        whole = add_low(v, lax.ppermute(v, "z", [(1, 2), (2, 1)]))
         outer = lax.ppermute(whole, "z", [(1, 0), (2, 3)])
         return jnp.where((z == 0) | (z == 3), outer, whole)
-    bit = 1
+    bit = 2
     while bit < n:
         v = add_low(v, lax.ppermute(v, "z", [(i, i ^ bit) for i in range(n)]))
         bit *= 2
     return v
 
 
-def plane_reduce(mine, other, y, x):
-    n = lax.axis_size("y")
-    rows = mine.shape[0] // (2 * n)
-    h = rows // 2
-    got = swap(other, "core")
-
-    def block(dy, dx, part):
-        place = (lax.rem(y + dy, n) * 2 + (x if dx == 0 else 1 - x)) * rows + part * h
-        one = lax.dynamic_slice_in_dim(mine, place, h, 0)
-        two = lax.dynamic_slice_in_dim(got, place, h, 0)
-        return one.astype(F32) + two.astype(F32)
-
-    sent_a = swap(jnp.stack([block(dy, 1, 0) for dy in range(n)]).astype(BF), "x")
-    sent_b = [
-        to_y(jnp.stack([block(d, 0, 1), block(d, 1, 1)]).astype(BF), d) for d in range(1, n)
-    ]
-    part_a = [block(dy, 0, 0) + sent_a[dy].astype(F32) for dy in range(n)]
-    part_b = [
-        block(0, dx, 1) + sum(got_b[dx].astype(F32) for got_b in sent_b) for dx in range(2)
-    ]
-    total_a = part_a[0]
-    for d in range(1, n):
-        total_a = total_a + to_y(part_a[d].astype(BF), d).astype(F32)
-    total_b = part_b[0] + swap(part_b[1].astype(BF), "x").astype(F32)
-    return jnp.concatenate([total_a.astype(BF), total_b.astype(BF)], axis=0)
-
-
-def whole_grads(mine, other, count, y, x, z, core):
-    parts = plane_reduce(mine, other, y, x)
-    n = parts.shape[1] // count
-    outs = []
-    for k in range(count):
-        own = z_sum(parts[:, k * n : (k + 1) * n], z)
-        beside = swap(own, "core").astype(F32)
-        own = own.astype(F32)
-        outs.append(
-            jnp.where(
-                core == 0,
-                jnp.concatenate([own, beside], axis=1),
-                jnp.concatenate([beside, own], axis=1),
-            )
-        )
-    return outs
+def whole_grad(own, core):
+    beside = swap(own, "core").astype(F32)
+    own = own.astype(F32)
+    return jnp.where(core == 0, own, beside), jnp.where(core == 0, beside, own)
 
 
 class Gathered:
@@ -424,7 +410,7 @@
     )(ids, q, seg_col, seg_row, *keys)
 
 
-def attention_backward(q, keys, seg_col, seg_row, attended, grad_att, lse, ids, nz):
+def attention_backward(q, keys, seg_col, seg_row, attended, grad_att, lse, ids, nz, after=()):
     rows = q.shape[0]
     half = rows // 2
     slots = nz + 1
@@ -434,7 +420,7 @@
 
     def kernel(ids_ref, q_ref, col_ref, row_ref, att_ref, grad_ref, lse_ref, *refs):
         key_refs = refs[:count]
-        dq_ref, mine_ref, other_ref, kv, dkv, masks, sems = refs[count:]
+        dq_ref, mine_ref, other_ref, kv, dkv, masks, sems = refs[count + len(after) :]
         copies = load_keys(nz, half, ids_ref, key_refs, kv, sems)
         fill_masks(nz, half, ids_ref, col_ref, row_ref, masks)
         dkv[...] = jnp.zeros_like(dkv)
@@ -500,7 +486,7 @@
             shape((slots, half, 1024), BF),
             shape((slots, half, 1024), BF),
         ),
-        in_specs=[SMEM] + [VMEM] * 6 + [ANY] * count,
+        in_specs=[SMEM] + [VMEM] * 6 + [ANY] * (count + len(after)),
         out_specs=(VMEM,) * 3,
         scratch_shapes=[
             pltpu.VMEM((slots * slot, 1024), BF),
@@ -511,7 +497,7 @@
         compiler_params=params(),
         cost_estimate=cost(300 * 256 * pairs, 2 * slots * slot * 1024, pairs),
         name="attend_back",
-    )(ids, q, seg_col, seg_row, attended, grad_att, lse, *keys)
+    )(ids, q, seg_col, seg_row, attended, grad_att, lse, *keys, *after)
 
 
 def out_project(tokens, attended, gain, weight, ids, ny, shard):
@@ -812,14 +798,28 @@
     )(grads)
 
 
-def weight_grads(ids, pairs, after=()):
+def tie(values, *after):
+    return pl.pallas_call(
+        lambda *refs: None,
+        out_shape=[shape(v.shape, v.dtype) for v in values],
+        in_specs=[ANY] * (len(values) + len(after)),
+        out_specs=[ANY] * len(values),
+        input_output_aliases={k: k for k in range(len(values))},
+        compiler_params=params(),
+        cost_estimate=cost(0, 0),
+        name="tie",
+    )(*values, *after)
+
+
+def weight_grads(ids, pairs, extra=(), after=()):
     depth = pairs[0][0].shape[1]
     halves = [right.shape[1] // 2 for _, right in pairs]
-    width = sum(halves)
+    width = sum(halves) + (128 if extra else 0)
     rows = pairs[0][0].shape[0]
+    inputs = 2 * len(pairs) + len(extra)
 
     def kernel(ids_ref, *refs):
-        mine_ref, other_ref = refs[2 * len(pairs) + len(after) :]
+        mine_ref, other_ref = refs[inputs + len(after) :]
         core, at = ids_ref[1], 0
         for k, n in enumerate(halves):
             left, right = refs[2 * k][...], refs[2 * k + 1]
@@ -827,16 +827,22 @@
                 columns = right[:, pl.ds(pl.multiple_of(side * n, 128), n)]
                 out_ref[:, at : at + n] = tn(left, columns).astype(BF)
             at += n
+        if extra:
+            lines = [ref[...] for ref in refs[2 * len(pairs) : inputs]]
+            lines.append(jnp.zeros((128 - len(extra), depth), F32))
+            turned = jnp.concatenate(lines, axis=0).T.astype(BF)
+            mine_ref[:, at:] = turned
+            other_ref[:, at:] = turned
 
     return pl.pallas_call(
         kernel,
         out_shape=(shape((depth, width), BF),) * 2,
-        in_specs=[SMEM] + [VMEM] * (2 * len(pairs)) + [ANY] * len(after),
+        in_specs=[SMEM] + [VMEM] * inputs + [ANY] * len(after),
         out_specs=(VMEM,) * 2,
         compiler_params=params(),
         cost_estimate=cost(4 * rows * depth * width, 4 * depth * width),
         name="weight_grads",
-    )(ids, *[v for pair in pairs for v in pair], *after)
+    )(ids, *[v for pair in pairs for v in pair], *extra, *after)
 
 
 def body(
@@ -921,9 +927,9 @@
     for group in groups:
         own = group == [(0, 0)]
         (h, gg, gu), mix, gnf = expert_block(
-            jnp.concatenate([owners[where] for where in group]),
+            jnp.concatenate([jnp.zeros_like(owners[where]) if own else owners[where] for where in group]),
             [norms[where] for where in group],
-            cot_all,
+            cotangent if own else cot_all,
             [coeffs[where] for where in group],
             w_gate,
             w_up,
@@ -936,7 +942,7 @@
         grad_gate.append(gg)
         grad_up.append(gu)
         for where, one, two in zip(group, mix, gnf):
-            mixes.append(one if own else to_plane(one, *where))
+            mixes.append(one)
             grad_norms.append(two if own else to_plane(two, *where))
     order = [where for group in groups for where in group]
     expert_parts = expert_grads(
@@ -952,19 +958,21 @@
     expert_shard = lax.psum_scatter(
         expert_parts, ("z", "core"), scatter_dimension=0, tiled=True
     )
-    result = resid
-    for mix in mixes:
+    gres, branch, grad_att, ggain_f = out_back(
+        resid, cotangent, gain_f, grad_norms, weight_o, ids, ny, shard, (expert_parts,)
+    )
+    mixes[1:] = tie(mixes[1:], branch)
+    result, came = resid, []
+    for where, mix in zip(order, mixes):
+        mix = mix if where == (0, 0) else to_plane(mix, *where)
+        came.append(mix)
         result = result + mix.astype(F32)
     result = result.astype(BF)
-
-    gres, branch, grad_att, ggain_f = out_back(
-        resid, cotangent, gain_f, grad_norms, weight_o, ids, ny, shard, (expert_parts,)
-    )
+    o_grads = weight_grads(ids, [(attended, branch)])
     dq, dkv_mine, dkv_other = attention_backward(
-        queries, keys, seg_col, seg_row, attended, grad_att, lse, ids, nz
-    )
-    oq = weight_grads(ids, [(attended, branch), (normed, dq)])
-    dkv_mine = lax.optimization_barrier((dkv_mine, oq[0]))[0]
+        queries, keys, seg_col, seg_row, attended, grad_att, lse, ids, nz, o_grads[:1]
+    )
+    q_grads = weight_grads(ids, [(normed, dq)], (), came[1:])
     parts = add_low(dkv_mine, swap(dkv_other, "core"))
     low = parts[0].astype(F32)
     high = lax.dynamic_index_in_dim(parts, z + 1, 0, keepdims=False).astype(F32)
@@ -975,38 +983,33 @@
         low = low + jnp.where(z + d < nz, got, 0.0)
         high = high + jnp.where(z + d < nz, 0.0, got)
     dkv = jnp.concatenate([low, high], axis=0).astype(BF)
-    expert_shard = lax.optimization_barrier((expert_shard, dkv))[0]
+    o_blocks, q_blocks = plane_blocks(*o_grads, y, x), plane_blocks(*q_grads, y, x)
+    o_total, q_total = plane_total(o_blocks), plane_total(q_blocks)
+    (expert_shard,) = tie([expert_shard], o_total, q_total, dkv)
     expert_totals = spread_grads(
         lax.all_gather(expert_shard, ("z", "core"), axis=0, tiled=True), experts
     )
-    grad_wo, grad_wq = whole_grads(*oq, 2, y, x, z, core)
-    (grad_wkv,) = whole_grads(*weight_grads(ids, [(normed, dkv)]), 1, y, x, z, core)
     grad_tokens, ggain_a = in_back(
-        tokens, gres, gain_a, dq, dkv, weight_q, weight_kv, ids, ny, shard, (result,)
-    )
-
-    ggains = jnp.concatenate([ggain_a, ggain_f], axis=0)
-    ggains = ggains + swap(ggains, "core")
-    ggains = ggains.reshape(2, 2 * ny, shard)
-
-    def gain_block(dy, dx):
-        place = lax.rem(y + dy, ny) * 2 + (x if dx == 0 else 1 - x)
-        return lax.dynamic_index_in_dim(ggains, place, 1, keepdims=False)
-
-    total = gain_block(0, 0)
-    for dy, dx in plane[1:]:
-        total = total + to_plane(gain_block(dy, dx), dy, dx)
-    total = z_sum(total, z)
-    kv_cut = w_key.shape[1]
+        tokens, gres, gain_a, dq, dkv, weight_q, weight_kv, ids, ny, shard
+    )
+    o_first, q_first = z_first(o_total), z_first(q_total)
+    kv_grads = weight_grads(ids, [(normed, dkv)], (ggain_a, ggain_f), (o_first,))
+    kv_blocks = plane_blocks(*kv_grads, y, x)
+    grad_wo = jnp.concatenate(whole_grad(z_rest(o_first, z), core), axis=1)
+    grad_wq = jnp.concatenate(whole_grad(z_rest(q_first, z), core), axis=1)
+    kv_first = z_first(plane_total(kv_blocks))
+    grad_wk, grad_wv = whole_grad(z_rest(kv_first, z), core)
+    ggain_a, ggain_f = grad_wk[:, -128], grad_wk[:, -127]
+    grad_wk, grad_wv = grad_wk[:, :-128], grad_wv[:, :-128]
     return (
         result[None],
         grad_tokens[None],
-        total[0],
+        ggain_a,
         grad_wq,
-        grad_wkv[:, :kv_cut],
-        grad_wkv[:, kv_cut:],
+        grad_wk,
+        grad_wv,
         grad_wo,
-        total[1],
+        ggain_f,
         *expert_totals,
     )
 

time: 550 us -> 516 us (0.938)
  waiting for transfers between devices: 230 us -> 200 us
  starting transfers between devices: 90.7 us -> 75 us
  other arithmetic: 28.9 us -> 36.1 us
    ppermute x12 -> x9, waiting for transfers between devices: 38.4 us -> 75.4 us  [the longest x3 45.5 us: z_rest(): outer = lax.ppermute(whole, 'z', [(1, 0), (2, 3)])]
    reduce_scatter x1, waiting for transfers between devices: 27.7 us -> 0.01 us  [body(): lax.psum_scatter(expert_parts, ('z', 'core'), scatter_dimension=0, tiled=...]
    ppermute x8 -> x6, waiting for transfers between devices: 51 us -> 23.8 us  [to_y(): return lax.ppermute(v, 'y', [(i, (i + d) % n) for i in range(n)])]
    convert_element_type x7 -> x13, other arithmetic: 1.27 us -> 19 us  [add_low(): return total.astype(terms[0].dtype)]
    all_gather x1, waiting for transfers between devices: 15.6 us -> 0.01 us  [body(): cot_all = lax.all_gather(cotangent, ('y', 'x'), axis=0, tiled=True)]
    convert_element_type x13 -> x2, other arithmetic: 13.2 us -> 0.17 us  [the longest x1 0.11 us: whole_grad(): own = own.astype(F32)]
    ppermute x4 -> x6, waiting for transfers between devices: 0.01 us -> 8.59 us  [to_plane(): return lax.ppermute(v, ('y', 'x'), perm)]
    ppermute x3, starting transfers between devices: 11.9 us -> 4.14 us  [body(): lax.ppermute(piece, 'z', [((i + d) % nz, i) for i in range(nz)]).astype(F32)]
  transfers between devices with their start and end apart: 60 -> 55, of which waited for: 23 -> 19; matrix products, arithmetic and copies ran while one was open for 7% -> 9% of each run, Pallas kernels for 28% -> 30%
where the time goes in v3:
time: 516 us; the launch traced here: 507 us
  waiting for transfers between devices  200 us (39%)
  Pallas kernels  164 us (32%)
  starting transfers between devices  75 us (15%)
  other arithmetic  36.1 us (7%)
  local copies, waits for them, and re-layouts  17.4 us (3%)
  between operations  15 us (3%)
    pallas_call x3, Pallas kernels, expert_block(): pl.pallas_call(kernel, grid_spec=pltpu.PrefetchScalarGridSpec(num_scalar_...  48.4 us
    ppermute x3, waiting for transfers between devices, z_rest(): outer = lax.ppermute(whole, 'z', [(1, 0), (2, 3)])  45.5 us
    ppermute x3, waiting for transfers between devices, body(): lax.ppermute(piece, 'z', [((i + d) % nz, i) for i in range(nz)]).astype(F32)  33.8 us
    ppermute x3, waiting for transfers between devices, z_first(): return add_low(v, lax.ppermute(v, 'z', perm))  29.9 us
    ppermute x20, waiting for transfers between devices, swap(): return lax.ppermute(v, axis, [(0, 1), (1, 0)])  28.7 us
    ppermute x6, waiting for transfers between devices, to_y(): return lax.ppermute(v, 'y', [(i, (i + d) % n) for i in range(n)])  23.8 us
    ppermute x3, starting transfers between devices, z_first(): return add_low(v, lax.ppermute(v, 'z', perm))  22.9 us
    ppermute x3, waiting for transfers between devices, body(): lax.ppermute(piece, 'z', [(i, (i + d) % nz) for i in range(nz)])  21.7 us
  transfers between devices with their start and end apart: 55, of which 19 were waited for; matrix products, arithmetic and copies ran while one was open for 9% of the time, Pallas kernels for 30%

profile of v3, /device:TPU:0, one launch (start us, length us, event | category | flops | bytes accessed | tf_op | source)
XLA Modules:
  0.0 507.4 jit_solution(8620656921622357712)
XLA Ops:
  19.2 11.4 %collective-permute-done.3 = bf16[384,512]{1,0:T(8,128)(2,1)S(1)} collective-permute-done((bf16[384,512]{1,0:T(8,128)(2,1)S(1)}, bf16[384,512]{1,0:T(8,128)(2,1)S(1)}, u32[]{:S(2)}, u32[]{:S(2)}) %collective-permute-start.3) | collective-permute-done | bytes 393248 | tf_op jit(solution)/shard_map/ppermute | solution.py:53
  34.9 5.8 %collective-permute-done.5 = bf16[192,512]{1,0:T(8,128)(2,1)S(1)} collective-permute-done((bf16[192,512]{1,0:T(8,128)(2,1)S(1)}, bf16[192,512]{1,0:T(8,128)(2,1)S(1)}, u32[]{:S(2)}, u32[]{:S(2)}) %collective-permute-start.5) | collective-permute-done | bytes 196640 | tf_op jit(solution)/shard_map/ppermute | solution.py:63
  46.6 4.8 project.3.refs_0_
  57.4 5.8 %collective-permute-done.11 = bf16[128,1024]{1,0:T(8,128)(2,1)S(1)} collective-permute-done((bf16[128,1024]{1,0:T(8,128)(2,1)S(1)}, bf16[128,1024]{1,0:T(8,128)(2,1)S(1)}, u32[]{:S(2)}, u32[]{:S(2)}) %collective-permute-start.11) | collective-permute-done | bytes 262176 | tf_op jit(solution)/shard_map/ppermute | solution.py:908
  63.2 16.0 %collective-permute-done.10 = bf16[128,1024]{1,0:T(8,128)(2,1)S(1)} collective-permute-done((bf16[128,1024]{1,0:T(8,128)(2,1)S(1)}, bf16[128,1024]{1,0:T(8,128)(2,1)S(1)}, u32[]{:S(2)}, u32[]{:S(2)}) %collective-permute-start.10) | collective-permute-done | bytes 262176 | tf_op jit(solution)/shard_map/ppermute | solution.py:908
  81.8 5.8 %project.2.q_ref = bf16[256,1536]{1,0:T(8,128)(2,1)} custom-call(s32[4]{0:T(128)} %pad_add_fusion.ids_ref, bf16[256,1536]{1,0:T(8,128)(2,1)} %fusion.2.lhs_ref.refs_0_, bf16[3072,1536]{1,0:T(8,128)(2,1)} %all-gather.5.cloned.1.call-done.refs_0_.refs_4_), custom_call_target="tpu_custom_call" | custom-call | flops 1207959552 | bytes 5505024 | tf_op jit(solution)/shard_map/project/pallas_call | solution.py:219
  89.3 16.9 %attend.1 = (bf16[256,1536]{1,0:T(8,128)(2,1)}, f32[8,768]{1,0:T(8,128)}) custom-call(s32[4]{0:T(128)} %pad_add_fusion.ids_ref, bf16[256,1536]{1,0:T(8,128)(2,1)} %project.2.q_ref, s32[2048,1]{1,0:T(8,128)} %copy.43.col_ref, s32[1,2048]{1,0:T(1,128)} %row_ref.3, bf16[256,1024]{1,0:T(8,128)(2,1)} %project.3.refs_0_, bf16[256,1024]{1,0:T(8,128)(2,1)} %copy-done.30, ...), custom_call_target="tpu_custom_call" | custom-call | flops 8053063680 | bytes 2621440 | tf_op jit(solution)/shard_map/attend/pallas_call | solution.py:396
  106.2 6.7 %out_project.1 = (f32[256,1536]{1,0:T(8,128)}, bf16[256,1536]{1,0:T(8,128)(2,1)}) custom-call(s32[4]{0:T(128)} %pad_add_fusion.ids_ref, bf16[256,1536]{1,0:T(8,128)(2,1)} %bitcast.46, bf16[256,1536]{1,0:T(8,128)(2,1)} %get-tuple-element.53.att_ref.refs_0_, f32[1,1536]{1,0:T(1,128)} %bitcast.53, bf16[3072,1536]{1,0:T(8,128)(2,1)} %all-gather.5.cloned.1.call-done.refs_0_.refs_4_), custom_call_target="tpu_custom_call" | custom-call | flops 1207959552 | bytes 8650752 | tf_op jit(solution)/shard_map/out_project/pallas_call | solution.py:516
  119.0 13.6 %experts.3 = (bf16[256,1024]{1,0:T(8,128)(2,1)}, bf16[256,1024]{1,0:T(8,128)(2,1)}, bf16[256,1024]{1,0:T(8,128)(2,1)}, f32[256,1536]{1,0:T(8,128)}, f32[256,1536]{1,0:T(8,128)}) custom-call(s32[1]{0:T(128)} %constant.65.clone.1.id_ref, bf16[256,1536]{1,0:T(8,128)(2,1)} %get-tuple-element.55.refs_0_, bf16[256,1536]{1,0:T(8,128)(2,1)} %bitcast.48, ...), custom_call_target="tpu_custom_call" | custom-call | flops 4831838208 | bytes 13369344 | tf_op jit(solution)/shard_map/experts/pallas_call | solution.py:664
  132.6 9.4 %collective-permute-done.13.refs_0_.refs_1_ = bf16[256,1536]{1,0:T(8,128)(2,1)S(1)} collective-permute-done((bf16[256,1536]{1,0:T(8,128)(2,1)}, bf16[256,1536]{1,0:T(8,128)(2,1)S(1)}, u32[]{:S(2)}, u32[]{:S(2)}) %collective-permute-start.13) | collective-permute-done | bytes 786464 | tf_op jit(solution)/shard_map/ppermute | solution.py:53
  144.5 22.2 %experts.4 = (bf16[512,1024]{1,0:T(8,128)(2,1)}, bf16[512,1024]{1,0:T(8,128)(2,1)}, bf16[512,1024]{1,0:T(8,128)(2,1)}, bf16[256,1536]{1,0:T(8,128)(2,1)}, bf16[2...) custom-call(s32[2]{0:T(128)} %pad_add_fusion.1.id_ref, bf16[256,1536]{1,0:T(8,128)(2,1)} %copy-done.21, ...), custom_call_target="tpu_custom_call" | custom-call | flops 9663676416 | bytes 17301504 | tf_op jit(solution)/shard_map/experts/pallas_call | solution.py:664
  169.3 12.6 %experts.5 = (bf16[256,1024]{1,0:T(8,128)(2,1)}, bf16[256,1024]{1,0:T(8,128)(2,1)}, bf16[256,1024]{1,0:T(8,128)(2,1)}, bf16[256,1536]{1,0:T(8,128)(2,1)}, bf16[256,1536]{1,0:T(8,128)(2,1)}) custom-call(s32[1]{0:T(128)} %bitcast.17.id_ref, bf16[128,1536]{1,0:T(8,128)(2,1)} %copy-done.31, bf16[128,1536]{1,0:T(8,128)(2,1)} %collective-permute-done.16.refs_1_.refs_4_, ...), custom_call_target="tpu_custom_call" | custom-call | flops 4831838208 | bytes 13369344 | tf_op jit(solution)/shard_map/experts/pallas_call | solution.py:664
  183.7 17.4 %expert_grads.1.refs_5_ = bf16[6144,768]{1,0:T(8,128)(2,1)} custom-call(s32[4]{0:T(128)} %pad_add_fusion.2.id_ref, bf16[256,1536]{1,0:T(8,128)(2,1)} %get-tuple-element.55.refs_0_, bf16[256,1536]{1,0:T(8,128)(2,1)} %copy-done.21, bf16[256,1536]{1,0:T(8,128)(2,1)} %copy-done.22, bf16[128,1536]{1,0:T(8,128)(2,1)} %copy-done.31, ...), custom_call_target="tpu_custom_call" | custom-call | flops 9663676416 | bytes 15728640 | tf_op jit(solution)/shard_map/expert_grads/pallas_call | solution.py:767
  204.6 8.4 %out_back.1 = (f32[256,1536]{1,0:T(8,128)}, bf16[256,1536]{1,0:T(8,128)(2,1)}, bf16[256,1536]{1,0:T(8,128)(2,1)}, f32[1,1536]{1,0:T(1,128)}) custom-call(s32[4]{0:T(128)} %pad_add_fusion.ids_ref, f32[256,1536]{1,0:T(8,128)} %get-tuple-element.54.resid_ref, bf16[256,1536]{1,0:T(8,128)(2,1)} %bitcast.49, f32[1,1536]{1,0:T(1,128)} %bitcast.54, ...), custom_call_target="tpu_custom_call" | custom-call | flops 1207959552 | bytes 12582912 | tf_op jit(solution)/shard_map/out_back/pallas_call | solution.py:555
  213.0 4.6 weight_grads.3
  221.1 21.1 %attend_back.1 = (bf16[256,1536]{1,0:T(8,128)(2,1)}, bf16[5,128,1024]{2,1,0:T(8,128)(2,1)}, bf16[5,128,1024]{2,1,0:T(8,128)(2,1)}) custom-call(s32[4]{0:T(128)} %pad_add_fusion.ids_ref, bf16[256,1536]{1,0:T(8,128)(2,1)} %project.2.q_ref, s32[2048,1]{1,0:T(8,128)} %copy.43.col_ref, s32[1,2048]{1,0:T(1,128)} %row_ref.3, ...), custom_call_target="tpu_custom_call" | custom-call | flops 301989888000 | bytes 2621440 | tf_op jit(solution)/shard_map/attend_back/pallas_call | solution.py:482
  242.2 10.6 %collective-permute-done.21.refs_3_ = bf16[256,1536]{1,0:T(8,128)(2,1)} collective-permute-done((bf16[256,1536]{1,0:T(8,128)(2,1)}, bf16[256,1536]{1,0:T(8,128)(2,1)}, u32[]{:S(2)}, u32[]{:S(2)}) %collective-permute-start.21) | collective-permute-done | bytes 786464 | tf_op jit(solution)/shard_map/ppermute | solution.py:58
  252.9 4.7 weight_grads.5
  258.1 6.0 %collective-permute-done.23 = bf16[5,128,1024]{2,1,0:T(8,128)(2,1)S(1)} collective-permute-done((bf16[5,128,1024]{2,1,0:T(8,128)(2,1)}, bf16[5,128,1024]{2,1,0:T(8,128)(2,1)S(1)}, u32[]{:S(2)}, u32[]{:S(2)}) %collective-permute-start.23) | collective-permute-done | bytes 1310752 | tf_op jit(solution)/shard_map/ppermute | solution.py:53
  276.0 11.0 %collective-permute-done.24 = bf16[128,1024]{1,0:T(8,128)(2,1)S(1)} collective-permute-done((bf16[128,1024]{1,0:T(8,128)(2,1)S(1)}, bf16[128,1024]{1,0:T(8,128)(2,1)S(1)}, u32[]{:S(2)}, u32[]{:S(2)}) %collective-permute-start.24) | collective-permute-done | bytes 262176 | tf_op jit(solution)/shard_map/ppermute | solution.py:982
  292.3 22.7 %collective-permute-done.25 = bf16[128,1024]{1,0:T(8,128)(2,1)} collective-permute-done((bf16[128,1024]{1,0:T(8,128)(2,1)}, bf16[128,1024]{1,0:T(8,128)(2,1)}, u32[]{:S(2)}, u32[]{:S(2)}) %collective-permute-start.25) | collective-permute-done | bytes 262176 | tf_op jit(solution)/shard_map/ppermute | solution.py:982
  323.7 8.6 %collective-permute-done.43 = bf16[384,768]{1,0:T(8,128)(2,1)S(1)} collective-permute-done((bf16[384,768]{1,0:T(8,128)(2,1)S(1)}, bf16[384,768]{1,0:T(8,128)(2,1)S(1)}, u32[]{:S(2)}, u32[]{:S(2)}) %collective-permute-start.43) | collective-permute-done | bytes 589856 | tf_op jit(solution)/shard_map/ppermute | solution.py:73
  332.2 11.0 %collective-permute-done.42 = bf16[384,768]{1,0:T(8,128)(2,1)S(1)} collective-permute-done((bf16[384,768]{1,0:T(8,128)(2,1)S(1)}, bf16[384,768]{1,0:T(8,128)(2,1)S(1)}, u32[]{:S(2)}, u32[]{:S(2)}) %collective-permute-start.42) | collective-permute-done | bytes 589856 | tf_op jit(solution)/shard_map/ppermute | solution.py:58
  348.7 10.4 %in_back.1 = (f32[256,1536]{1,0:T(8,128)}, f32[1,1536]{1,0:T(1,128)}) custom-call(s32[4]{0:T(128)} %pad_add_fusion.ids_ref, bf16[256,1536]{1,0:T(8,128)(2,1)} %bitcast.47, f32[256,1536]{1,0:T(8,128)} %get-tuple-element.77.gres_ref, f32[1,1536]{1,0:T(1,128)} %bitcast.55, bf16[256,1536]{1,0:T(8,128)(2,1)} %get-tuple-element.81.dq_ref.refs_1_, ...), custom_call_target="tpu_custom_call" | custom-call | flops 2013265920 | bytes 12582912 | tf_op jit(solution)/shard_map/in_back/pallas_call | solution.py:593
  359.1 11.4 %collective-permute-done.31 = bf16[384,768]{1,0:T(8,128)(2,1)S(1)} collective-permute-done((bf16[384,768]{1,0:T(8,128)(2,1)S(1)}, bf16[384,768]{1,0:T(8,128)(2,1)S(1)}, u32[]{:S(2)}, u32[]{:S(2)}) %collective-permute-start.31) | collective-permute-done | bytes 589856 | tf_op jit(solution)/shard_map/ppermute | solution.py:111
  376.5 5.6 %collective-permute-start.44 = (bf16[384,768]{1,0:T(8,128)(2,1)S(1)}, bf16[384,768]{1,0:T(8,128)(2,1)S(1)}, u32[]{:S(2)}, u32[]{:S(2)}) collective-permute-start(bf16[384,768]{1,0:T(8,128)(2,1)S(1)} %copy-done.3), channel_id=1, source_target_pairs={{0,8},{24,16},{1,9},{25,17},{2,10},{26,18},{3,11},{27,19},{4,12},{... | collective-permute-start | bytes 1769480 | tf_op jit(solution)/shard_map/ppermute | solution.py:111
  389.7 18.5 %collective-permute-done.44 = bf16[384,768]{1,0:T(8,128)(2,1)S(1)} collective-permute-done((bf16[384,768]{1,0:T(8,128)(2,1)S(1)}, bf16[384,768]{1,0:T(8,128)(2,1)S(1)}, u32[]{:S(2)}, u32[]{:S(2)}) %collective-permute-start.44) | collective-permute-done | bytes 589856 | tf_op jit(solution)/shard_map/ppermute | solution.py:111
  411.7 16.0 %collective-permute-start.36 = (bf16[384,640]{1,0:T(8,128)(2,1)S(1)}, bf16[384,640]{1,0:T(8,128)(2,1)S(1)}, u32[]{:S(2)}, u32[]{:S(2)}) collective-permute-start(bf16[384,640]{1,0:T(8,128)(2,1)S(1)} %add_convert_fusion.18), channel_id=1, source_target_pairs={{0,8},{24,16},{1,9},{25,17},{2,10},{26,18},{3,11},{27,19},{4,12},{... | collective-permute-start | bytes 1474568 | tf_op jit(solution)/shard_map/ppermute | solution.py:111
  427.7 19.9 %collective-permute-done.49 = bf16[384,768]{1,0:T(8,128)(2,1)} collective-permute-done((bf16[384,768]{1,0:T(8,128)(2,1)S(1)}, bf16[384,768]{1,0:T(8,128)(2,1)}, u32[]{:S(2)}, u32[]{:S(2)}) %collective-permute-start.49) | collective-permute-done | bytes 589856 | tf_op jit(solution)/shard_map/ppermute | solution.py:118
  457.4 13.6 %collective-permute-done.46 = bf16[384,768]{1,0:T(8,128)(2,1)S(1)} collective-permute-done((bf16[384,768]{1,0:T(8,128)(2,1)S(1)}, bf16[384,768]{1,0:T(8,128)(2,1)S(1)}, u32[]{:S(2)}, u32[]{:S(2)}) %collective-permute-start.46) | collective-permute-done | bytes 589856 | tf_op jit(solution)/shard_map/ppermute | solution.py:118
  472.8 12.0 %collective-permute-done.38 = bf16[384,640]{1,0:T(8,128)(2,1)S(1)} collective-permute-done((bf16[384,640]{1,0:T(8,128)(2,1)S(1)}, bf16[384,640]{1,0:T(8,128)(2,1)S(1)}, u32[]{:S(2)}, u32[]{:S(2)}) %collective-permute-start.38) | collective-permute-done | bytes 491552 | tf_op jit(solution)/shard_map/ppermute | solution.py:118
  489.9 10.5 %spread_grads.1 = (f32[4,1536,256]{2,1,0:T(8,128)}, f32[4,1536,256]{2,1,0:T(8,128)}, f32[4,256,1536]{2,1,0:T(8,128)}) custom-call(bf16[6144,768]{1,0:T(8,128)(2,1)} %all-gather.7.cloned.1.call-done.in_ref), custom_call_target="tpu_custom_call" | custom-call | bytes 28311552 | tf_op jit(solution)/shard_map/spread_grads/pallas_call | solution.py:788
  (241 shorter events, 117.5 us)
Async XLA Ops:
  7.2 74.6 %all-gather.5.cloned.1.call-start = ((), (), s32[]{:S(2)}) async-start(), calls=%async_computation.1 | async-start | bytes 10616832 | tf_op jit(solution)/shard_map/all_gather | solution.py:197
  9.7 134.5 %all-gather.9.cloned.1.call-start = ((), (), s32[]{:S(2)}) async-start(), calls=%async_computation.4 | async-start | bytes 3932160 | tf_op jit(solution)/shard_map/all_gather | solution.py:898
  10.7 33.0 %collective-permute-start.2 = (f32[14,128]{1,0:T(8,128)S(1)}, f32[14,128]{1,0:T(8,128)S(1)}, u32[]{:S(2)}, u32[]{:S(2)}) collective-permute-start(f32[14,128]{1,0:T(8,128)S(1)} %maximum_bitcast_fusion), channel_id=1, source_target_pairs={{0,3},{1,2},{2,1},{3,0},{4,7},{5,6},{6,5},{7,4},{8,11},{9,10},{10,... | collective-permute-start | bytes 21512 | tf_op jit(solution)/shard_map/ppermute | solution.py:73
  14.6 29.0 %collective-permute-start.1 = (f32[14,128]{1,0:T(8,128)S(1)}, f32[14,128]{1,0:T(8,128)S(1)}, u32[]{:S(2)}, u32[]{:S(2)}) collective-permute-start(f32[14,128]{1,0:T(8,128)S(1)} %maximum_bitcast_fusion), channel_id=1, source_target_pairs={{0,2},{2,0},{1,3},{3,1},{4,6},{6,4},{5,7},{7,5},{8,10},{10,8},{9,1... | collective-permute-start | bytes 21512 | tf_op jit(solution)/shard_map/ppermute | solution.py:58
  15.2 28.6 %collective-permute-start = (f32[14,128]{1,0:T(8,128)S(1)}, f32[14,128]{1,0:T(8,128)S(1)}, u32[]{:S(2)}, u32[]{:S(2)}) collective-permute-start(f32[14,128]{1,0:T(8,128)S(1)} %maximum_bitcast_fusion), channel_id=1, source_target_pairs={{0,1},{1,0},{2,3},{3,2},{4,5},{5,4},{6,7},{7,6},{8,9},{9,8},{10,11... | collective-permute-start | bytes 21512 | tf_op jit(solution)/shard_map/ppermute | solution.py:53
  18.8 326.8 %reduce-scatter.2.cloned.1.call-start = ((), (), s32[]{:S(2)}) async-start(), calls=%async_computation.2 | async-start | bytes 10616832 | tf_op jit(solution)/shard_map/reduce_scatter | solution.py:958
  112.9 29.1 %collective-permute-start.13 = (bf16[256,1536]{1,0:T(8,128)(2,1)}, bf16[256,1536]{1,0:T(8,128)(2,1)S(1)}, u32[]{:S(2)}, u32[]{:S(2)}) collective-permute-start(bf16[256,1536]{1,0:T(8,128)(2,1)} %get-tuple-element.55.refs_0_), channel_id=1, source_target_pairs={{0,1},{1,0},{2,3},{3,2},{4,5},{5,4},{6,7},{7,6},{8,9},{9,8},{10,11... | collective-permute-start | bytes 2359304 | tf_op jit(solution)/shard_map/ppermute | solution.py:53
  114.6 29.0 %collective-permute-start.14 = (bf16[256,1536]{1,0:T(8,128)(2,1)}, bf16[256,1536]{1,0:T(8,128)(2,1)S(1)}, u32[]{:S(2)}, u32[]{:S(2)}) collective-permute-start(bf16[256,1536]{1,0:T(8,128)(2,1)} %get-tuple-element.55.refs_0_), channel_id=1, source_target_pairs={{2,0},{0,2},{3,1},{1,3},{6,4},{4,6},{7,5},{5,7},{10,8},{8,10},{11,... | collective-permute-start | bytes 2359304 | tf_op jit(solution)/shard_map/ppermute | solution.py:63
  142.0 26.5 %collective-permute-start.15 = (bf16[128,1536]{1,0:T(8,128)(2,1)S(1)}, bf16[128,1536]{1,0:T(8,128)(2,1)S(1)}, u32[]{:S(2)}, u32[]{:S(2)}) collective-permute-start(bf16[128,1536]{1,0:T(8,128)(2,1)S(1)} %slice.86), channel_id=1, source_target_pairs={{2,0},{0,2},{3,1},{1,3},{6,4},{4,6},{7,5},{5,7},{10,8},{8,10},{11,... | collective-permute-start | bytes 1179656 | tf_op jit(solution)/shard_map/ppermute | solution.py:63
  143.6 24.9 %collective-permute-start.16 = (bf16[128,1536]{1,0:T(8,128)(2,1)S(1)}, bf16[128,1536]{1,0:T(8,128)(2,1)}, u32[]{:S(2)}, u32[]{:S(2)}) collective-permute-start(bf16[128,1536]{1,0:T(8,128)(2,1)S(1)} %slice.87), channel_id=1, source_target_pairs={{0,1},{1,0},{2,3},{3,2},{4,5},{5,4},{6,7},{7,6},{8,9},{9,8},{10,11... | collective-permute-start | bytes 1179656 | tf_op jit(solution)/shard_map/ppermute | solution.py:53
  166.7 34.6 %collective-permute-start.17 = (bf16[256,1536]{1,0:T(8,128)(2,1)}, bf16[256,1536]{1,0:T(8,128)(2,1)S(1)}, u32[]{:S(2)}, u32[]{:S(2)}) collective-permute-start(bf16[256,1536]{1,0:T(8,128)(2,1)} %get-tuple-element.63), channel_id=1, source_target_pairs={{0,1},{1,0},{2,3},{3,2},{4,5},{5,4},{6,7},{7,6},{8,9},{9,8},{10,11... | collective-permute-start | bytes 2359304 | tf_op jit(solution)/shard_map/ppermute | solution.py:53
  168.0 35.5 %collective-permute-start.18 = (bf16[256,1536]{1,0:T(8,128)(2,1)}, bf16[256,1536]{1,0:T(8,128)(2,1)S(1)}, u32[]{:S(2)}, u32[]{:S(2)}) collective-permute-start(bf16[256,1536]{1,0:T(8,128)(2,1)} %get-tuple-element.64), channel_id=1, source_target_pairs={{0,2},{2,0},{1,3},{3,1},{4,6},{6,4},{5,7},{7,5},{8,10},{10,8},{9,1... | collective-permute-start | bytes 2359304 | tf_op jit(solution)/shard_map/ppermute | solution.py:58
  201.0 288.9 %all-gather.7.cloned.1.call-start = ((), (), s32[]{:S(2)}) async-start(), calls=%async_computation.3 | async-start | bytes 10616832 | tf_op jit(solution)/shard_map/all_gather | solution.py:990
  217.6 24.6 %collective-permute-start.22 = (bf16[256,1536]{1,0:T(8,128)(2,1)}, bf16[256,1536]{1,0:T(8,128)(2,1)}, u32[]{:S(2)}, u32[]{:S(2)}) collective-permute-start(bf16[256,1536]{1,0:T(8,128)(2,1)} %get-tuple-element.76), channel_id=1, source_target_pairs={{0,3},{1,2},{2,1},{3,0},{4,7},{5,6},{6,5},{7,4},{8,11},{9,10},{10,... | collective-permute-start | bytes 2359304 | tf_op jit(solution)/shard_map/ppermute | solution.py:73
  218.1 34.8 %collective-permute-start.21 = (bf16[256,1536]{1,0:T(8,128)(2,1)}, bf16[256,1536]{1,0:T(8,128)(2,1)}, u32[]{:S(2)}, u32[]{:S(2)}) collective-permute-start(bf16[256,1536]{1,0:T(8,128)(2,1)} %get-tuple-element.75), channel_id=1, source_target_pairs={{0,2},{2,0},{1,3},{3,1},{4,6},{6,4},{5,7},{7,5},{8,10},{10,8},{9,1... | collective-permute-start | bytes 2359304 | tf_op jit(solution)/shard_map/ppermute | solution.py:58
  220.1 32.9 %collective-permute-start.20 = (bf16[256,1536]{1,0:T(8,128)(2,1)}, bf16[256,1536]{1,0:T(8,128)(2,1)}, u32[]{:S(2)}, u32[]{:S(2)}) collective-permute-start(bf16[256,1536]{1,0:T(8,128)(2,1)} %get-tuple-element.74), channel_id=1, source_target_pairs={{0,1},{1,0},{2,3},{3,2},{4,5},{5,4},{6,7},{7,6},{8,9},{9,8},{10,11... | collective-permute-start | bytes 2359304 | tf_op jit(solution)/shard_map/ppermute | solution.py:53
  221.1 46.1 %collective-permute-start.27 = (bf16[1536,768]{1,0:T(8,128)(2,1)}, bf16[1536,768]{1,0:T(8,128)(2,1)}, u32[]{:S(2)}, u32[]{:S(2)}) collective-permute-start(bf16[1536,768]{1,0:T(8,128)(2,1)} %get-tuple-element.87), channel_id=1, source_target_pairs={{0,4},{4,0},{1,5},{5,1},{2,6},{6,2},{3,7},{7,3},{8,12},{12,8},{9,1... | collective-permute-start | bytes 7077896 | tf_op jit(solution)/shard_map/ppermute | solution.py:53
  257.6 30.5 %collective-permute-start.40 = (bf16[1536,768]{1,0:T(8,128)(2,1)}, bf16[1536,768]{1,0:T(8,128)(2,1)}, u32[]{:S(2)}, u32[]{:S(2)}) collective-permute-start(bf16[1536,768]{1,0:T(8,128)(2,1)} %get-tuple-element.91), channel_id=1, source_target_pairs={{0,4},{4,0},{1,5},{5,1},{2,6},{6,2},{3,7},{7,3},{8,12},{12,8},{9,1... | collective-permute-start | bytes 7077896 | tf_op jit(solution)/shard_map/ppermute | solution.py:53
  269.2 48.2 %collective-permute-start.30 = (bf16[384,768]{1,0:T(8,128)(2,1)S(1)}, bf16[384,768]{1,0:T(8,128)(2,1)}, u32[]{:S(2)}, u32[]{:S(2)}) collective-permute-start(bf16[384,768]{1,0:T(8,128)(2,1)S(1)} %get-tuple-element.103), channel_id=1, source_target_pairs={{0,3},{1,2},{2,1},{3,0},{4,7},{5,6},{6,5},{7,4},{8,11},{9,10},{10,... | collective-permute-start | bytes 1769480 | tf_op jit(solution)/shard_map/ppermute | solution.py:73
  274.7 40.4 %collective-permute-start.25 = (bf16[128,1024]{1,0:T(8,128)(2,1)}, bf16[128,1024]{1,0:T(8,128)(2,1)}, u32[]{:S(2)}, u32[]{:S(2)}) collective-permute-start(bf16[128,1024]{1,0:T(8,128)(2,1)} %get-tuple-element.111), channel_id=1, source_target_pairs={{16,0},{24,8},{0,16},{8,24},{17,1},{25,9},{1,17},{9,25},{18,2},{26... | collective-permute-start | bytes 786440 | tf_op jit(solution)/shard_map/ppermute | solution.py:982
  274.7 42.0 %collective-permute-start.26 = (bf16[128,1024]{1,0:T(8,128)(2,1)S(1)}, bf16[128,1024]{1,0:T(8,128)(2,1)}, u32[]{:S(2)}, u32[]{:S(2)}) collective-permute-start(bf16[128,1024]{1,0:T(8,128)(2,1)S(1)} %get-tuple-element.110), channel_id=1, source_target_pairs={{24,0},{0,8},{8,16},{16,24},{25,1},{1,9},{9,17},{17,25},{26,2},{2,... | collective-permute-start | bytes 786440 | tf_op jit(solution)/shard_map/ppermute | solution.py:982
  287.0 33.7 %collective-permute-start.29 = (bf16[384,768]{1,0:T(8,128)(2,1)S(1)}, bf16[384,768]{1,0:T(8,128)(2,1)}, u32[]{:S(2)}, u32[]{:S(2)}) collective-permute-start(bf16[384,768]{1,0:T(8,128)(2,1)S(1)} %get-tuple-element.104), channel_id=1, source_target_pairs={{0,2},{2,0},{1,3},{3,1},{4,6},{6,4},{5,7},{7,5},{8,10},{10,8},{9,1... | collective-permute-start | bytes 1769480 | tf_op jit(solution)/shard_map/ppermute | solution.py:58
  288.1 32.7 %collective-permute-start.28 = (bf16[384,768]{1,0:T(8,128)(2,1)S(1)}, bf16[384,768]{1,0:T(8,128)(2,1)}, u32[]{:S(2)}, u32[]{:S(2)}) collective-permute-start(bf16[384,768]{1,0:T(8,128)(2,1)S(1)} %get-tuple-element.102), channel_id=1, source_target_pairs={{0,1},{1,0},{2,3},{3,2},{4,5},{5,4},{6,7},{7,6},{8,9},{9,8},{10,11... | collective-permute-start | bytes 1769480 | tf_op jit(solution)/shard_map/ppermute | solution.py:53
  316.6 26.6 %collective-permute-start.42 = (bf16[384,768]{1,0:T(8,128)(2,1)S(1)}, bf16[384,768]{1,0:T(8,128)(2,1)S(1)}, u32[]{:S(2)}, u32[]{:S(2)}) collective-permute-start(bf16[384,768]{1,0:T(8,128)(2,1)S(1)} %get-tuple-element.101), channel_id=1, source_target_pairs={{0,2},{2,0},{1,3},{3,1},{4,6},{6,4},{5,7},{7,5},{8,10},{10,8},{9,1... | collective-permute-start | bytes 1769480 | tf_op jit(solution)/shard_map/ppermute | solution.py:58
  317.4 25.8 %collective-permute-start.41 = (bf16[384,768]{1,0:T(8,128)(2,1)S(1)}, bf16[384,768]{1,0:T(8,128)(2,1)S(1)}, u32[]{:S(2)}, u32[]{:S(2)}) collective-permute-start(bf16[384,768]{1,0:T(8,128)(2,1)S(1)} %get-tuple-element.99), channel_id=1, source_target_pairs={{0,1},{1,0},{2,3},{3,2},{4,5},{5,4},{6,7},{7,6},{8,9},{9,8},{10,11... | collective-permute-start | bytes 1769480 | tf_op jit(solution)/shard_map/ppermute | solution.py:53
  376.5 31.7 %collective-permute-start.44 = (bf16[384,768]{1,0:T(8,128)(2,1)S(1)}, bf16[384,768]{1,0:T(8,128)(2,1)S(1)}, u32[]{:S(2)}, u32[]{:S(2)}) collective-permute-start(bf16[384,768]{1,0:T(8,128)(2,1)S(1)} %copy-done.3), channel_id=1, source_target_pairs={{0,8},{24,16},{1,9},{25,17},{2,10},{26,18},{3,11},{27,19},{4,12},{... | collective-permute-start | bytes 1769480 | tf_op jit(solution)/shard_map/ppermute | solution.py:111
  384.8 25.1 %collective-permute-start.35 = (bf16[384,640]{1,0:T(8,128)(2,1)}, bf16[384,640]{1,0:T(8,128)(2,1)}, u32[]{:S(2)}, u32[]{:S(2)}) collective-permute-start(bf16[384,640]{1,0:T(8,128)(2,1)} %get-tuple-element.106), channel_id=1, source_target_pairs={{0,3},{1,2},{2,1},{3,0},{4,7},{5,6},{6,5},{7,4},{8,11},{9,10},{10,... | collective-permute-start | bytes 1474568 | tf_op jit(solution)/shard_map/ppermute | solution.py:73
  385.3 24.5 %collective-permute-start.34 = (bf16[384,640]{1,0:T(8,128)(2,1)}, bf16[384,640]{1,0:T(8,128)(2,1)}, u32[]{:S(2)}, u32[]{:S(2)}) collective-permute-start(bf16[384,640]{1,0:T(8,128)(2,1)} %get-tuple-element.107), channel_id=1, source_target_pairs={{0,2},{2,0},{1,3},{3,1},{4,6},{6,4},{5,7},{7,5},{8,10},{10,8},{9,1... | collective-permute-start | bytes 1474568 | tf_op jit(solution)/shard_map/ppermute | solution.py:58
  388.4 59.2 %collective-permute-start.49 = (bf16[384,768]{1,0:T(8,128)(2,1)S(1)}, bf16[384,768]{1,0:T(8,128)(2,1)}, u32[]{:S(2)}, u32[]{:S(2)}) collective-permute-start(bf16[384,768]{1,0:T(8,128)(2,1)S(1)} %add_convert_fusion.2), channel_id=1, source_target_pairs={{8,0},{16,24},{9,1},{17,25},{10,2},{18,26},{11,3},{19,27},{12,4},{... | collective-permute-start | bytes 1769480 | tf_op jit(solution)/shard_map/ppermute | solution.py:118
  408.4 40.4 %collective-permute-start.45 = (bf16[384,768]{1,0:T(8,128)(2,1)S(1)}, bf16[384,768]{1,0:T(8,128)(2,1)}, u32[]{:S(2)}, u32[]{:S(2)}) collective-permute-start(bf16[384,768]{1,0:T(8,128)(2,1)S(1)} %add_convert_fusion.4), channel_id=1, source_target_pairs={{8,16},{16,8},{9,17},{17,9},{10,18},{18,10},{11,19},{19,11},{12,20... | collective-permute-start | bytes 1769480 | tf_op jit(solution)/shard_map/ppermute | solution.py:117
  411.7 39.8 %collective-permute-start.36 = (bf16[384,640]{1,0:T(8,128)(2,1)S(1)}, bf16[384,640]{1,0:T(8,128)(2,1)S(1)}, u32[]{:S(2)}, u32[]{:S(2)}) collective-permute-start(bf16[384,640]{1,0:T(8,128)(2,1)S(1)} %add_convert_fusion.18), channel_id=1, source_target_pairs={{0,8},{24,16},{1,9},{25,17},{2,10},{26,18},{3,11},{27,19},{4,12},{... | collective-permute-start | bytes 1474568 | tf_op jit(solution)/shard_map/ppermute | solution.py:111
  456.1 28.7 %collective-permute-start.38 = (bf16[384,640]{1,0:T(8,128)(2,1)S(1)}, bf16[384,640]{1,0:T(8,128)(2,1)S(1)}, u32[]{:S(2)}, u32[]{:S(2)}) collective-permute-start(bf16[384,640]{1,0:T(8,128)(2,1)S(1)} %add_convert_fusion.16), channel_id=1, source_target_pairs={{8,0},{16,24},{9,1},{17,25},{10,2},{18,26},{11,3},{19,27},{12,4},{... | collective-permute-start | bytes 1474568 | tf_op jit(solution)/shard_map/ppermute | solution.py:118
  (55 other events, 474.5 us)
Sparse Core Ops, SparseCore 0:
  10.5 68.7 all-gather.4
  81.1 53.5 all-gather.8
  201.2 115.2 reduce-scatter.1
  345.8 114.5 all-gather.6

commit v4 on v3

--- a/solution.py
+++ b/solution.py
@@ -985,19 +985,20 @@
     dkv = jnp.concatenate([low, high], axis=0).astype(BF)
     o_blocks, q_blocks = plane_blocks(*o_grads, y, x), plane_blocks(*q_grads, y, x)
     o_total, q_total = plane_total(o_blocks), plane_total(q_blocks)
-    (expert_shard,) = tie([expert_shard], o_total, q_total, dkv)
+    grad_tokens, ggain_a = in_back(
+        tokens, gres, gain_a, dq, dkv, weight_q, weight_kv, ids, ny, shard
+    )
+    (expert_shard,) = tie([expert_shard], o_total, grad_tokens)
     expert_totals = spread_grads(
         lax.all_gather(expert_shard, ("z", "core"), axis=0, tiled=True), experts
     )
-    grad_tokens, ggain_a = in_back(
-        tokens, gres, gain_a, dq, dkv, weight_q, weight_kv, ids, ny, shard
-    )
+    kv_grads = weight_grads(ids, [(normed, dkv)], (ggain_a, ggain_f))
+    kv_blocks = plane_blocks(*kv_grads, y, x)
+    o_total, q_total = tie([o_total, q_total], *kv_blocks.values())
     o_first, q_first = z_first(o_total), z_first(q_total)
-    kv_grads = weight_grads(ids, [(normed, dkv)], (ggain_a, ggain_f), (o_first,))
-    kv_blocks = plane_blocks(*kv_grads, y, x)
+    kv_first = z_first(plane_total(kv_blocks))
     grad_wo = jnp.concatenate(whole_grad(z_rest(o_first, z), core), axis=1)
     grad_wq = jnp.concatenate(whole_grad(z_rest(q_first, z), core), axis=1)
-    kv_first = z_first(plane_total(kv_blocks))
     grad_wk, grad_wv = whole_grad(z_rest(kv_first, z), core)
     ggain_a, ggain_f = grad_wk[:, -128], grad_wk[:, -127]
     grad_wk, grad_wv = grad_wk[:, :-128], grad_wv[:, :-128]

time: 516 us -> 510 us (0.988)
  other arithmetic: 36.1 us -> 25.5 us
  waiting for transfers between devices: 200 us -> 206 us
    ppermute x3, waiting for transfers between devices: 45.5 us -> 27.5 us  [z_rest(): outer = lax.ppermute(whole, 'z', [(1, 0), (2, 3)])]
    ppermute x6, waiting for transfers between devices: 8.59 us -> 25.3 us  [to_plane(): return lax.ppermute(v, ('y', 'x'), perm)]
    reduce_scatter x1, waiting for transfers between devices: 0.01 us -> 9.2 us  [body(): lax.psum_scatter(expert_parts, ('z', 'core'), scatter_dimension=0, tiled=...]
    ppermute x3, starting transfers between devices: 4.14 us -> 13.2 us  [body(): lax.ppermute(piece, 'z', [((i + d) % nz, i) for i in range(nz)]).astype(F32)]
    ppermute x6, waiting for transfers between devices: 23.8 us -> 31.8 us  [to_y(): return lax.ppermute(v, 'y', [(i, (i + d) % n) for i in range(n)])]
    convert_element_type x13, other arithmetic: 19 us -> 11.3 us  [add_low(): return total.astype(terms[0].dtype)]
    ppermute x3, starting transfers between devices: 22.9 us -> 15.5 us  [z_first(): return add_low(v, lax.ppermute(v, 'z', perm))]
    ppermute x3, waiting for transfers between devices: 33.8 us -> 28.3 us  [body(): lax.ppermute(piece, 'z', [((i + d) % nz, i) for i in range(nz)]).astype(F32)]
  transfers between devices with their start and end apart: 55 -> 55, of which waited for: 19 -> 29; matrix products, arithmetic and copies ran while one was open for 9% -> 7% of each run, Pallas kernels for 30% -> 30%
where the time goes in v4:
time: 510 us; the launch traced here: 501 us
  waiting for transfers between devices  206 us (40%)
  Pallas kernels  163 us (32%)
  starting transfers between devices  75 us (15%)
  other arithmetic  25.5 us (5%)
  local copies, waits for them, and re-layouts  17.4 us (3%)
  between operations  14.8 us (3%)
    pallas_call x3, Pallas kernels, expert_block(): pl.pallas_call(kernel, grid_spec=pltpu.PrefetchScalarGridSpec(num_scalar_...  48.3 us
    ppermute x6, waiting for transfers between devices, to_y(): return lax.ppermute(v, 'y', [(i, (i + d) % n) for i in range(n)])  31.8 us
    ppermute x3, waiting for transfers between devices, z_first(): return add_low(v, lax.ppermute(v, 'z', perm))  28.4 us
    ppermute x3, waiting for transfers between devices, body(): lax.ppermute(piece, 'z', [((i + d) % nz, i) for i in range(nz)]).astype(F32)  28.3 us
    ppermute x3, waiting for transfers between devices, z_rest(): outer = lax.ppermute(whole, 'z', [(1, 0), (2, 3)])  27.5 us
    ppermute x20, waiting for transfers between devices, swap(): return lax.ppermute(v, axis, [(0, 1), (1, 0)])  25.9 us
    ppermute x6, waiting for transfers between devices, to_plane(): return lax.ppermute(v, ('y', 'x'), perm)  25.3 us
    ppermute x3, waiting for transfers between devices, body(): lax.ppermute(piece, 'z', [(i, (i + d) % nz) for i in range(nz)])  21.7 us
  transfers between devices with their start and end apart: 55, of which 29 were waited for; matrix products, arithmetic and copies ran while one was open for 7% of the time, Pallas kernels for 30%

profile of v4, /device:TPU:0, one launch (start us, length us, event | category | flops | bytes accessed | tf_op | source)
XLA Modules:
  0.0 501.5 jit_solution(1843277041315856985)
XLA Ops:
  19.2 11.4 %collective-permute-done.3 = bf16[384,512]{1,0:T(8,128)(2,1)S(1)} collective-permute-done((bf16[384,512]{1,0:T(8,128)(2,1)S(1)}, bf16[384,512]{1,0:T(8,128)(2,1)S(1)}, u32[]{:S(2)}, u32[]{:S(2)}) %collective-permute-start.3) | collective-permute-done | bytes 393248 | tf_op jit(solution)/shard_map/ppermute | solution.py:53
  34.9 5.8 %collective-permute-done.5 = bf16[192,512]{1,0:T(8,128)(2,1)S(1)} collective-permute-done((bf16[192,512]{1,0:T(8,128)(2,1)S(1)}, bf16[192,512]{1,0:T(8,128)(2,1)S(1)}, u32[]{:S(2)}, u32[]{:S(2)}) %collective-permute-start.5) | collective-permute-done | bytes 196640 | tf_op jit(solution)/shard_map/ppermute | solution.py:63
  57.5 5.7 %collective-permute-done.11 = bf16[128,1024]{1,0:T(8,128)(2,1)S(1)} collective-permute-done((bf16[128,1024]{1,0:T(8,128)(2,1)S(1)}, bf16[128,1024]{1,0:T(8,128)(2,1)S(1)}, u32[]{:S(2)}, u32[]{:S(2)}) %collective-permute-start.11) | collective-permute-done | bytes 262176 | tf_op jit(solution)/shard_map/ppermute | solution.py:908
  63.2 15.9 %collective-permute-done.10 = bf16[128,1024]{1,0:T(8,128)(2,1)S(1)} collective-permute-done((bf16[128,1024]{1,0:T(8,128)(2,1)S(1)}, bf16[128,1024]{1,0:T(8,128)(2,1)S(1)}, u32[]{:S(2)}, u32[]{:S(2)}) %collective-permute-start.10) | collective-permute-done | bytes 262176 | tf_op jit(solution)/shard_map/ppermute | solution.py:908
  81.8 5.8 %project.2.q_ref = bf16[256,1536]{1,0:T(8,128)(2,1)} custom-call(s32[4]{0:T(128)} %pad_add_fusion.ids_ref, bf16[256,1536]{1,0:T(8,128)(2,1)} %fusion.2.lhs_ref.refs_0_, bf16[3072,1536]{1,0:T(8,128)(2,1)} %all-gather.5.cloned.1.call-done.refs_0_.refs_4_), custom_call_target="tpu_custom_call" | custom-call | flops 1207959552 | bytes 5505024 | tf_op jit(solution)/shard_map/project/pallas_call | solution.py:219
  89.4 16.9 %attend.1 = (bf16[256,1536]{1,0:T(8,128)(2,1)}, f32[8,768]{1,0:T(8,128)}) custom-call(s32[4]{0:T(128)} %pad_add_fusion.ids_ref, bf16[256,1536]{1,0:T(8,128)(2,1)} %project.2.q_ref, s32[2048,1]{1,0:T(8,128)} %copy.45.col_ref, s32[1,2048]{1,0:T(1,128)} %row_ref.3, bf16[256,1024]{1,0:T(8,128)(2,1)} %project.3.refs_0_, bf16[256,1024]{1,0:T(8,128)(2,1)} %copy-done.35, ...), custom_call_target="tpu_custom_call" | custom-call | flops 8053063680 | bytes 2621440 | tf_op jit(solution)/shard_map/attend/pallas_call | solution.py:396
  106.3 6.8 %out_project.1 = (f32[256,1536]{1,0:T(8,128)}, bf16[256,1536]{1,0:T(8,128)(2,1)}) custom-call(s32[4]{0:T(128)} %pad_add_fusion.ids_ref, bf16[256,1536]{1,0:T(8,128)(2,1)} %bitcast.46, bf16[256,1536]{1,0:T(8,128)(2,1)} %get-tuple-element.55.att_ref.refs_0_, f32[1,1536]{1,0:T(1,128)} %bitcast.54, bf16[3072,1536]{1,0:T(8,128)(2,1)} %all-gather.5.cloned.1.call-done.refs_0_.refs_4_), custom_call_target="tpu_custom_call" | custom-call | flops 1207959552 | bytes 8650752 | tf_op jit(solution)/shard_map/out_project/pallas_call | solution.py:516
  119.3 13.4 %experts.3 = (bf16[256,1024]{1,0:T(8,128)(2,1)}, bf16[256,1024]{1,0:T(8,128)(2,1)}, bf16[256,1024]{1,0:T(8,128)(2,1)}, f32[256,1536]{1,0:T(8,128)}, f32[256,1536]{1,0:T(8,128)}) custom-call(s32[1]{0:T(128)} %constant.65.clone.1.id_ref, bf16[256,1536]{1,0:T(8,128)(2,1)} %get-tuple-element.57.refs_0_, bf16[256,1536]{1,0:T(8,128)(2,1)} %bitcast.48, ...), custom_call_target="tpu_custom_call" | custom-call | flops 4831838208 | bytes 13369344 | tf_op jit(solution)/shard_map/experts/pallas_call | solution.py:664
  132.7 9.3 %collective-permute-done.13.refs_0_.refs_1_ = bf16[256,1536]{1,0:T(8,128)(2,1)S(1)} collective-permute-done((bf16[256,1536]{1,0:T(8,128)(2,1)}, bf16[256,1536]{1,0:T(8,128)(2,1)S(1)}, u32[]{:S(2)}, u32[]{:S(2)}) %collective-permute-start.13) | collective-permute-done | bytes 786464 | tf_op jit(solution)/shard_map/ppermute | solution.py:53
  144.4 22.3 %experts.4 = (bf16[512,1024]{1,0:T(8,128)(2,1)}, bf16[512,1024]{1,0:T(8,128)(2,1)}, bf16[512,1024]{1,0:T(8,128)(2,1)}, bf16[256,1536]{1,0:T(8,128)(2,1)}, bf16[2...) custom-call(s32[2]{0:T(128)} %pad_add_fusion.1.id_ref, bf16[256,1536]{1,0:T(8,128)(2,1)} %copy-done.26, ...), custom_call_target="tpu_custom_call" | custom-call | flops 9663676416 | bytes 17301504 | tf_op jit(solution)/shard_map/experts/pallas_call | solution.py:664
  169.5 12.6 %experts.5 = (bf16[256,1024]{1,0:T(8,128)(2,1)}, bf16[256,1024]{1,0:T(8,128)(2,1)}, bf16[256,1024]{1,0:T(8,128)(2,1)}, bf16[256,1536]{1,0:T(8,128)(2,1)}, bf16[256,1536]{1,0:T(8,128)(2,1)}) custom-call(s32[1]{0:T(128)} %bitcast.17.id_ref, bf16[128,1536]{1,0:T(8,128)(2,1)} %copy-done.36, bf16[128,1536]{1,0:T(8,128)(2,1)} %copy-done.37, ...), custom_call_target="tpu_custom_call" | custom-call | flops 4831838208 | bytes 13369344 | tf_op jit(solution)/shard_map/experts/pallas_call | solution.py:664
  183.9 17.3 %expert_grads.1.refs_5_ = bf16[6144,768]{1,0:T(8,128)(2,1)} custom-call(s32[4]{0:T(128)} %pad_add_fusion.2.id_ref, bf16[256,1536]{1,0:T(8,128)(2,1)} %get-tuple-element.57.refs_0_, bf16[256,1536]{1,0:T(8,128)(2,1)} %copy-done.26, bf16[256,1536]{1,0:T(8,128)(2,1)} %copy-done.27, bf16[128,1536]{1,0:T(8,128)(2,1)} %copy-done.36, bf16[128,1536]{1,0:T(8,128)(2,1)} %copy-done.37, ...), custom_call_target="tpu_custom_call" | custom-call | flops 9663676416 | bytes 15728640 | tf_op jit(solution)/shard_map/expert_grads/pallas_call | solution.py:767
  204.7 8.6 %out_back.1 = (f32[256,1536]{1,0:T(8,128)}, bf16[256,1536]{1,0:T(8,128)(2,1)}, bf16[256,1536]{1,0:T(8,128)(2,1)}, f32[1,1536]{1,0:T(1,128)}) custom-call(s32[4]{0:T(128)} %pad_add_fusion.ids_ref, f32[256,1536]{1,0:T(8,128)} %get-tuple-element.56.resid_ref, bf16[256,1536]{1,0:T(8,128)(2,1)} %bitcast.49, f32[1,1536]{1,0:T(1,128)} %bitcast.55, ...), custom_call_target="tpu_custom_call" | custom-call | flops 1207959552 | bytes 12582912 | tf_op jit(solution)/shard_map/out_back/pallas_call | solution.py:555
  217.9 20.9 %attend_back.1 = (bf16[256,1536]{1,0:T(8,128)(2,1)}, bf16[5,128,1024]{2,1,0:T(8,128)(2,1)}, bf16[5,128,1024]{2,1,0:T(8,128)(2,1)}) custom-call(s32[4]{0:T(128)} %pad_add_fusion.ids_ref, bf16[256,1536]{1,0:T(8,128)(2,1)} %project.2.q_ref, s32[2048,1]{1,0:T(8,128)} %copy.45.col_ref, s32[1,2048]{1,0:T(1,128)} %row_ref.3, ...), custom_call_target="tpu_custom_call" | custom-call | flops 301989888000 | bytes 2621440 | tf_op jit(solution)/shard_map/attend_back/pallas_call | solution.py:482
  244.9 12.6 %collective-permute-start.24 = (bf16[128,1024]{1,0:T(8,128)(2,1)}, bf16[128,1024]{1,0:T(8,128)(2,1)}, u32[]{:S(2)}, u32[]{:S(2)}) collective-permute-start(bf16[128,1024]{1,0:T(8,128)(2,1)} %get-tuple-element.118), channel_id=1, source_target_pairs={{8,0},{16,8},{24,16},{0,24},{9,1},{17,9},{25,17},{1,25},{10,2},{18... | collective-permute-start | bytes 786440 | tf_op jit(solution)/shard_map/ppermute | solution.py:982
  263.1 7.0 %collective-permute-done.24 = bf16[128,1024]{1,0:T(8,128)(2,1)} collective-permute-done((bf16[128,1024]{1,0:T(8,128)(2,1)}, bf16[128,1024]{1,0:T(8,128)(2,1)}, u32[]{:S(2)}, u32[]{:S(2)}) %collective-permute-start.24) | collective-permute-done | bytes 262176 | tf_op jit(solution)/shard_map/ppermute | solution.py:982
  271.7 13.4 %collective-permute-done.25 = bf16[128,1024]{1,0:T(8,128)(2,1)} collective-permute-done((bf16[128,1024]{1,0:T(8,128)(2,1)}, bf16[128,1024]{1,0:T(8,128)(2,1)}, u32[]{:S(2)}, u32[]{:S(2)}) %collective-permute-start.25) | collective-permute-done | bytes 262176 | tf_op jit(solution)/shard_map/ppermute | solution.py:982
  285.1 7.9 %collective-permute-done.26 = bf16[128,1024]{1,0:T(8,128)(2,1)} collective-permute-done((bf16[128,1024]{1,0:T(8,128)(2,1)S(1)}, bf16[128,1024]{1,0:T(8,128)(2,1)}, u32[]{:S(2)}, u32[]{:S(2)}) %collective-permute-start.26) | collective-permute-done | bytes 262176 | tf_op jit(solution)/shard_map/ppermute | solution.py:982
  295.2 9.2 %in_back.1 = (f32[256,1536]{1,0:T(8,128)}, f32[1,1536]{1,0:T(1,128)}) custom-call(s32[4]{0:T(128)} %pad_add_fusion.ids_ref, bf16[256,1536]{1,0:T(8,128)(2,1)} %bitcast.47, f32[256,1536]{1,0:T(8,128)} %get-tuple-element.79.gres_ref, f32[1,1536]{1,0:T(1,128)} %bitcast.56, bf16[256,1536]{1,0:T(8,128)(2,1)} %get-tuple-element.83.dq_ref.refs_1_, ...), custom_call_target="tpu_custom_call" | custom-call | flops 2013265920 | bytes 12582912 | tf_op jit(solution)/shard_map/in_back/pallas_call | solution.py:593
  307.4 9.2 %reduce-scatter.2.cloned.1.call-done.refs_0_ = bf16[768,768]{1,0:T(8,128)(2,1)} async-done(((bf16[6144,768]{1,0:T(8,128)(2,1)}), bf16[768,768]{1,0:T(8,128)(2,1)}) %reduce-scatter.2.cloned.1.call-update) | async-done | bytes 1179664 | tf_op jit(solution)/shard_map/reduce_scatter | solution.py:958
  324.5 13.8 %collective-permute-done.22.refs_4_ = bf16[256,1536]{1,0:T(8,128)(2,1)S(1)} collective-permute-done((bf16[256,1536]{1,0:T(8,128)(2,1)}, bf16[256,1536]{1,0:T(8,128)(2,1)S(1)}, u32[]{:S(2)}, u32[]{:S(2)}) %collective-permute-start.22) | collective-permute-done | bytes 786464 | tf_op jit(solution)/shard_map/ppermute | solution.py:73
  338.3 13.5 %collective-permute-done.21.refs_3_ = bf16[256,1536]{1,0:T(8,128)(2,1)S(1)} collective-permute-done((bf16[256,1536]{1,0:T(8,128)(2,1)}, bf16[256,1536]{1,0:T(8,128)(2,1)S(1)}, u32[]{:S(2)}, u32[]{:S(2)}) %collective-permute-start.21) | collective-permute-done | bytes 786464 | tf_op jit(solution)/shard_map/ppermute | solution.py:58
  362.3 11.5 %collective-permute-done.30 = bf16[384,640]{1,0:T(8,128)(2,1)S(1)} collective-permute-done((bf16[384,640]{1,0:T(8,128)(2,1)S(1)}, bf16[384,640]{1,0:T(8,128)(2,1)S(1)}, u32[]{:S(2)}, u32[]{:S(2)}) %collective-permute-start.30) | collective-permute-done | bytes 491552 | tf_op jit(solution)/shard_map/ppermute | solution.py:73
  373.8 10.0 %collective-permute-done.29 = bf16[384,640]{1,0:T(8,128)(2,1)S(1)} collective-permute-done((bf16[384,640]{1,0:T(8,128)(2,1)S(1)}, bf16[384,640]{1,0:T(8,128)(2,1)S(1)}, u32[]{:S(2)}, u32[]{:S(2)}) %collective-permute-start.29) | collective-permute-done | bytes 491552 | tf_op jit(solution)/shard_map/ppermute | solution.py:58
  385.0 4.9 collective-permute-start.31
  394.0 17.7 %collective-permute-done.31 = bf16[384,640]{1,0:T(8,128)(2,1)S(1)} collective-permute-done((bf16[384,640]{1,0:T(8,128)(2,1)S(1)}, bf16[384,640]{1,0:T(8,128)(2,1)S(1)}, u32[]{:S(2)}, u32[]{:S(2)}) %collective-permute-start.31) | collective-permute-done | bytes 491552 | tf_op jit(solution)/shard_map/ppermute | solution.py:111
  412.6 6.5 %collective-permute-done.41 = bf16[384,768]{1,0:T(8,128)(2,1)S(1)} collective-permute-done((bf16[384,768]{1,0:T(8,128)(2,1)S(1)}, bf16[384,768]{1,0:T(8,128)(2,1)S(1)}, u32[]{:S(2)}, u32[]{:S(2)}) %collective-permute-start.41) | collective-permute-done | bytes 589856 | tf_op jit(solution)/shard_map/ppermute | solution.py:58
  423.5 8.8 %collective-permute-start.47 = (bf16[384,768]{1,0:T(8,128)(2,1)S(1)}, bf16[384,768]{1,0:T(8,128)(2,1)S(1)}, u32[]{:S(2)}, u32[]{:S(2)}) collective-permute-start(bf16[384,768]{1,0:T(8,128)(2,1)S(1)} %copy-done.1), channel_id=1, source_target_pairs={{0,8},{24,16},{1,9},{25,17},{2,10},{26,18},{3,11},{27,19},{4,12},{... | collective-permute-start | bytes 1769480 | tf_op jit(solution)/shard_map/ppermute | solution.py:111
  440.6 7.1 %collective-permute-done.47 = bf16[384,768]{1,0:T(8,128)(2,1)S(1)} collective-permute-done((bf16[384,768]{1,0:T(8,128)(2,1)S(1)}, bf16[384,768]{1,0:T(8,128)(2,1)S(1)}, u32[]{:S(2)}, u32[]{:S(2)}) %collective-permute-start.47) | collective-permute-done | bytes 589856 | tf_op jit(solution)/shard_map/ppermute | solution.py:111
  453.2 13.9 %collective-permute-done.45 = bf16[384,768]{1,0:T(8,128)(2,1)S(1)} collective-permute-done((bf16[384,768]{1,0:T(8,128)(2,1)S(1)}, bf16[384,768]{1,0:T(8,128)(2,1)S(1)}, u32[]{:S(2)}, u32[]{:S(2)}) %collective-permute-start.45) | collective-permute-done | bytes 589856 | tf_op jit(solution)/shard_map/ppermute | solution.py:118
  470.2 10.0 %collective-permute-done.49 = bf16[384,768]{1,0:T(8,128)(2,1)S(1)} collective-permute-done((bf16[384,768]{1,0:T(8,128)(2,1)S(1)}, bf16[384,768]{1,0:T(8,128)(2,1)S(1)}, u32[]{:S(2)}, u32[]{:S(2)}) %collective-permute-start.49) | collective-permute-done | bytes 589856 | tf_op jit(solution)/shard_map/ppermute | solution.py:118
  484.2 10.5 %spread_grads.1 = (f32[4,1536,256]{2,1,0:T(8,128)}, f32[4,1536,256]{2,1,0:T(8,128)}, f32[4,256,1536]{2,1,0:T(8,128)}) custom-call(bf16[6144,768]{1,0:T(8,128)(2,1)} %all-gather.7.cloned.1.call-done.in_ref), custom_call_target="tpu_custom_call" | custom-call | bytes 28311552 | tf_op jit(solution)/shard_map/spread_grads/pallas_call | solution.py:788
  (254 shorter events, 126.2 us)
Async XLA Ops:
  7.2 74.7 %all-gather.5.cloned.1.call-start = ((), (), s32[]{:S(2)}) async-start(), calls=%async_computation.1 | async-start | bytes 10616832 | tf_op jit(solution)/shard_map/all_gather | solution.py:197
  9.7 134.5 %all-gather.9.cloned.1.call-start = ((), (), s32[]{:S(2)}) async-start(), calls=%async_computation.4 | async-start | bytes 3932160 | tf_op jit(solution)/shard_map/all_gather | solution.py:898
  10.7 32.9 %collective-permute-start.2 = (f32[14,128]{1,0:T(8,128)S(1)}, f32[14,128]{1,0:T(8,128)S(1)}, u32[]{:S(2)}, u32[]{:S(2)}) collective-permute-start(f32[14,128]{1,0:T(8,128)S(1)} %maximum_bitcast_fusion), channel_id=1, source_target_pairs={{0,3},{1,2},{2,1},{3,0},{4,7},{5,6},{6,5},{7,4},{8,11},{9,10},{10,... | collective-permute-start | bytes 21512 | tf_op jit(solution)/shard_map/ppermute | solution.py:73
  14.6 28.9 %collective-permute-start.1 = (f32[14,128]{1,0:T(8,128)S(1)}, f32[14,128]{1,0:T(8,128)S(1)}, u32[]{:S(2)}, u32[]{:S(2)}) collective-permute-start(f32[14,128]{1,0:T(8,128)S(1)} %maximum_bitcast_fusion), channel_id=1, source_target_pairs={{0,2},{2,0},{1,3},{3,1},{4,6},{6,4},{5,7},{7,5},{8,10},{10,8},{9,1... | collective-permute-start | bytes 21512 | tf_op jit(solution)/shard_map/ppermute | solution.py:58
  15.2 28.5 %collective-permute-start = (f32[14,128]{1,0:T(8,128)S(1)}, f32[14,128]{1,0:T(8,128)S(1)}, u32[]{:S(2)}, u32[]{:S(2)}) collective-permute-start(f32[14,128]{1,0:T(8,128)S(1)} %maximum_bitcast_fusion), channel_id=1, source_target_pairs={{0,1},{1,0},{2,3},{3,2},{4,5},{5,4},{6,7},{7,6},{8,9},{9,8},{10,11... | collective-permute-start | bytes 21512 | tf_op jit(solution)/shard_map/ppermute | solution.py:53
  18.8 297.8 %reduce-scatter.2.cloned.1.call-start = ((), (), s32[]{:S(2)}) async-start(), calls=%async_computation.2 | async-start | bytes 10616832 | tf_op jit(solution)/shard_map/reduce_scatter | solution.py:958
  56.5 22.7 %collective-permute-start.10 = (bf16[128,1024]{1,0:T(8,128)(2,1)S(1)}, bf16[128,1024]{1,0:T(8,128)(2,1)S(1)}, u32[]{:S(2)}, u32[]{:S(2)}) collective-permute-start(bf16[128,1024]{1,0:T(8,128)(2,1)S(1)} %get-tuple-element.125), channel_id=1, source_target_pairs={{0,16},{8,24},{16,0},{24,8},{1,17},{9,25},{17,1},{25,9},{2,18},{10... | collective-permute-start | bytes 786440 | tf_op jit(solution)/shard_map/ppermute | solution.py:908
  56.5 22.7 %collective-permute-start.9 = (bf16[128,1024]{1,0:T(8,128)(2,1)S(1)}, bf16[128,1024]{1,0:T(8,128)(2,1)S(1)}, u32[]{:S(2)}, u32[]{:S(2)}) collective-permute-start(bf16[128,1024]{1,0:T(8,128)(2,1)S(1)} %get-tuple-element.123), channel_id=1, source_target_pairs={{0,8},{8,16},{16,24},{24,0},{1,9},{9,17},{17,25},{25,1},{2,10},{10... | collective-permute-start | bytes 786440 | tf_op jit(solution)/shard_map/ppermute | solution.py:908
  113.1 28.8 %collective-permute-start.13 = (bf16[256,1536]{1,0:T(8,128)(2,1)}, bf16[256,1536]{1,0:T(8,128)(2,1)S(1)}, u32[]{:S(2)}, u32[]{:S(2)}) collective-permute-start(bf16[256,1536]{1,0:T(8,128)(2,1)} %get-tuple-element.57.refs_0_), channel_id=1, source_target_pairs={{0,1},{1,0},{2,3},{3,2},{4,5},{5,4},{6,7},{7,6},{8,9},{9,8},{10,11... | collective-permute-start | bytes 2359304 | tf_op jit(solution)/shard_map/ppermute | solution.py:53
  114.8 28.7 %collective-permute-start.14 = (bf16[256,1536]{1,0:T(8,128)(2,1)}, bf16[256,1536]{1,0:T(8,128)(2,1)S(1)}, u32[]{:S(2)}, u32[]{:S(2)}) collective-permute-start(bf16[256,1536]{1,0:T(8,128)(2,1)} %get-tuple-element.57.refs_0_), channel_id=1, source_target_pairs={{2,0},{0,2},{3,1},{1,3},{6,4},{4,6},{7,5},{5,7},{10,8},{8,10},{11,... | collective-permute-start | bytes 2359304 | tf_op jit(solution)/shard_map/ppermute | solution.py:63
  142.0 26.6 %collective-permute-start.15 = (bf16[128,1536]{1,0:T(8,128)(2,1)S(1)}, bf16[128,1536]{1,0:T(8,128)(2,1)S(1)}, u32[]{:S(2)}, u32[]{:S(2)}) collective-permute-start(bf16[128,1536]{1,0:T(8,128)(2,1)S(1)} %slice.86), channel_id=1, source_target_pairs={{2,0},{0,2},{3,1},{1,3},{6,4},{4,6},{7,5},{5,7},{10,8},{8,10},{11,... | collective-permute-start | bytes 1179656 | tf_op jit(solution)/shard_map/ppermute | solution.py:63
  143.6 25.0 %collective-permute-start.16 = (bf16[128,1536]{1,0:T(8,128)(2,1)S(1)}, bf16[128,1536]{1,0:T(8,128)(2,1)S(1)}, u32[]{:S(2)}, u32[]{:S(2)}) collective-permute-start(bf16[128,1536]{1,0:T(8,128)(2,1)S(1)} %slice.87), channel_id=1, source_target_pairs={{0,1},{1,0},{2,3},{3,2},{4,5},{5,4},{6,7},{7,6},{8,9},{9,8},{10,11... | collective-permute-start | bytes 1179656 | tf_op jit(solution)/shard_map/ppermute | solution.py:53
  166.7 35.0 %collective-permute-start.17 = (bf16[256,1536]{1,0:T(8,128)(2,1)}, bf16[256,1536]{1,0:T(8,128)(2,1)S(1)}, u32[]{:S(2)}, u32[]{:S(2)}) collective-permute-start(bf16[256,1536]{1,0:T(8,128)(2,1)} %get-tuple-element.65), channel_id=1, source_target_pairs={{0,1},{1,0},{2,3},{3,2},{4,5},{5,4},{6,7},{7,6},{8,9},{9,8},{10,11... | collective-permute-start | bytes 2359304 | tf_op jit(solution)/shard_map/ppermute | solution.py:53
  168.0 35.5 %collective-permute-start.18 = (bf16[256,1536]{1,0:T(8,128)(2,1)}, bf16[256,1536]{1,0:T(8,128)(2,1)S(1)}, u32[]{:S(2)}, u32[]{:S(2)}) collective-permute-start(bf16[256,1536]{1,0:T(8,128)(2,1)} %get-tuple-element.66), channel_id=1, source_target_pairs={{0,2},{2,0},{1,3},{3,1},{4,6},{6,4},{5,7},{7,5},{8,10},{10,8},{9,1... | collective-permute-start | bytes 2359304 | tf_op jit(solution)/shard_map/ppermute | solution.py:58
  201.3 283.0 %all-gather.7.cloned.1.call-start = ((), (), s32[]{:S(2)}) async-start(), calls=%async_computation.3 | async-start | bytes 10616832 | tf_op jit(solution)/shard_map/all_gather | solution.py:993
  217.9 40.2 %collective-permute-start.35 = (bf16[1536,768]{1,0:T(8,128)(2,1)}, bf16[1536,768]{1,0:T(8,128)(2,1)}, u32[]{:S(2)}, u32[]{:S(2)}) collective-permute-start(bf16[1536,768]{1,0:T(8,128)(2,1)} %get-tuple-element.91), channel_id=1, source_target_pairs={{0,4},{4,0},{1,5},{5,1},{2,6},{6,2},{3,7},{7,3},{8,12},{12,8},{9,1... | collective-permute-start | bytes 7077896 | tf_op jit(solution)/shard_map/ppermute | solution.py:53
  244.9 25.2 %collective-permute-start.24 = (bf16[128,1024]{1,0:T(8,128)(2,1)}, bf16[128,1024]{1,0:T(8,128)(2,1)}, u32[]{:S(2)}, u32[]{:S(2)}) collective-permute-start(bf16[128,1024]{1,0:T(8,128)(2,1)} %get-tuple-element.118), channel_id=1, source_target_pairs={{8,0},{16,8},{24,16},{0,24},{9,1},{17,9},{25,17},{1,25},{10,2},{18... | collective-permute-start | bytes 786440 | tf_op jit(solution)/shard_map/ppermute | solution.py:982
  257.5 27.6 %collective-permute-start.25 = (bf16[128,1024]{1,0:T(8,128)(2,1)}, bf16[128,1024]{1,0:T(8,128)(2,1)}, u32[]{:S(2)}, u32[]{:S(2)}) collective-permute-start(bf16[128,1024]{1,0:T(8,128)(2,1)} %get-tuple-element.117), channel_id=1, source_target_pairs={{16,0},{24,8},{0,16},{8,24},{17,1},{25,9},{1,17},{9,25},{18,2},{26... | collective-permute-start | bytes 786440 | tf_op jit(solution)/shard_map/ppermute | solution.py:982
  257.5 35.5 %collective-permute-start.26 = (bf16[128,1024]{1,0:T(8,128)(2,1)S(1)}, bf16[128,1024]{1,0:T(8,128)(2,1)}, u32[]{:S(2)}, u32[]{:S(2)}) collective-permute-start(bf16[128,1024]{1,0:T(8,128)(2,1)S(1)} %get-tuple-element.116), channel_id=1, source_target_pairs={{24,0},{0,8},{8,16},{16,24},{25,1},{1,9},{9,17},{17,25},{26,2},{2,... | collective-permute-start | bytes 786440 | tf_op jit(solution)/shard_map/ppermute | solution.py:982
  260.6 43.8 %collective-permute-start.38 = (bf16[384,768]{1,0:T(8,128)(2,1)S(1)}, bf16[384,768]{1,0:T(8,128)(2,1)}, u32[]{:S(2)}, u32[]{:S(2)}) collective-permute-start(bf16[384,768]{1,0:T(8,128)(2,1)S(1)} %get-tuple-element.109), channel_id=1, source_target_pairs={{0,3},{1,2},{2,1},{3,0},{4,7},{5,6},{6,5},{7,4},{8,11},{9,10},{10,... | collective-permute-start | bytes 1769480 | tf_op jit(solution)/shard_map/ppermute | solution.py:73
  260.9 43.5 %collective-permute-start.37 = (bf16[384,768]{1,0:T(8,128)(2,1)S(1)}, bf16[384,768]{1,0:T(8,128)(2,1)}, u32[]{:S(2)}, u32[]{:S(2)}) collective-permute-start(bf16[384,768]{1,0:T(8,128)(2,1)S(1)} %get-tuple-element.110), channel_id=1, source_target_pairs={{0,2},{2,0},{1,3},{3,1},{4,6},{6,4},{5,7},{7,5},{8,10},{10,8},{9,1... | collective-permute-start | bytes 1769480 | tf_op jit(solution)/shard_map/ppermute | solution.py:58
  270.1 34.3 %collective-permute-start.36 = (bf16[384,768]{1,0:T(8,128)(2,1)S(1)}, bf16[384,768]{1,0:T(8,128)(2,1)}, u32[]{:S(2)}, u32[]{:S(2)}) collective-permute-start(bf16[384,768]{1,0:T(8,128)(2,1)S(1)} %get-tuple-element.108), channel_id=1, source_target_pairs={{0,1},{1,0},{2,3},{3,2},{4,5},{5,4},{6,7},{7,6},{8,9},{9,8},{10,11... | collective-permute-start | bytes 1769480 | tf_op jit(solution)/shard_map/ppermute | solution.py:53
  319.1 32.7 %collective-permute-start.21 = (bf16[256,1536]{1,0:T(8,128)(2,1)}, bf16[256,1536]{1,0:T(8,128)(2,1)S(1)}, u32[]{:S(2)}, u32[]{:S(2)}) collective-permute-start(bf16[256,1536]{1,0:T(8,128)(2,1)} %get-tuple-element.77), channel_id=1, source_target_pairs={{0,2},{2,0},{1,3},{3,1},{4,6},{6,4},{5,7},{7,5},{8,10},{10,8},{9,1... | collective-permute-start | bytes 2359304 | tf_op jit(solution)/shard_map/ppermute | solution.py:58
  319.7 32.2 %collective-permute-start.20 = (bf16[256,1536]{1,0:T(8,128)(2,1)}, bf16[256,1536]{1,0:T(8,128)(2,1)S(1)}, u32[]{:S(2)}, u32[]{:S(2)}) collective-permute-start(bf16[256,1536]{1,0:T(8,128)(2,1)} %get-tuple-element.76), channel_id=1, source_target_pairs={{0,1},{1,0},{2,3},{3,2},{4,5},{5,4},{6,7},{7,6},{8,9},{9,8},{10,11... | collective-permute-start | bytes 2359304 | tf_op jit(solution)/shard_map/ppermute | solution.py:53
  324.5 33.9 %collective-permute-start.27 = (bf16[1536,640]{1,0:T(8,128)(2,1)}, bf16[1536,640]{1,0:T(8,128)(2,1)S(1)}, u32[]{:S(2)}, u32[]{:S(2)}) collective-permute-start(bf16[1536,640]{1,0:T(8,128)(2,1)} %get-tuple-element.90), channel_id=1, source_target_pairs={{0,4},{4,0},{1,5},{5,1},{2,6},{6,2},{3,7},{7,3},{8,12},{12,8},{9,1... | collective-permute-start | bytes 5898248 | tf_op jit(solution)/shard_map/ppermute | solution.py:53
  358.3 31.7 %collective-permute-start.39 = (bf16[1536,768]{1,0:T(8,128)(2,1)}, bf16[1536,768]{1,0:T(8,128)(2,1)S(1)}, u32[]{:S(2)}, u32[]{:S(2)}) collective-permute-start(bf16[1536,768]{1,0:T(8,128)(2,1)} %get-tuple-element.93), channel_id=1, source_target_pairs={{0,4},{4,0},{1,5},{5,1},{2,6},{6,2},{3,7},{7,3},{8,12},{12,8},{9,1... | collective-permute-start | bytes 7077896 | tf_op jit(solution)/shard_map/ppermute | solution.py:53
  360.5 23.4 %collective-permute-start.29 = (bf16[384,640]{1,0:T(8,128)(2,1)S(1)}, bf16[384,640]{1,0:T(8,128)(2,1)S(1)}, u32[]{:S(2)}, u32[]{:S(2)}) collective-permute-start(bf16[384,640]{1,0:T(8,128)(2,1)S(1)} %get-tuple-element.113.refs_4_), channel_id=1, source_target_pairs={{0,2},{2,0},{1,3},{3,1},{4,6},{6,4},{5,7},{7,5},{8,10},{10,8},{9,1... | collective-permute-start | bytes 1474568 | tf_op jit(solution)/shard_map/ppermute | solution.py:58
  385.0 26.7 %collective-permute-start.31 = (bf16[384,640]{1,0:T(8,128)(2,1)S(1)}, bf16[384,640]{1,0:T(8,128)(2,1)S(1)}, u32[]{:S(2)}, u32[]{:S(2)}) collective-permute-start(bf16[384,640]{1,0:T(8,128)(2,1)S(1)} %get-tuple-element.103), channel_id=1, source_target_pairs={{0,8},{24,16},{1,9},{25,17},{2,10},{26,18},{3,11},{27,19},{4,12},{... | collective-permute-start | bytes 1474568 | tf_op jit(solution)/shard_map/ppermute | solution.py:111
  392.2 26.9 %collective-permute-start.41 = (bf16[384,768]{1,0:T(8,128)(2,1)S(1)}, bf16[384,768]{1,0:T(8,128)(2,1)S(1)}, u32[]{:S(2)}, u32[]{:S(2)}) collective-permute-start(bf16[384,768]{1,0:T(8,128)(2,1)S(1)} %get-tuple-element.107), channel_id=1, source_target_pairs={{0,2},{2,0},{1,3},{3,1},{4,6},{6,4},{5,7},{7,5},{8,10},{10,8},{9,1... | collective-permute-start | bytes 1769480 | tf_op jit(solution)/shard_map/ppermute | solution.py:58
  393.4 25.8 %collective-permute-start.40 = (bf16[384,768]{1,0:T(8,128)(2,1)S(1)}, bf16[384,768]{1,0:T(8,128)(2,1)S(1)}, u32[]{:S(2)}, u32[]{:S(2)}) collective-permute-start(bf16[384,768]{1,0:T(8,128)(2,1)S(1)} %get-tuple-element.105), channel_id=1, source_target_pairs={{0,1},{1,0},{2,3},{3,2},{4,5},{5,4},{6,7},{7,6},{8,9},{9,8},{10,11... | collective-permute-start | bytes 1769480 | tf_op jit(solution)/shard_map/ppermute | solution.py:53
  423.5 24.2 %collective-permute-start.47 = (bf16[384,768]{1,0:T(8,128)(2,1)S(1)}, bf16[384,768]{1,0:T(8,128)(2,1)S(1)}, u32[]{:S(2)}, u32[]{:S(2)}) collective-permute-start(bf16[384,768]{1,0:T(8,128)(2,1)S(1)} %copy-done.1), channel_id=1, source_target_pairs={{0,8},{24,16},{1,9},{25,17},{2,10},{26,18},{3,11},{27,19},{4,12},{... | collective-permute-start | bytes 1769480 | tf_op jit(solution)/shard_map/ppermute | solution.py:111
  451.9 28.3 %collective-permute-start.49 = (bf16[384,768]{1,0:T(8,128)(2,1)S(1)}, bf16[384,768]{1,0:T(8,128)(2,1)S(1)}, u32[]{:S(2)}, u32[]{:S(2)}) collective-permute-start(bf16[384,768]{1,0:T(8,128)(2,1)S(1)} %add_convert_fusion.2), channel_id=1, source_target_pairs={{8,0},{16,24},{9,1},{17,25},{10,2},{18,26},{11,3},{19,27},{12,4},{... | collective-permute-start | bytes 1769480 | tf_op jit(solution)/shard_map/ppermute | solution.py:118
  (61 other events, 622.0 us)
Sparse Core Ops, SparseCore 0:
  10.5 68.7 all-gather.4
  81.1 53.2 all-gather.8
  201.4 115.1 reduce-scatter.1
  318.1 99.0 all-gather.6
